TPU v7x, 256 devices: a whole 4x4x8 slice. The times are simulated.
256 devices in a mesh: role: 2 (over x_lo), grp: 2 (over x_hi), tp: 64 (over y, z, core).
Axes of the slice: x: 4 (x_hi: 2, x_lo: 2; x = x_hi * 2 + x_lo), y: 4, z: 8, core: 2. Of those that a mesh axis runs over, the one named last changes fastest.
Arguments:
- queries: bfloat16 [2, 8, 8192], P(None, None, ('grp', 'tp')), may hold values from -130 to 130
- step_token_keys: bfloat16 [2, 8, 1024], replicated, may hold values from -6 to 6
- step_token_values: bfloat16 [2, 8, 1024], replicated, may hold values from -6 to 6
- stored_key_cache: bfloat16 [8, 4096, 1024], P(None, ('grp', 'tp')), may hold values from -6 to 6
- stored_value_cache: bfloat16 [8, 4096, 1024], P(None, ('grp', 'tp')), may hold values from -6 to 6
- lengths: int32 [8], replicated, may hold values from 2 to 4096
- wo_sides: bfloat16 [2, 8192, 8192], P('role', ('grp', 'tp')), may hold values from -1 to 1
- gain_sides: float32 [2, 8192], P('role', ('grp', 'tp')), may hold values from 0.5 to 1.5
- head: bfloat16 [8192, 64128], P(None, ('grp', 'tp')), may hold values from -8 to 8
- resid: bfloat16 [2, 8, 8192], P(None, None, ('grp', 'tp')), may hold values from -90 to 90
- actions: int32 [2, 8], replicated, may hold values from 0 to 64127
Outputs:
- log_probs: float32 [2, 8], P('role')
- normed: bfloat16 [2, 8, 8192], P('role', None, ('grp', 'tp'))
All inputs are finite; a program needn't handle non-finite values.
Results may differ from a plain program's by a relative error of at most 0.017.
Values may be sent and summed in bfloat16 or wider, within the bound.
No kernel may reach another device: no remote copies, remote signals or barrier semaphores. Data moves between devices by JAX's collectives and lax.ppermute only.
A program may use at most 128 MiB of HBM per device.

v0:
```python
import math

import jax
import jax.numpy as jnp
from jax import lax
from jax.sharding import Mesh
from jax.sharding import PartitionSpec as P

D = 8192
QUERY_HEADS = 64
KEY_VALUE_HEADS = 8
HEAD_SIZE = 128
DECODE_STEPS = 2
GRP_TP = ("grp", "tp_0", "tp_1", "tp_2")


def sent_to_all(x, axis):
    copies = jnp.broadcast_to(x, (lax.axis_size(axis), *x.shape))
    return lax.all_to_all(copies, axis, split_axis=0, concat_axis=0, tiled=True)


def joined_along(tiles, dim):
    tiles = jnp.moveaxis(tiles, 0, dim)
    dims = tiles.shape
    return tiles.reshape(*dims[:dim], dims[dim] * dims[dim + 1], *dims[dim + 2 :])


def whole_of(x, axes, dim):
    far, near = axes
    tiles = sent_to_all(sent_to_all(x, far), near)
    return joined_along(tiles.swapaxes(0, 1).reshape(-1, *x.shape), dim)


def all_in_one(x, axis):
    leaves = jax.tree.leaves(x)
    sequence = sorted(range(len(leaves)), key=lambda k: -leaves[k].size)
    width = (1, *leaves[sequence[0]].shape)[-1]
    lines = [
        jnp.pad(leaves[k].reshape(-1), (0, -leaves[k].size % width)).reshape(-1, width)
        for k in sequence
    ]
    both, at, found = (lax.all_gather(jnp.concatenate(lines), axis), 0, {})
    for k, line in zip(sequence, lines):
        section = both[:, at : at + len(line)].reshape(len(both), -1)
        found[k] = section[:, : leaves[k].size].reshape(-1, *leaves[k].shape)
        at += len(line)
    numbers = iter(range(len(leaves)))
    return jax.tree.map(lambda _: found[next(numbers)], x)


def joined_all(x, axes, combine):
    for axis in axes:
        pieces = all_in_one(
            jax.tree.map(
                lambda part, kind: part.astype(kind), x, (jnp.bfloat16, jnp.bfloat16, jnp.bfloat16)
            ),
            axis,
        )
        widened = [
            jax.tree.map(lambda part, own: part[k].astype(own.dtype), pieces, x)
            for k in range(lax.axis_size(axis))
        ]
        x = widened[0]
        for partner_block in widened[1:]:
            x = combine(x, partner_block)
    return x


def of_everyone(x, axis):
    return sent_to_all(x, axis).sum(axis=0)


def one_axis_at_a_time(x, axes):
    far, near = axes
    nearer = of_everyone(x, near)
    return of_everyone(nearer, far)


def combined_by_axis(x, axes, combine):
    for axis in axes:
        pieces = all_in_one(x, axis)
        x = jax.tree.map(lambda part: part[0], pieces)
        for k in range(1, lax.axis_size(axis)):
            x = combine(x, jax.tree.map(lambda part: part[k], pieces))
    return x


def from_partner(value, axis, apart):
    mask = 2**apart
    pairs = [(source, source ^ mask) for source in range(lax.axis_size(axis))]
    return lax.ppermute(value, axis, pairs)


def soft_combine(earlier, later):
    highest = jnp.maximum(earlier[0], later[0])
    left_factor = jnp.exp(earlier[0] - highest)
    right_factor = jnp.exp(later[0] - highest)
    return (
        highest,
        earlier[1] * left_factor + later[1] * right_factor,
        earlier[2] * left_factor[..., None] + later[2] * right_factor[..., None],
    )


def vocab_combine(earlier, later):
    highest = jnp.maximum(earlier[0], later[0])
    return (
        highest,
        earlier[1] * jnp.exp(earlier[0] - highest) + later[1] * jnp.exp(later[0] - highest),
        earlier[2] + later[2],
    )


def on_device(
    queries,
    step_token_keys,
    step_token_values,
    stored_key_cache,
    stored_value_cache,
    lengths,
    wo_sides,
    gain_sides,
    head,
    resid,
    actions,
):
    place = lax.axis_index(GRP_TP)
    side_index = lax.axis_index("role")
    count_of_rows = lengths.shape[0]
    shard_length = stored_key_cache.shape[1]
    query_group_width = QUERY_HEADS // KEY_VALUE_HEADS
    logit_scale = 1.0 / math.sqrt(HEAD_SIZE)
    gathered = whole_of(queries, (("grp", "tp_0", "tp_1"), "tp_2"), 2)
    positions = place * shard_length + jnp.arange(shard_length, dtype=jnp.int32)
    valid = positions[None, :] < lengths[:, None]
    masking = valid[:, None, None, :]
    prior_keys = stored_key_cache.astype(jnp.float32).reshape(
        count_of_rows, shard_length, KEY_VALUE_HEADS, HEAD_SIZE
    )
    prior_values = stored_value_cache.astype(jnp.float32).reshape(
        count_of_rows, shard_length, KEY_VALUE_HEADS, HEAD_SIZE
    )
    weight_used = wo_sides[0]
    gain_used = gain_sides[0]
    step_here = 1 - side_index
    columns = lax.all_to_all(weight_used, GRP_TP, split_axis=1, concat_axis=0, tiled=True)
    head_width = head.shape[1]
    vocab_ids = place * head_width + jnp.arange(head_width, dtype=jnp.int32)
    step_ids = jnp.arange(DECODE_STEPS, dtype=jnp.int32)
    incoming_keys = step_token_keys.astype(jnp.float32).reshape(
        DECODE_STEPS, count_of_rows, KEY_VALUE_HEADS, HEAD_SIZE
    )
    incoming_values = step_token_values.astype(jnp.float32).reshape(
        DECODE_STEPS, count_of_rows, KEY_VALUE_HEADS, HEAD_SIZE
    )
    query_matrix = lax.dynamic_index_in_dim(gathered, step_here, 0, keepdims=False)
    current_query = (
        query_matrix.astype(jnp.float32).reshape(
            count_of_rows, KEY_VALUE_HEADS, query_group_width, HEAD_SIZE
        )
        * logit_scale
    )
    scores = jnp.einsum("rkgd,rskd->rkgs", current_query, prior_keys)
    scores = jnp.where(masking, scores, -1e30)
    highest = jnp.max(scores, axis=-1)
    cache_probs = jnp.exp(scores - highest[..., None]) * masking
    totals = jnp.sum(cache_probs, axis=-1)
    weighted = jnp.einsum("rkgs,rskd->rkgd", cache_probs, prior_values)
    highest, totals, weighted = joined_all((highest, totals, weighted), GRP_TP, soft_combine)
    fresh_live = step_ids <= step_here
    fresh_scores = jnp.einsum("rkgd,trkd->rkgt", current_query, incoming_keys)
    fresh_scores = jnp.where(fresh_live, fresh_scores, -1e30)
    overall = jnp.maximum(highest, jnp.max(fresh_scores, axis=-1))
    cache_factor = jnp.exp(highest - overall)
    fresh_probs = jnp.exp(fresh_scores - overall[..., None]) * fresh_live
    denominator = totals * cache_factor + jnp.sum(fresh_probs, axis=-1)
    mixed = weighted * cache_factor[..., None] + jnp.einsum(
        "rkgt,trkd->rkgd", fresh_probs, incoming_values
    )
    attended = (
        (mixed / denominator[..., None])
        .reshape(count_of_rows, QUERY_HEADS * HEAD_SIZE)
        .astype(jnp.bfloat16)
    )
    branch_out = jnp.dot(attended, columns, preferred_element_type=jnp.float32)
    resid_now = lax.dynamic_index_in_dim(resid, step_here, 0, keepdims=False)
    state = resid_now.astype(jnp.float32) + branch_out
    square_sum = one_axis_at_a_time(
        jnp.sum(state * state, axis=-1), ("grp", ("tp_0", "tp_1", "tp_2"))
    )
    normed_now = (state * lax.rsqrt(square_sum[:, None] / D + 1e-05) * gain_used[None, :]).astype(
        jnp.bfloat16
    )
    logits = jnp.dot(
        whole_of(normed_now, (("grp", "tp_0", "tp_1"), "tp_2"), 1),
        head,
        preferred_element_type=jnp.float32,
    )
    local_highest = jnp.max(logits, axis=-1)
    action_now = lax.dynamic_index_in_dim(actions, step_here, 0, keepdims=False)
    is_target = vocab_ids[None, :] == action_now[:, None]
    target = jnp.sum(jnp.where(is_target, logits, 0.0), axis=-1)
    exp_sum = jnp.sum(jnp.exp(logits - local_highest[:, None]), axis=-1)
    largest, exp_sum, target = combined_by_axis(
        (local_highest, exp_sum, target), GRP_TP, vocab_combine
    )
    prob_now = target - largest - jnp.log(exp_sum)
    peer_prob, peer_normed = (
        from_partner(prob_now, "role", 0),
        from_partner(normed_now.astype(jnp.float32), "role", 0).astype(normed_now.dtype),
    )
    return (peer_prob[None], peer_normed[None])


def solution(mesh):
    split = Mesh(
        mesh.devices.reshape(mesh.shape["role"], mesh.shape["grp"], 4, 8, 2),
        ("role", "grp", "tp_0", "tp_1", "tp_2"),
    )
    return jax.shard_map(
        on_device,
        mesh=split,
        in_specs=(
            P(None, None, GRP_TP),
            P(),
            P(),
            P(None, GRP_TP, None),
            P(None, GRP_TP, None),
            P(),
            P("role", GRP_TP, None),
            P("role", GRP_TP),
            P(None, GRP_TP),
            P(None, None, GRP_TP),
            P(),
        ),
        out_specs=(P("role", None), P("role", None, GRP_TP)),
        check_vma=False,
    )
```

profile of v0, /device:TPU:1, one launch (start us, length us, event | category | flops | bytes accessed | tf_op | source)
XLA Modules:
  0.0 238.4 jit_solution(9583879579267579101)
XLA Ops:
  7.2 0.8 broadcast_in_dim.38
  8.0 0.8 reshape.1871
  8.8 15.1 %all-to-all-start = ((bf16[64,2,512]{2,1,0:T(2,128)(2,1)}), bf16[64,2,512]{2,1,0:T(2,128)(2,1)S(1)}, u32[]{:S(2)}, u32[]{:S(2)}) async-start(bf16[64,2,512]{2,1,0:T(2,128)(2,1)} %reshape.1871), calls=%async_computation | async-start | bytes 262144 | tf_op jit(solution)/shard_map/all_to_all | solution.py:19
  23.9 4.2 %all_to_all.36 = bf16[64,128,64]{2,1,0:T(8,128)(2,1)} reshape(bf16[1,64,8192]{2,1,0:T(8,128)(2,1)} %param.17) | data formatting | bytes 2097152 | tf_op jit(solution)/shard_map/all_to_all | solution.py:146
  28.2 2.9 %copy.108 = bf16[64,128,64]{2,0,1:T(8,128)(2,1)S(1)} copy(bf16[64,128,64]{2,1,0:T(8,128)(2,1)} %all_to_all.36) | data formatting | bytes 2097152 | tf_op jit(solution)/shard_map/all_to_all | solution.py:146
  31.1 2.3 reshape.1869
  33.5 1.9 all-to-all-done
  36.2 5.7 %all_to_all.51 = bf16[2,2,32768]{2,1,0:T(2,128)(2,1)S(1)} all-to-all(bf16[2,2,32768]{2,1,0:T(2,128)(2,1)S(1)} %reshape.1873), channel_id=1, replica_groups=mesh['role'=2,'grp'=2,'tp_0'=4,'tp_1'=8,'tp_2'=2] {'tp_2'}, dimensions={0} | all-to-all | bytes 524288 | tf_op jit(solution)/shard_map/all_to_all | solution.py:19
  42.0 10.9 %all-to-all-start.2 = ((bf16[128,2,2048]{2,1,0:T(2,128)(2,1)}), bf16[128,2,2048]{2,1,0:T(2,128)(2,1)}, u32[]{:S(2)}, u32[]{:S(2)}) async-start(bf16[128,2,2048]{2,1,0:T(2,128)(2,1)} %reshape.1869), calls=%async_computation.2 | async-start | bytes 2097152 | tf_op jit(solution)/shard_map/all_to_all | solution.py:146
  55.6 8.7 %all-gather = bf16[1040,128]{1,0:T(8,128)(2,1)S(1)} all-gather(bf16[520,128]{1,0:T(8,128)(2,1)S(1)} %pad_maximum_fusion), channel_id=2, replica_groups=mesh['role'=2,'grp'=2,'tp_0'=4,'tp_1'=8,'tp_2'=2] {'grp'}, dimensions={0}, use_global_device_ids=true | all-gather | bytes 399360 | tf_op jit(solution)/shard_map/all_gather | solution.py:42
  64.6 15.3 %all-gather.1 = bf16[2080,128]{1,0:T(8,128)(2,1)S(1)} all-gather(bf16[520,128]{1,0:T(8,128)(2,1)S(1)} %pad_maximum_fusion.1), channel_id=3, replica_groups=mesh['role'=2,'grp'=2,'tp_0'=4,'tp_1'=8,'tp_2'=2] {'tp_0'}, dimensions={0}, use_global_device_ids=true | all-gather | bytes 665600 | tf_op jit(solution)/shard_map/all_gather | solution.py:42
  81.4 1.4 all-to-all-done.2
  82.8 3.8 %reshape.1870 = bf16[128,64,64]{2,1,0:T(8,128)(2,1)S(1)} reshape(bf16[128,2,2048]{2,1,0:T(2,128)(2,1)} %all-to-all-done.2) | data formatting | bytes 2097152
  86.6 31.9 %all-gather.14.cloned.1.call-done = bf16[4160,128]{1,0:T(8,128)(2,1)} async-done(((bf16[520,128]{1,0:T(8,128)(2,1)}), bf16[4160,128]{1,0:T(8,128)(2,1)}) %all-gather.14.cloned.1.call-update) | async-done | bytes 1064976 | tf_op jit(solution)/shard_map/all_gather | solution.py:42
  118.4 0.8 fusion.97
  119.3 0.7 fusion.93
  121.4 0.7 fusion.151
  122.1 2.2 fusion.12
  124.4 7.3 %all-gather.3 = bf16[1040,128]{1,0:T(8,128)(2,1)S(1)} all-gather(bf16[520,128]{1,0:T(8,128)(2,1)S(1)} %pad_maximum_fusion.3), channel_id=5, replica_groups=mesh['role'=2,'grp'=2,'tp_0'=4,'tp_1'=8,'tp_2'=2] {'tp_2'}, dimensions={0}, use_global_device_ids=true | all-gather | bytes 399360 | tf_op jit(solution)/shard_map/all_gather | solution.py:42
  133.4 16.7 %all_to_all.52 = f32[64,1,8]{2,1,0:T(1,128)S(1)} all-to-all(f32[64,1,8]{2,1,0:T(1,128)S(1)} %broadcast_in_dim.45), channel_id=1, replica_groups=mesh['role'=2,'grp'=2,'tp_0'=4,'tp_1'=8,'tp_2'=2] {'tp_0','tp_1','tp_2'}, dimensions={0} | all-to-all | bytes 4096 | tf_op jit(solution)/shard_map/all_to_all | solution.py:19
  150.2 7.9 %all_to_all.53 = f32[2,1,8]{2,1,0:T(1,128)S(1)} all-to-all(f32[2,1,8]{2,1,0:T(1,128)S(1)} %broadcast_in_dim.46), channel_id=1, replica_groups=mesh['role'=2,'grp'=2,'tp_0'=4,'tp_1'=8,'tp_2'=2] {'grp'}, dimensions={0} | all-to-all | bytes 128 | tf_op jit(solution)/shard_map/all_to_all | solution.py:19
  158.2 0.8 reshape.1875
  159.0 4.6 %all-to-all-start.5 = ((bf16[64,2,256]{2,1,0:T(2,128)(2,1)}), bf16[64,2,256]{2,1,0:T(2,128)(2,1)S(1)}, u32[]{:S(2)}, u32[]{:S(2)}) async-start(bf16[64,2,256]{2,1,0:T(2,128)(2,1)} %reshape.1875), calls=%async_computation.5 | async-start | bytes 131072 | tf_op jit(solution)/shard_map/all_to_all | solution.py:19
  163.6 11.0 %all-to-all-done.5 = bf16[64,2,256]{2,1,0:T(2,128)(2,1)S(1)} async-done(((bf16[64,2,256]{2,1,0:T(2,128)(2,1)}), bf16[64,2,256]{2,1,0:T(2,128)(2,1)S(1)}, u32[]{:S(2)}, u32[]{:S(2)}) %all-to-all-start.5) | async-done | bytes 65568 | tf_op jit(solution)/shard_map/all_to_all | solution.py:19
  175.0 6.7 %all_to_all.54 = bf16[2,2,16384]{2,1,0:T(2,128)(2,1)S(1)} all-to-all(bf16[2,2,16384]{2,1,0:T(2,128)(2,1)S(1)} %reshape.1877), channel_id=1, replica_groups=mesh['role'=2,'grp'=2,'tp_0'=4,'tp_1'=8,'tp_2'=2] {'tp_2'}, dimensions={0} | all-to-all | bytes 262144 | tf_op jit(solution)/shard_map/all_to_all | solution.py:19
  182.3 5.7 %fusion.241 = (f32[8]{0:T(128)S(1)}, f32[8,501]{1,0:T(8,128)S(1)}) fusion(bf16[8,8192]{1,0:T(8,128)(2,1)S(1)} %reshape.1779, bf16[8192,501]{0,1:T(8,128)(2,1)} %param.19), kind=kOutput, calls=%fused_computation.398 | convolution fusion | flops 65671072 | bytes 8355520 | tf_op jit(solution)/shard_map/dot_general | solution.py:194
  188.7 4.7 %all-gather.8 = f32[2,3,8]{2,1,0:T(4,128)S(1)} all-gather(f32[1,3,8]{2,1,0:T(4,128)S(1)} %maximum_bitcast_fusion), channel_id=6, replica_groups=mesh['role'=2,'grp'=2,'tp_0'=4,'tp_1'=8,'tp_2'=2] {'grp'}, dimensions={0}, use_global_device_ids=true | all-gather | bytes 288 | tf_op jit(solution)/shard_map/all_gather | solution.py:42
  193.4 8.1 %all-gather.9 = f32[4,3,8]{2,1,0:T(4,128)S(1)} all-gather(f32[1,3,8]{2,1,0:T(4,128)S(1)} %maximum_bitcast_fusion.1), channel_id=7, replica_groups=mesh['role'=2,'grp'=2,'tp_0'=4,'tp_1'=8,'tp_2'=2] {'tp_0'}, dimensions={0}, use_global_device_ids=true | all-gather | bytes 480 | tf_op jit(solution)/shard_map/all_gather | solution.py:42
  201.5 15.5 %all-gather.10 = f32[8,3,8]{2,1,0:T(4,128)S(1)} all-gather(f32[1,3,8]{2,1,0:T(4,128)S(1)} %maximum_bitcast_fusion.2), channel_id=8, replica_groups=mesh['role'=2,'grp'=2,'tp_0'=4,'tp_1'=8,'tp_2'=2] {'tp_1'}, dimensions={0}, use_global_device_ids=true | all-gather | bytes 864 | tf_op jit(solution)/shard_map/all_gather | solution.py:42
  217.1 10.9 %all-gather.11 = f32[2,3,8]{2,1,0:T(4,128)S(1)} all-gather(f32[1,3,8]{2,1,0:T(4,128)S(1)} %maximum_bitcast_fusion.3), channel_id=9, replica_groups=mesh['role'=2,'grp'=2,'tp_0'=4,'tp_1'=8,'tp_2'=2] {'tp_2'}, dimensions={0}, use_global_device_ids=true | all-gather | bytes 288 | tf_op jit(solution)/shard_map/all_gather | solution.py:42
  228.0 1.3 collective-permute-start
  229.3 1.2 collective-permute-done
  (94 shorter events, 11.3 us)
Async XLA Ops:
  7.2 48.1 %copy-start = (bf16[8,32,1024]{2,1,0:T(8,128)(2,1)S(1)}, bf16[8,32,1024]{2,1,0:T(8,128)(2,1)}, u32[]{:S(2)}) copy-start(bf16[8,32,1024]{2,1,0:T(8,128)(2,1)} %param.15) | copy-start | bytes 1572868
  8.8 26.6 %all-to-all-start = ((bf16[64,2,512]{2,1,0:T(2,128)(2,1)}), bf16[64,2,512]{2,1,0:T(2,128)(2,1)S(1)}, u32[]{:S(2)}, u32[]{:S(2)}) async-start(bf16[64,2,512]{2,1,0:T(2,128)(2,1)} %reshape.1871), calls=%async_computation | async-start | bytes 262144 | tf_op jit(solution)/shard_map/all_to_all | solution.py:19
  31.1 2.3 copy-start.4
  42.0 40.8 %all-to-all-start.2 = ((bf16[128,2,2048]{2,1,0:T(2,128)(2,1)}), bf16[128,2,2048]{2,1,0:T(2,128)(2,1)}, u32[]{:S(2)}, u32[]{:S(2)}) async-start(bf16[128,2,2048]{2,1,0:T(2,128)(2,1)} %reshape.1869), calls=%async_computation.2 | async-start | bytes 2097152 | tf_op jit(solution)/shard_map/all_to_all | solution.py:146
  52.8 65.6 %all-gather.14.cloned.1.call-start = ((), (), s32[]{:S(2)}) async-start(), calls=%async_computation.7 | async-start | bytes 1198080 | tf_op jit(solution)/shard_map/all_gather | solution.py:42
  53.2 1.1 copy-start.1
  55.1 26.0 %copy-start.5 = (bf16[2,8,1024]{2,1,0:T(8,128)(2,1)S(1)}, bf16[2,8,1024]{2,1,0:T(8,128)(2,1)}, u32[]{:S(2)}) copy-start(bf16[2,8,1024]{2,1,0:T(8,128)(2,1)} %param.12) | copy-start | bytes 98308
  86.6 45.7 %copy-start.6 = (bf16[2,8,1024]{2,1,0:T(8,128)(2,1)S(1)}, bf16[2,8,1024]{2,1,0:T(8,128)(2,1)}, u32[]{:S(2)}) copy-start(bf16[2,8,1024]{2,1,0:T(8,128)(2,1)} %param.13) | copy-start | bytes 98308
  124.3 8.5 %copy-start.2 = (bf16[2,8,64]{2,1,0:T(8,128)(2,1)S(1)}, bf16[2,8,64]{2,1,0:T(8,128)(2,1)}, u32[]{:S(2)}) copy-start(bf16[2,8,64]{2,1,0:T(8,128)(2,1)} %param.20) | copy-start | bytes 6148
  132.3 25.8 %copy-start.3 = (f32[1,64]{1,0:T(1,128)S(1)}, f32[1,64]{1,0:T(1,128)}, u32[]{:S(2)}) copy-start(f32[1,64]{1,0:T(1,128)} %param.18) | copy-start | bytes 772
  132.3 31.3 %copy-start.7 = (s32[2,8]{1,0:T(2,128)S(1)}, s32[2,8]{1,0:T(2,128)}, u32[]{:S(2)}) copy-start(s32[2,8]{1,0:T(2,128)} %param.21) | copy-start | bytes 196
  159.0 15.6 %all-to-all-start.5 = ((bf16[64,2,256]{2,1,0:T(2,128)(2,1)}), bf16[64,2,256]{2,1,0:T(2,128)(2,1)S(1)}, u32[]{:S(2)}, u32[]{:S(2)}) async-start(bf16[64,2,256]{2,1,0:T(2,128)(2,1)} %reshape.1875), calls=%async_computation.5 | async-start | bytes 131072 | tf_op jit(solution)/shard_map/all_to_all | solution.py:19
  188.3 28.7 %collective-permute-start.1 = (bf16[8,64]{1,0:T(8,128)(2,1)S(1)}, bf16[8,64]{1,0:T(8,128)(2,1)S(1)}, u32[]{:S(2)}, u32[]{:S(2)}) collective-permute-start(bf16[8,64]{1,0:T(8,128)(2,1)S(1)} %multiply_convert_fusion), channel_id=1, source_target_pairs={{0,128},{128,0},{1,129},{129,1},{2,130},{130,2},{3,131},{131,3},{4... | collective-permute-start | bytes 3080 | tf_op jit(solution)/shard_map/ppermute | solution.py:91
  228.0 2.5 %collective-permute-start = (f32[8]{0:T(128)S(1)}, f32[8]{0:T(128)S(1)}, u32[]{:S(2)}, u32[]{:S(2)}) collective-permute-start(f32[8]{0:T(128)S(1)} %fusion.180), channel_id=1, source_target_pairs={{0,128},{128,0},{1,129},{129,1},{2,130},{130,2},{3,131},{131,3},{4... | collective-permute-start | bytes 104 | tf_op jit(solution)/shard_map/ppermute | solution.py:91
Sparse Core Ops, SparseCore 0:
  81.2 37.1 all-gather.13
where the time goes:
time: 239 us; the launch traced here: 238 us
  blocking collectives  107 us (45%)
  waiting for transfers between devices  47.4 us (20%)
  starting transfers between devices  32.3 us (14%)
  local copies, waits for them, and re-layouts  20.5 us (9%)
  between operations  14.6 us (6%)
  other arithmetic  8.5 us (4%)
  matrix products  7.77 us (3%)
    all_gather x7, blocking collectives, all_in_one(): both, at, found = (lax.all_gather(jnp.concatenate(lines), axis), 0, {})  70.4 us
    all_to_all x4, blocking collectives, sent_to_all(): return lax.all_to_all(copies, axis, split_axis=0, concat_axis=0, tiled=True)  37 us
    all_gather x1, waiting for transfers between devices, all_in_one(): both, at, found = (lax.all_gather(jnp.concatenate(lines), axis), 0, {})  31.9 us
    all_to_all x2, starting transfers between devices, sent_to_all(): return lax.all_to_all(copies, axis, split_axis=0, concat_axis=0, tiled=True)  19.7 us
    all_to_all x2, waiting for transfers between devices, sent_to_all(): return lax.all_to_all(copies, axis, split_axis=0, concat_axis=0, tiled=True)  12.9 us
    all_to_all x1, starting transfers between devices, on_device(): lax.all_to_all(weight_used, GRP_TP, split_axis=1, concat_axis=0, tiled=True)  10.9 us
    unnamed x29, local copies, waits for them, and re-layouts  10.5 us
    all_to_all x2, local copies, waits for them, and re-layouts, on_device(): lax.all_to_all(weight_used, GRP_TP, split_axis=1, concat_axis=0, tiled=True)  7.18 us
  transfers between devices with their start and end apart: 6, of which 5 were waited for; matrix products, arithmetic and copies ran while one was open for 6% of the time, Pallas kernels for 0%

commit v1 on v0

v1 whole, which is shorter than its diff:
```python
import math

import jax
import jax.numpy as jnp
from jax import lax
from jax.sharding import Mesh
from jax.sharding import PartitionSpec as P

D = 8192
KV_HEADS = 8
GROUP = 8
HEAD_SIZE = 128
CHIP = ("grp", "tp_0", "tp_1")
CORE = "tp_2"
GRP_TP = CHIP + (CORE,)
CHIPS = 64
HALF = 4
LOW = -(2.0**100)
BF = jnp.bfloat16
F32 = jnp.float32


def swap(x):
    return lax.ppermute(x, CORE, [(0, 1), (1, 0)])


def exchange(x, axes):
    return lax.all_to_all(x, axes, split_axis=0, concat_axis=0, tiled=True)


def to_every(x, axes, count):
    return exchange(jnp.broadcast_to(x[None], (count, *x.shape)), axes)


def rounded(x):
    return lax.reduce_precision(x, 8, 7)


def by_core(core, mine, other, axis):
    first = jnp.concatenate([mine, other], axis)
    second = jnp.concatenate([other, mine], axis)
    return jnp.where(core == 0, first, second)


def on_device(
    queries,
    step_token_keys,
    step_token_values,
    stored_key_cache,
    stored_value_cache,
    lengths,
    wo_sides,
    gain_sides,
    head,
    resid,
    actions,
):
    place = lax.axis_index(GRP_TP)
    chip = lax.axis_index(CHIP)
    core = lax.axis_index(CORE)
    side = lax.axis_index("role")
    step = 1 - side
    scale = 1.0 / math.sqrt(HEAD_SIZE)
    slots = stored_key_cache.shape[1]
    row0 = core * HALF
    far0 = (1 - core) * HALF

    def rows_of(x, start, axis=0):
        return lax.dynamic_slice_in_dim(x, start, HALF, axis)

    q_now = lax.dynamic_index_in_dim(queries, step, 0, keepdims=False)
    r_now = lax.dynamic_index_in_dim(resid, step, 0, keepdims=False)
    pair = jnp.stack([q_now, r_now])
    pair_kept = rows_of(pair, row0, 1)
    pair_got = swap(rows_of(pair, far0, 1))
    q_r = by_core(core, pair_kept, pair_got, 2)
    q_chip, r_chip = q_r[0], q_r[1].astype(F32)

    keys = jnp.concatenate(
        [rows_of(stored_key_cache, row0), swap(rows_of(stored_key_cache, far0))], 1
    )
    values = jnp.concatenate(
        [rows_of(stored_value_cache, row0), swap(rows_of(stored_value_cache, far0))], 1
    )
    keys = keys.reshape(HALF, 2 * slots, KV_HEADS, HEAD_SIZE)
    values = values.reshape(HALF, 2 * slots, KV_HEADS, HEAD_SIZE)
    w_mine = wo_sides[0]
    w_far = swap(w_mine)
    gain = gain_sides[0]
    gain_far = swap(gain)
    gain_chip = by_core(core, gain, gain_far, 0)

    q = to_every(q_chip, CHIP, CHIPS)
    q = q.reshape(KV_HEADS, GROUP, HALF, HEAD_SIZE)
    lens = rows_of(lengths, row0)
    at = jnp.arange(slots, dtype=jnp.int32)
    position = jnp.concatenate([place * slots + at, (place + 1 - 2 * core) * slots + at])
    valid = (position[None, :] < lens[:, None])[:, None, None, :]
    scores = jnp.einsum("kgrd,rskd->rkgs", q, keys, preferred_element_type=F32) * scale
    scores = jnp.where(valid, scores, LOW)
    top = rounded(jnp.max(scores, axis=-1, keepdims=True))
    probs = jnp.exp(scores - top) * valid
    total = jnp.sum(probs, axis=-1, keepdims=True)
    part = jnp.einsum(
        "rkgs,rskd->kgrd", probs.astype(BF), values, preferred_element_type=F32
    ).reshape(CHIPS, HALF, HEAD_SIZE)

    def by_head(x):
        return jnp.transpose(x, (1, 2, 0, 3)).reshape(CHIPS, HALF, 1)

    top, total = by_head(top), by_head(total)
    total_hi = rounded(total)
    total_lo = total - total_hi
    gain_hi = rounded(gain_chip)
    gain_pack = jnp.concatenate([gain_hi, gain_chip - gain_hi]).reshape(1, HALF, 64)
    stats = jnp.concatenate(
        [
            jnp.broadcast_to(top, (CHIPS, HALF, 16)),
            jnp.broadcast_to(total_hi, (CHIPS, HALF, 16)),
            jnp.broadcast_to(total_lo, (CHIPS, HALF, 32)),
            jnp.broadcast_to(gain_pack, (CHIPS, HALF, 64)),
        ],
        -1,
    )
    sent = jnp.concatenate([part.astype(BF), stats.astype(BF)], 1)
    got = exchange(sent, CHIP).astype(F32)
    tops, totals = got[:, HALF:, 0:1], got[:, HALF:, 16:17] + got[:, HALF:, 32:33]
    gains = got[:, HALF:, 64:].reshape(CHIPS, 2, HEAD_SIZE).sum(1)
    kv = chip // GROUP
    fresh_k = lax.dynamic_slice(
        step_token_keys, (0, row0, kv * HEAD_SIZE), (2, HALF, HEAD_SIZE)
    ).astype(F32)
    fresh_v = lax.dynamic_slice(
        step_token_values, (0, row0, kv * HEAD_SIZE), (2, HALF, HEAD_SIZE)
    ).astype(F32)
    live = (jnp.arange(2) <= step)[:, None, None]
    fresh_s = jnp.sum(fresh_k * q_chip.astype(F32)[None], -1, keepdims=True) * scale
    fresh_s = jnp.where(live, fresh_s, LOW)
    peak = jnp.maximum(jnp.max(tops, 0), jnp.max(fresh_s, 0))
    factor = jnp.exp(tops - peak[None])
    fresh_p = jnp.exp(fresh_s - peak[None]) * live
    below = jnp.sum(totals * factor, 0) + jnp.sum(fresh_p, 0)
    above = jnp.sum(got[:, :HALF] * factor, 0) + jnp.sum(fresh_p * fresh_v, 0)
    attended = (above / below).astype(BF)

    a0, a1 = attended[:, :64], attended[:, 64:]
    a_mine = jnp.where(core == 0, a0, a1)
    a_far = jnp.where(core == 0, a1, a0)
    share = jnp.dot(a_mine, w_mine, preferred_element_type=F32) + jnp.dot(
        a_far, w_far, preferred_element_type=F32
    )
    share = share.astype(BF).reshape(HALF, CHIPS, HEAD_SIZE).transpose(1, 0, 2)
    state = jnp.sum(exchange(share, CHIP).astype(F32), 0) + r_chip

    mine = to_every(state.astype(BF), CHIP, CHIPS)
    whole = by_core(core, mine, swap(mine), 1).astype(F32)
    square = jnp.sum(jnp.sum(whole * whole, 0), -1, keepdims=True)
    inverse = lax.rsqrt(square / D + 1e-05)
    normed = (whole * inverse[None] * gains[:, None, :]).astype(BF)
    own = lax.dynamic_index_in_dim(normed, chip, 0, keepdims=False)
    own = jnp.where(core == 0, own[:, :64], own[:, 64:])
    to_side = [(0, 1), (1, 0)]
    peer_normed = lax.ppermute(own, "role", to_side)
    logits = jnp.dot(
        normed.transpose(1, 0, 2).reshape(8, D), head, preferred_element_type=F32
    )

    width = head.shape[1]
    action = lax.dynamic_index_in_dim(actions, step, 0, keepdims=False)
    ids = place * width + jnp.arange(width, dtype=jnp.int32)
    target = jnp.sum(jnp.where(ids[None, :] == action[:, None], logits, 0.0), -1)
    high = jnp.max(logits, -1)
    expsum = jnp.sum(jnp.exp(logits - high[:, None]), -1)
    local = jnp.stack([high, expsum, target])
    far = swap(local)
    both = jnp.maximum(local[0], far[0])
    sums = local[1] * jnp.exp(local[0] - both) + far[1] * jnp.exp(far[0] - both)
    packed = jnp.concatenate([both, sums, local[2] + far[2], jnp.zeros_like(sums)])
    heard = to_every(packed[None], ("role",) + CHIP, 2 * CHIPS).reshape(2, CHIPS, 4, 8)
    heard = lax.dynamic_index_in_dim(heard, 1 - side, 0, keepdims=False)
    largest = jnp.max(heard[:, 0], 0)
    sums = jnp.sum(heard[:, 1] * jnp.exp(heard[:, 0] - largest), 0)
    prob = jnp.sum(heard[:, 2], 0) - largest - jnp.log(sums)
    return prob[None], peer_normed[None]


def solution(mesh):
    split = Mesh(
        mesh.devices.reshape(mesh.shape["role"], mesh.shape["grp"], 4, 8, 2),
        ("role", "grp", "tp_0", "tp_1", "tp_2"),
    )
    return jax.shard_map(
        on_device,
        mesh=split,
        in_specs=(
            P(None, None, GRP_TP),
            P(),
            P(),
            P(None, GRP_TP, None),
            P(None, GRP_TP, None),
            P(),
            P("role", GRP_TP, None),
            P("role", GRP_TP),
            P(None, GRP_TP),
            P(None, None, GRP_TP),
            P(),
        ),
        out_specs=(P("role", None), P("role", None, GRP_TP)),
        check_vma=False,
    )
```

time: 239 us -> 121 us (0.51)
  blocking collectives: 107 us -> 15 us
  between operations: 14.6 us -> 0.95 us
  local copies, waits for them, and re-layouts: 20.5 us -> 8.33 us
  starting transfers between devices: 32.3 us -> 38.7 us
  waiting for transfers between devices: 47.4 us -> 43.6 us
  other arithmetic: 8.5 us -> 5.73 us
    all_gather x7 -> x0, blocking collectives: 70.4 us -> none  [all_in_one(): both, at, found = (lax.all_gather(jnp.concatenate(lines), axis), 0, {})]
    all_gather x1 -> x0, waiting for transfers between devices: 31.9 us -> none  [all_in_one(): both, at, found = (lax.all_gather(jnp.concatenate(lines), axis), 0, {})]
    all_to_all x3 -> x4, waiting for transfers between devices: 14.3 us -> 40.4 us  [exchange(): return lax.all_to_all(x, axes, split_axis=0, concat_axis=0, tiled=True)]
    all_to_all x4 -> x1, blocking collectives: 37 us -> 15 us  [exchange(): return lax.all_to_all(x, axes, split_axis=0, concat_axis=0, tiled=True)]
    unnamed x29 -> x5, local copies, waits for them, and re-layouts: 10.5 us -> 0.59 us
    ppermute x2 -> x8, starting transfers between devices: 1.64 us -> 10.8 us  [the longest x7 9.85 us: swap(): return lax.ppermute(x, CORE, [(0, 1), (1, 0)])]
    all_to_all x3 -> x2, local copies, waits for them, and re-layouts: 7.24 us -> 0.27 us  [exchange(): return lax.all_to_all(x, axes, split_axis=0, concat_axis=0, tiled=True)]
    convert_element_type x12 -> x6, other arithmetic: 4.65 us -> 0.5 us  [the longest x1 0.22 us: on_device(): probs.astype(BF)]
  transfers between devices with their start and end apart: 6 -> 12, of which waited for: 5 -> 7; matrix products, arithmetic and copies ran while one was open for 6% -> 10% of each run, Pallas kernels for 0% -> 0%
where the time goes in v1:
time: 121 us; the launch traced here: 120 us
  waiting for transfers between devices  43.6 us (36%)
  starting transfers between devices  38.7 us (32%)
  blocking collectives  15 us (12%)
  local copies, waits for them, and re-layouts  8.33 us (7%)
  matrix products  8.02 us (7%)
  other arithmetic  5.73 us (5%)
    all_to_all x4, waiting for transfers between devices, exchange(): return lax.all_to_all(x, axes, split_axis=0, concat_axis=0, tiled=True)  40.4 us
    all_to_all x4, starting transfers between devices, exchange(): return lax.all_to_all(x, axes, split_axis=0, concat_axis=0, tiled=True)  28 us
    all_to_all x1, blocking collectives, exchange(): return lax.all_to_all(x, axes, split_axis=0, concat_axis=0, tiled=True)  15 us
    ppermute x7, starting transfers between devices, swap(): return lax.ppermute(x, CORE, [(0, 1), (1, 0)])  9.85 us
    dot_general x1, matrix products, on_device(): jnp.dot(normed.transpose(1, 0, 2).reshape(8, D), head, preferred_element_...  5.72 us
    dynamic_slice x3, local copies, waits for them, and re-layouts, rows_of(): return lax.dynamic_slice_in_dim(x, start, HALF, axis)  2.87 us
  transfers between devices with their start and end apart: 12, of which 7 were waited for; matrix products, arithmetic and copies ran while one was open for 10% of the time, Pallas kernels for 0%

profile of v1, /device:TPU:1, one launch (start us, length us, event | category | flops | bytes accessed | tf_op | source)
XLA Modules:
  0.0 120.3 jit_solution(849471258008190399)
XLA Ops:
  0.7 0.8 constant_dynamic-slice_fusion.7
  1.5 3.3 %collective-permute-start.1 = (bf16[2,4,64]{2,1,0:T(4,128)(2,1)S(1)}, bf16[2,4,64]{2,1,0:T(4,128)(2,1)S(1)}, u32[]{:S(2)}, u32[]{:S(2)}) collective-permute-start(bf16[2,4,64]{2,1,0:T(4,128)(2,1)S(1)} %get-tuple-element.19), channel_id=1, source_target_pairs={{0,1},{1,0},{2,3},{3,2},{4,5},{5,4},{6,7},{7,6},{8,9},{9,8},{10,11... | collective-permute-start | bytes 3080 | tf_op jit(solution)/shard_map/ppermute | solution.py:24
  4.8 1.1 constant_dynamic-slice_fusion.6
  6.0 1.1 constant_dynamic-slice_fusion.10
  7.1 0.6 collective-permute-start
  8.1 0.7 dynamic_slice.48
  9.0 0.8 broadcast_select_fusion.1
  10.0 0.6 broadcast_in_dim.58
  10.7 12.6 %all-to-all-start = ((bf16[64,4,128]{2,1,0:T(4,128)(2,1)}), bf16[64,4,128]{2,1,0:T(4,128)(2,1)S(1)}, u32[]{:S(2)}, u32[]{:S(2)}) async-start(bf16[64,4,128]{2,1,0:T(4,128)(2,1)} %broadcast_in_dim.58), calls=%async_computation | async-start | bytes 131072 | tf_op jit(solution)/shard_map/all_to_all | solution.py:28
  23.3 11.1 %all-to-all-done = bf16[64,4,128]{2,1,0:T(4,128)(2,1)S(1)} async-done(((bf16[64,4,128]{2,1,0:T(4,128)(2,1)}), bf16[64,4,128]{2,1,0:T(4,128)(2,1)S(1)}, u32[]{:S(2)}, u32[]{:S(2)}) %all-to-all-start) | async-done | bytes 65568 | tf_op jit(solution)/shard_map/all_to_all | solution.py:28
  34.4 1.4 %fusion.53 = (f32[4,8,8]{2,1,0:T(8,128)S(1)}, f32[4,8,8,64]{3,2,1,0:T(8,128)S(1)}) fusion(bf16[64,4,128]{2,1,0:T(4,128)(2,1)S(1)} %all-to-all-done, pred[4,64]{1,0:T(4,128)(4,1)S(1)} %get-tuple-element.7, bf16[4,32,1024]{2,1,0:T(8,128)(2,1)} %collective-permute-done.2, bf16[4,32,1024]{2,1,0:T(8,128)(2,1)S(1)} %get-tuple-element.12), kind=kOutput, calls=%fused_computation.120 | convolution fusion | flops 5291776 | bytes 656640 | tf_op jit(solution)/shard_map/kgrd,rskd->rkgs/dot_general | solution.py:99
  37.0 0.7 copy.61
  37.7 4.6 %all-to-all-start.1 = ((bf16[64,8,128]{2,1,0:T(8,128)(2,1)}), bf16[64,8,128]{2,1,0:T(8,128)(2,1)S(1)}, u32[]{:S(2)}, u32[]{:S(2)}) async-start(bf16[64,8,128]{2,1,0:T(8,128)(2,1)} %copy.61), calls=%async_computation.1 | async-start | bytes 262144 | tf_op jit(solution)/shard_map/all_to_all | solution.py:28
  42.4 0.9 multiply_reduce_fusion.1
  43.3 10.5 %all-to-all-done.1 = bf16[64,8,128]{2,1,0:T(8,128)(2,1)S(1)} async-done(((bf16[64,8,128]{2,1,0:T(8,128)(2,1)}), bf16[64,8,128]{2,1,0:T(8,128)(2,1)S(1)}, u32[]{:S(2)}, u32[]{:S(2)}) %all-to-all-start.1) | async-done | bytes 131104 | tf_op jit(solution)/shard_map/all_to_all | solution.py:28
  54.3 0.8 multiply_reduce_fusion
  56.4 15.0 %all_to_all.25 = bf16[64,4,128]{2,1,0:T(4,128)(2,1)S(1)} all-to-all(bf16[64,4,128]{2,1,0:T(4,128)(2,1)S(1)} %fusion.2), channel_id=1, replica_groups=mesh['role'=2,'grp'=2,'tp_0'=4,'tp_1'=8,'tp_2'=2] {'grp','tp_0','tp_1'}, dimensions={0} | all-to-all | bytes 131072 | tf_op jit(solution)/shard_map/all_to_all | solution.py:28
  71.5 0.6 broadcast_in_dim.112
  72.1 4.6 %all-to-all-start.3 = ((bf16[64,4,128]{2,1,0:T(4,128)(2,1)}), bf16[64,4,128]{2,1,0:T(4,128)(2,1)S(1)}, u32[]{:S(2)}, u32[]{:S(2)}) async-start(bf16[64,4,128]{2,1,0:T(4,128)(2,1)} %broadcast_in_dim.112), calls=%async_computation.3 | async-start | bytes 131072 | tf_op jit(solution)/shard_map/all_to_all | solution.py:28
  76.7 11.0 %all-to-all-done.3 = bf16[64,4,128]{2,1,0:T(4,128)(2,1)S(1)} async-done(((bf16[64,4,128]{2,1,0:T(4,128)(2,1)}), bf16[64,4,128]{2,1,0:T(4,128)(2,1)S(1)}, u32[]{:S(2)}, u32[]{:S(2)}) %all-to-all-start.3) | async-done | bytes 65568 | tf_op jit(solution)/shard_map/all_to_all | solution.py:28
  87.7 4.9 %collective-permute-start.5 = (bf16[64,4,128]{2,1,0:T(4,128)(2,1)S(1)}, bf16[64,4,128]{2,1,0:T(4,128)(2,1)S(1)}, u32[]{:S(2)}, u32[]{:S(2)}) collective-permute-start(bf16[64,4,128]{2,1,0:T(4,128)(2,1)S(1)} %all-to-all-done.3), channel_id=1, source_target_pairs={{0,1},{1,0},{2,3},{3,2},{4,5},{5,4},{6,7},{7,6},{8,9},{9,8},{10,11... | collective-permute-start | bytes 196616 | tf_op jit(solution)/shard_map/ppermute | solution.py:24
  93.0 0.5 collective-permute-done.5
  93.9 5.7 %fusion.54 = (f32[8]{0:T(128)S(1)}, f32[8,501]{1,0:T(8,128)S(1)}) fusion(bf16[8192,501]{0,1:T(8,128)(2,1)} %param.19, bf16[64,8,128]{2,1,0:T(8,128)(2,1)S(1)} %fusion.10), kind=kOutput, calls=%fused_computation.121 | convolution fusion | flops 65671072 | bytes 8355520 | tf_op jit(solution)/shard_map/dot_general | solution.py:164
  99.9 0.4 collective-permute-start.6
  100.3 0.8 collective-permute-done.6
  101.2 0.7 broadcast_in_dim.114
  101.9 6.2 %all-to-all-start.4 = ((f32[128,1,32]{2,1,0:T(1,128)}), f32[128,1,32]{2,1,0:T(1,128)S(1)}, u32[]{:S(2)}, u32[]{:S(2)}) async-start(f32[128,1,32]{2,1,0:T(1,128)} %broadcast_in_dim.114), calls=%async_computation.4 | async-start | bytes 131072 | tf_op jit(solution)/shard_map/all_to_all | solution.py:28
  108.2 0.9 collective-permute-start.7
  109.1 1.8 %collective-permute-done.7 = bf16[8,64]{1,0:T(8,128)(2,1)S(1)} collective-permute-done((bf16[8,64]{1,0:T(8,128)(2,1)S(1)}, bf16[8,64]{1,0:T(8,128)(2,1)S(1)}, u32[]{:S(2)}, u32[]{:S(2)}) %collective-permute-start.7) | collective-permute-done | bytes 1056 | tf_op jit(solution)/shard_map/ppermute | solution.py:163
  110.9 7.7 %all-to-all-done.4 = f32[128,1,32]{2,1,0:T(1,128)S(1)} async-done(((f32[128,1,32]{2,1,0:T(1,128)}), f32[128,1,32]{2,1,0:T(1,128)S(1)}, u32[]{:S(2)}, u32[]{:S(2)}) %all-to-all-start.4) | async-done | bytes 16416 | tf_op jit(solution)/shard_map/all_to_all | solution.py:28
  119.2 0.5 subtract_bitcast_fusion
  119.7 0.6 copy.90
  (72 shorter events, 5.7 us)
Async XLA Ops:
  0.6 92.0 %copy-start = (s32[2,8]{1,0:T(2,128)S(1)}, s32[2,8]{1,0:T(2,128)}, u32[]{:S(2)}) copy-start(s32[2,8]{1,0:T(2,128)} %param.21) | copy-start | bytes 196
  0.6 55.1 %copy-start.1 = (bf16[1,64,8192]{2,1,0:T(8,128)(2,1)S(1)}, bf16[1,64,8192]{2,1,0:T(8,128)(2,1)}, u32[]{:S(2)}) copy-start(bf16[1,64,8192]{2,1,0:T(8,128)(2,1)} %param.17) | copy-start | bytes 3145732
  1.5 8.5 %collective-permute-start.1 = (bf16[2,4,64]{2,1,0:T(4,128)(2,1)S(1)}, bf16[2,4,64]{2,1,0:T(4,128)(2,1)S(1)}, u32[]{:S(2)}, u32[]{:S(2)}) collective-permute-start(bf16[2,4,64]{2,1,0:T(4,128)(2,1)S(1)} %get-tuple-element.19), channel_id=1, source_target_pairs={{0,1},{1,0},{2,3},{3,2},{4,5},{5,4},{6,7},{7,6},{8,9},{9,8},{10,11... | collective-permute-start | bytes 3080 | tf_op jit(solution)/shard_map/ppermute | solution.py:24
  5.9 28.6 %collective-permute-start.2 = (bf16[4,32,1024]{2,1,0:T(8,128)(2,1)S(1)}, bf16[4,32,1024]{2,1,0:T(8,128)(2,1)}, u32[]{:S(2)}, u32[]{:S(2)}) collective-permute-start(bf16[4,32,1024]{2,1,0:T(8,128)(2,1)S(1)} %get-tuple-element.13), channel_id=1, source_target_pairs={{0,1},{1,0},{2,3},{3,2},{4,5},{5,4},{6,7},{7,6},{8,9},{9,8},{10,11... | collective-permute-start | bytes 786440 | tf_op jit(solution)/shard_map/ppermute | solution.py:24
  7.1 29.2 %collective-permute-start = (bf16[4,32,1024]{2,1,0:T(8,128)(2,1)S(1)}, bf16[4,32,1024]{2,1,0:T(8,128)(2,1)S(1)}, u32[]{:S(2)}, u32[]{:S(2)}) collective-permute-start(bf16[4,32,1024]{2,1,0:T(8,128)(2,1)S(1)} %get-tuple-element.11), channel_id=1, source_target_pairs={{0,1},{1,0},{2,3},{3,2},{4,5},{5,4},{6,7},{7,6},{8,9},{9,8},{10,11... | collective-permute-start | bytes 786440 | tf_op jit(solution)/shard_map/ppermute | solution.py:24
  7.6 1.4 %collective-permute-start.3 = (f32[64]{0:T(128)}, f32[64]{0:T(128)S(1)}, u32[]{:S(2)}, u32[]{:S(2)}) collective-permute-start(f32[64]{0:T(128)} %bitcast.131), channel_id=1, source_target_pairs={{0,1},{1,0},{2,3},{3,2},{4,5},{5,4},{6,7},{7,6},{8,9},{9,8},{10,11... | collective-permute-start | bytes 776 | tf_op jit(solution)/shard_map/ppermute | solution.py:24
  7.7 48.3 %collective-permute-start.4 = (bf16[64,8192]{1,0:T(8,128)(2,1)}, bf16[64,8192]{1,0:T(8,128)(2,1)S(1)}, u32[]{:S(2)}, u32[]{:S(2)}) collective-permute-start(bf16[64,8192]{1,0:T(8,128)(2,1)} %bitcast.122), channel_id=1, source_target_pairs={{0,1},{1,0},{2,3},{3,2},{4,5},{5,4},{6,7},{7,6},{8,9},{9,8},{10,11... | collective-permute-start | bytes 3145736 | tf_op jit(solution)/shard_map/ppermute | solution.py:24
  10.7 23.8 %all-to-all-start = ((bf16[64,4,128]{2,1,0:T(4,128)(2,1)}), bf16[64,4,128]{2,1,0:T(4,128)(2,1)S(1)}, u32[]{:S(2)}, u32[]{:S(2)}) async-start(bf16[64,4,128]{2,1,0:T(4,128)(2,1)} %broadcast_in_dim.58), calls=%async_computation | async-start | bytes 131072 | tf_op jit(solution)/shard_map/all_to_all | solution.py:28
  37.7 16.1 %all-to-all-start.1 = ((bf16[64,8,128]{2,1,0:T(8,128)(2,1)}), bf16[64,8,128]{2,1,0:T(8,128)(2,1)S(1)}, u32[]{:S(2)}, u32[]{:S(2)}) async-start(bf16[64,8,128]{2,1,0:T(8,128)(2,1)} %copy.61), calls=%async_computation.1 | async-start | bytes 262144 | tf_op jit(solution)/shard_map/all_to_all | solution.py:28
  72.1 15.6 %all-to-all-start.3 = ((bf16[64,4,128]{2,1,0:T(4,128)(2,1)}), bf16[64,4,128]{2,1,0:T(4,128)(2,1)S(1)}, u32[]{:S(2)}, u32[]{:S(2)}) async-start(bf16[64,4,128]{2,1,0:T(4,128)(2,1)} %broadcast_in_dim.112), calls=%async_computation.3 | async-start | bytes 131072 | tf_op jit(solution)/shard_map/all_to_all | solution.py:28
  87.7 5.8 %collective-permute-start.5 = (bf16[64,4,128]{2,1,0:T(4,128)(2,1)S(1)}, bf16[64,4,128]{2,1,0:T(4,128)(2,1)S(1)}, u32[]{:S(2)}, u32[]{:S(2)}) collective-permute-start(bf16[64,4,128]{2,1,0:T(4,128)(2,1)S(1)} %all-to-all-done.3), channel_id=1, source_target_pairs={{0,1},{1,0},{2,3},{3,2},{4,5},{5,4},{6,7},{7,6},{8,9},{9,8},{10,11... | collective-permute-start | bytes 196616 | tf_op jit(solution)/shard_map/ppermute | solution.py:24
  99.9 1.3 %collective-permute-start.6 = (f32[3,8]{1,0:T(4,128)S(1)}, f32[3,8]{1,0:T(4,128)S(1)}, u32[]{:S(2)}, u32[]{:S(2)}) collective-permute-start(f32[3,8]{1,0:T(4,128)S(1)} %pad_maximum_fusion), channel_id=1, source_target_pairs={{0,1},{1,0},{2,3},{3,2},{4,5},{5,4},{6,7},{7,6},{8,9},{9,8},{10,11... | collective-permute-start | bytes 296 | tf_op jit(solution)/shard_map/ppermute | solution.py:24
  101.9 16.8 %all-to-all-start.4 = ((f32[128,1,32]{2,1,0:T(1,128)}), f32[128,1,32]{2,1,0:T(1,128)S(1)}, u32[]{:S(2)}, u32[]{:S(2)}) async-start(f32[128,1,32]{2,1,0:T(1,128)} %broadcast_in_dim.114), calls=%async_computation.4 | async-start | bytes 131072 | tf_op jit(solution)/shard_map/all_to_all | solution.py:28
  108.2 2.8 %collective-permute-start.7 = (bf16[8,64]{1,0:T(8,128)(2,1)S(1)}, bf16[8,64]{1,0:T(8,128)(2,1)S(1)}, u32[]{:S(2)}, u32[]{:S(2)}) collective-permute-start(bf16[8,64]{1,0:T(8,128)(2,1)S(1)} %slice_select_fusion), channel_id=1, source_target_pairs={{0,128},{128,0},{1,129},{129,1},{2,130},{130,2},{3,131},{131,3},{4... | collective-permute-start | bytes 3080 | tf_op jit(solution)/shard_map/ppermute | solution.py:163

commit v2 on v1

v2 whole, which is shorter than its diff:
```python
import math

import jax
import jax.numpy as jnp
from jax import lax
from jax.experimental import pallas as pl
from jax.experimental.pallas import tpu as pltpu
from jax.sharding import Mesh
from jax.sharding import PartitionSpec as P

D = 8192
KV_HEADS = 8
GROUP = 8
HEAD_SIZE = 128
CHIP = ("grp", "tp_0", "tp_1")
CORE = "tp_2"
GRP_TP = CHIP + (CORE,)
CHIPS = 64
HALF = 4
LOW = -(2.0**100)
BF = jnp.bfloat16
F32 = jnp.float32


def swap(x):
    return lax.ppermute(x, CORE, [(0, 1), (1, 0)])


def exchange(x, axes):
    return lax.all_to_all(x, axes, split_axis=0, concat_axis=0, tiled=True)


def to_every(x, axes, count):
    return exchange(jnp.broadcast_to(x[None], (count, *x.shape)), axes)


def rounded(x):
    return lax.reduce_precision(x, 8, 7)


def by_core(core, mine, other, axis):
    first = jnp.concatenate([mine, other], axis)
    second = jnp.concatenate([other, mine], axis)
    return jnp.where(core == 0, first, second)


NT = (((1,), (1,)), ((), ()))
VMEM = pl.BlockSpec(memory_space=pltpu.VMEM)
SMEM = pl.BlockSpec(memory_space=pltpu.SMEM)


def call(kernel, shapes, specs, limit, cost, *operands):
    return pl.pallas_call(
        kernel,
        out_shape=shapes,
        in_specs=specs,
        out_specs=jax.tree.map(lambda _: VMEM, shapes),
        compiler_params=pltpu.CompilerParams(vmem_limit_bytes=limit * 2**20),
        cost_estimate=pl.CostEstimate(
            flops=cost, bytes_accessed=cost // 16, transcendentals=0
        ),
    )(*operands)


def attend_kernel(core_ref, q_ref, k_ref, kf_ref, v_ref, vf_ref, ok_ref, pack_ref, out_ref):
    base = core_ref[0] * HALF
    row = lax.broadcasted_iota(jnp.int32, (32, 256), 0)
    col = lax.broadcasted_iota(jnp.int32, (32, 256), 1)
    valid = ((row % HALF) == (col // 64)) & (ok_ref[...] > 0)
    lane = lax.broadcasted_iota(jnp.int32, (32, 128), 1)
    upper = lax.broadcasted_iota(jnp.int32, (4, 8, 128), 1) < HALF
    pack = jnp.concatenate([pack_ref[...]] * 4, 0)
    for kv in range(KV_HEADS):
        cols = slice(kv * HEAD_SIZE, (kv + 1) * HEAD_SIZE)

        def both(near, far):
            parts = []
            for r in range(HALF):
                parts += [near[base + r, :, cols], far[base + r, :, cols]]
            return jnp.concatenate(parts, 0)

        q = q_ref[kv * 32 : (kv + 1) * 32, :]
        s = lax.dot_general(q, both(k_ref, kf_ref), NT, preferred_element_type=F32)
        s = jnp.where(valid, s * (1.0 / math.sqrt(HEAD_SIZE)), LOW)
        top = jnp.max(s, 1, keepdims=True).astype(BF).astype(F32)
        p = jnp.where(valid, jnp.exp(s - top), 0.0)
        total = jnp.sum(p, 1, keepdims=True)
        total_hi = total.astype(BF).astype(F32)
        acc = jnp.dot(p.astype(BF), both(v_ref, vf_ref), preferred_element_type=F32)
        stats = jnp.where(lane < 32, total_hi, total - total_hi)
        stats = jnp.where(lane < 16, top, jnp.where(lane < 64, stats, pack))
        acc, stats = acc.reshape(4, 8, 128), stats.reshape(4, 8, 128)
        even = jnp.where(upper, acc, pltpu.roll(stats, HALF, 1)).astype(BF)
        odd = jnp.where(upper, pltpu.roll(acc, HALF, 1), stats).astype(BF)
        for t in range(4):
            out_ref[kv * 8 + 2 * t] = even[t]
            out_ref[kv * 8 + 2 * t + 1] = odd[t]


def merge_kernel(step_ref, got_ref, q_ref, fk_ref, fv_ref, out_ref):
    x = got_ref[...].astype(F32)
    stats = pltpu.roll(x, HALF, 1)
    tops = stats[:, :, 0:1]
    totals = stats[:, :, 16:17] + stats[:, :, 32:33]
    q = q_ref[...]
    scale = 1.0 / math.sqrt(HEAD_SIZE)
    s0 = jnp.sum(fk_ref[0] * q, 1, keepdims=True) * scale
    s1 = jnp.sum(fk_ref[1] * q, 1, keepdims=True) * scale
    second = step_ref[0] >= 1
    s1 = jnp.where(second, s1, LOW)
    peak = jnp.maximum(jnp.max(tops, 0), jnp.maximum(s0, s1))
    factor = jnp.exp(tops - peak[None])
    p0 = jnp.exp(s0 - peak)
    p1 = jnp.where(second, jnp.exp(s1 - peak), 0.0)
    below = jnp.sum(totals * factor, 0) + p0 + p1
    above = jnp.sum(x * factor, 0) + p0 * fv_ref[0] + p1 * fv_ref[1]
    row = lax.broadcasted_iota(jnp.int32, (8, 128), 0)
    out_ref[...] = jnp.where(row < HALF, above / below, 0.0).astype(BF)


def head_kernel(u_ref, head_ref, action_ref, out_ref):
    u = jnp.concatenate([u_ref[i] for i in range(CHIPS)], 1)
    logits = lax.dot_general(head_ref[...], u, NT, preferred_element_type=F32)
    ids = lax.broadcasted_iota(jnp.int32, logits.shape, 0)
    high = jnp.max(logits, 0, keepdims=True)
    out_ref[0:1, :] = high
    out_ref[1:2, :] = jnp.sum(jnp.exp(logits - high), 0, keepdims=True)
    out_ref[2:3, :] = jnp.sum(
        jnp.where(ids == action_ref[...], logits, 0.0), 0, keepdims=True
    )


def on_device(
    queries,
    step_token_keys,
    step_token_values,
    stored_key_cache,
    stored_value_cache,
    lengths,
    wo_sides,
    gain_sides,
    head,
    resid,
    actions,
):
    place = lax.axis_index(GRP_TP)
    chip = lax.axis_index(CHIP)
    core = lax.axis_index(CORE)
    side = lax.axis_index("role")
    step = 1 - side
    slots = stored_key_cache.shape[1]
    row0 = core * HALF

    def rows_of(x, start, axis=0):
        return lax.dynamic_slice_in_dim(x, start, HALF, axis)

    def chip_rows(x, far):
        near = rows_of(lax.dynamic_index_in_dim(x, step, 0, keepdims=False), row0)
        far = rows_of(lax.dynamic_index_in_dim(far, step, 0, keepdims=False), row0)
        return by_core(core, near, far, 1)

    q_chip = chip_rows(queries, swap(queries))
    q = to_every(q_chip, CHIP, CHIPS).reshape(CHIPS * HALF, HEAD_SIZE)

    keys, values, w_mine, gain, resid, lengths, _ = lax.optimization_barrier(
        (stored_key_cache, stored_value_cache, wo_sides[0], gain_sides[0], resid, lengths, q_chip)
    )
    keys_far, values_far, w_far = swap(keys), swap(values), swap(w_mine)
    gain_chip = by_core(core, gain, swap(gain), 0)
    r_chip = chip_rows(resid, swap(resid)).astype(F32)

    lens = rows_of(lengths, row0)
    at = jnp.arange(slots, dtype=jnp.int32)
    position = jnp.concatenate([place * slots + at, (place + 1 - 2 * core) * slots + at])
    valid = (position[None, :] < lens[:, None]).astype(F32).reshape(1, 4 * 2 * slots)
    gain_hi = rounded(gain_chip)
    pack = jnp.concatenate([gain_hi, gain_chip - gain_hi]).reshape(HALF, 64)
    pack = jnp.concatenate([jnp.zeros_like(pack), pack], 1)
    pack = jnp.concatenate([pack, pack], 0)
    sent = call(
        attend_kernel,
        jax.ShapeDtypeStruct((CHIPS, 8, HEAD_SIZE), BF),
        [SMEM] + [VMEM] * 7,
        16,
        2 * 2 * 256 * 256 * 128,
        core[None],
        q,
        keys,
        keys_far,
        values,
        values_far,
        valid,
        pack,
    )
    got = exchange(sent, CHIP)
    gains = got[:, HALF:, 64:].astype(F32).reshape(CHIPS, 2, HEAD_SIZE).sum(1)
    kv = chip // GROUP

    def fresh(x):
        x = lax.dynamic_slice(x, (0, row0, kv * HEAD_SIZE), (2, HALF, HEAD_SIZE))
        return jnp.pad(x.astype(F32), ((0, 0), (0, HALF), (0, 0)))

    attended = call(
        merge_kernel,
        jax.ShapeDtypeStruct((8, HEAD_SIZE), BF),
        [SMEM] + [VMEM] * 4,
        8,
        CHIPS * 8 * HEAD_SIZE * 8,
        step[None],
        got,
        jnp.pad(q_chip.astype(F32), ((0, HALF), (0, 0))),
        fresh(step_token_keys),
        fresh(step_token_values),
    )[:HALF]

    a0, a1 = attended[:, :64], attended[:, 64:]
    a_mine = jnp.where(core == 0, a0, a1)
    a_far = jnp.where(core == 0, a1, a0)
    share = jnp.dot(a_mine, w_mine, preferred_element_type=F32) + jnp.dot(
        a_far, w_far, preferred_element_type=F32
    )
    share = share.astype(BF).reshape(HALF, CHIPS, HEAD_SIZE).transpose(1, 0, 2)
    state = jnp.sum(exchange(share, CHIP).astype(F32), 0) + r_chip

    mine = to_every(state.astype(BF), CHIP, CHIPS)
    whole = by_core(core, mine, swap(mine), 1).astype(F32)
    square = jnp.sum(jnp.sum(whole * whole, 0), -1, keepdims=True)
    inverse = lax.rsqrt(square / D + 1e-05)
    normed = (whole * inverse[None] * gains[:, None, :]).astype(BF)
    own = lax.dynamic_index_in_dim(normed, chip, 0, keepdims=False)
    own = jnp.where(core == 0, own[:, :64], own[:, 64:])
    to_side = [(0, 1), (1, 0)]
    peer_normed = lax.ppermute(own, "role", to_side)
    width = head.shape[1]
    action = lax.dynamic_index_in_dim(actions, step, 0, keepdims=True)
    local = call(
        head_kernel,
        jax.ShapeDtypeStruct((3, 8), F32),
        [VMEM] * 3,
        24,
        2 * 8 * D * width,
        normed,
        head.T,
        action - place * width,
    )
    far = swap(local)
    both = jnp.maximum(local[0], far[0])
    sums = local[1] * jnp.exp(local[0] - both) + far[1] * jnp.exp(far[0] - both)
    packed = jnp.concatenate([both, sums, local[2] + far[2], jnp.zeros_like(sums)])
    heard = to_every(packed[None], ("role",) + CHIP, 2 * CHIPS).reshape(2, CHIPS, 4, 8)
    heard = lax.dynamic_index_in_dim(heard, 1 - side, 0, keepdims=False)
    largest = jnp.max(heard[:, 0], 0)
    sums = jnp.sum(heard[:, 1] * jnp.exp(heard[:, 0] - largest), 0)
    prob = jnp.sum(heard[:, 2], 0) - largest - jnp.log(sums)
    return prob[None], peer_normed[None]


def solution(mesh):
    split = Mesh(
        mesh.devices.reshape(mesh.shape["role"], mesh.shape["grp"], 4, 8, 2),
        ("role", "grp", "tp_0", "tp_1", "tp_2"),
    )
    return jax.shard_map(
        on_device,
        mesh=split,
        in_specs=(
            P(None, None, GRP_TP),
            P(),
            P(),
            P(None, GRP_TP, None),
            P(None, GRP_TP, None),
            P(),
            P("role", GRP_TP, None),
            P("role", GRP_TP),
            P(None, GRP_TP),
            P(None, None, GRP_TP),
            P(),
        ),
        out_specs=(P("role", None), P("role", None, GRP_TP)),
        check_vma=False,
    )
```

time: 121 us -> 119 us (0.983)
  blocking collectives: 15 us -> 0 us
  waiting for transfers between devices: 43.6 us -> 50.7 us
  matrix products: 8.02 us -> 2.47 us
  Pallas kernels: 0 us -> 5.43 us
  starting transfers between devices: 38.7 us -> 44.1 us
  local copies, waits for them, and re-layouts: 8.33 us -> 11.3 us
  other arithmetic: 5.73 us -> 3.62 us
    all_to_all x1 -> x0, blocking collectives: 15 us -> none  [exchange(): return lax.all_to_all(x, axes, split_axis=0, concat_axis=0, tiled=True)]
    dot_general x3 -> x0, matrix products: 7.39 us -> none  [the longest x1 5.72 us: on_device(): jnp.dot(normed.transpose(1, 0, 2).reshape(8, D), head, preferred_element_...]
    all_to_all x4 -> x5, waiting for transfers between devices: 40.4 us -> 46.5 us  [exchange(): return lax.all_to_all(x, axes, split_axis=0, concat_axis=0, tiled=True)]
    all_to_all x4 -> x5, starting transfers between devices: 28 us -> 33.4 us  [exchange(): return lax.all_to_all(x, axes, split_axis=0, concat_axis=0, tiled=True)]
    pallas_call x0 -> x3, Pallas kernels: none -> 5.43 us  [call(): pl.pallas_call(kernel, out_shape=shapes, in_specs=specs, out_specs=jax.tr...]
    unnamed x5 -> x7, local copies, waits for them, and re-layouts: 0.59 us -> 6 us
    reduce_sum x7 -> x1, other arithmetic: 2.43 us -> 0.08 us  [on_device(): gains = got[:, HALF:, 64:].astype(F32).reshape(CHIPS, 2, HEAD_SIZE).sum(1)]
    dynamic_slice x3 -> x1, local copies, waits for them, and re-layouts: 2.87 us -> 0.73 us  [rows_of(): return lax.dynamic_slice_in_dim(x, start, HALF, axis)]
  transfers between devices with their start and end apart: 12 -> 14, of which waited for: 7 -> 9; matrix products, arithmetic and copies ran while one was open for 10% -> 6% of each run, Pallas kernels for 0% -> 3%
where the time goes in v2:
time: 119 us; the launch traced here: 118 us
  waiting for transfers between devices  50.7 us (43%)
  starting transfers between devices  44.1 us (37%)
  local copies, waits for them, and re-layouts  11.3 us (9%)
  Pallas kernels  5.43 us (5%)
  other arithmetic  3.62 us (3%)
  matrix products  2.47 us (2%)
    all_to_all x5, waiting for transfers between devices, exchange(): return lax.all_to_all(x, axes, split_axis=0, concat_axis=0, tiled=True)  46.5 us
    all_to_all x5, starting transfers between devices, exchange(): return lax.all_to_all(x, axes, split_axis=0, concat_axis=0, tiled=True)  33.4 us
    ppermute x8, starting transfers between devices, swap(): return lax.ppermute(x, CORE, [(0, 1), (1, 0)])  9.77 us
    unnamed x7, local copies, waits for them, and re-layouts  6 us
    pallas_call x3, Pallas kernels, call(): pl.pallas_call(kernel, out_shape=shapes, in_specs=specs, out_specs=jax.tr...  5.43 us
  transfers between devices with their start and end apart: 14, of which 9 were waited for; matrix products, arithmetic and copies ran while one was open for 6% of the time, Pallas kernels for 3%

profile of v2, /device:TPU:1, one launch (start us, length us, event | category | flops | bytes accessed | tf_op | source)
XLA Modules:
  0.0 118.4 jit_solution(14310006702936318173)
XLA Ops:
  0.6 3.3 %collective-permute-start = (bf16[2,8,64]{2,1,0:T(8,128)(2,1)}, bf16[2,8,64]{2,1,0:T(8,128)(2,1)S(1)}, u32[]{:S(2)}, u32[]{:S(2)}) collective-permute-start(bf16[2,8,64]{2,1,0:T(8,128)(2,1)} %param.11), channel_id=1, source_target_pairs={{0,1},{1,0},{2,3},{3,2},{4,5},{5,4},{6,7},{7,6},{8,9},{9,8},{10,11... | collective-permute-start | bytes 6152 | tf_op jit(solution)/shard_map/ppermute | solution.py:26
  4.0 0.7 fusion.9
  4.6 0.8 constant_dynamic-slice_fusion.5
  5.6 0.6 broadcast_in_dim.14
  6.2 12.6 %all-to-all-start = ((bf16[64,4,128]{2,1,0:T(4,128)(2,1)}), bf16[64,4,128]{2,1,0:T(4,128)(2,1)S(1)}, u32[]{:S(2)}, u32[]{:S(2)}) async-start(bf16[64,4,128]{2,1,0:T(4,128)(2,1)} %broadcast_in_dim.14), calls=%async_computation | async-start | bytes 131072 | tf_op jit(solution)/shard_map/all_to_all | solution.py:30
  19.4 0.7 dynamic_slice.40
  20.8 1.0 collective-permute-done.3
  21.8 0.8 broadcast_select_fusion
  22.7 7.1 %all-to-all-done = bf16[64,4,128]{2,1,0:T(4,128)(2,1)S(1)} async-done(((bf16[64,4,128]{2,1,0:T(4,128)(2,1)}), bf16[64,4,128]{2,1,0:T(4,128)(2,1)S(1)}, u32[]{:S(2)}, u32[]{:S(2)}) %all-to-all-start) | async-done | bytes 65568 | tf_op jit(solution)/shard_map/all_to_all | solution.py:30
  29.9 1.0 copy-done.1
  30.9 1.0 copy-done.2
  31.9 2.7 %shard_map.122 = bf16[64,8,128]{2,1,0:T(8,128)(2,1)} custom-call(s32[1]{0:T(128)} %bitcast.1.core_ref, bf16[256,128]{1,0:T(8,128)(2,1)S(1)} %bitcast.67, bf16[8,32,1024]{2,1,0:T(8,128)(2,1)S(1)} %copy-done.1, bf16[8,32,1024]{2,1,0:T(8,128)(2,1)S(1)} %collective-permute-done.1.kf_ref, bf16[8,32,1024]{2,1,0:T(8,128)(2,1)S(1)} %copy-done.2, ...), custom_call_target="tpu_custom_call" | custom-call | flops 33554432 | bytes 2097152 | tf_op jit(solution)/shard_map/pallas_call | solution.py:53
  34.6 5.4 %all-to-all-start.1 = ((bf16[64,8,128]{2,1,0:T(8,128)(2,1)}), bf16[64,8,128]{2,1,0:T(8,128)(2,1)S(1)}, u32[]{:S(2)}, u32[]{:S(2)}) async-start(bf16[64,8,128]{2,1,0:T(8,128)(2,1)} %shard_map.122), calls=%async_computation.1 | async-start | bytes 262144 | tf_op jit(solution)/shard_map/all_to_all | solution.py:30
  40.1 0.7 collective-permute-start.5
  40.8 11.0 %all-to-all-done.1.got_ref = bf16[64,8,128]{2,1,0:T(8,128)(2,1)S(1)} async-done(((bf16[64,8,128]{2,1,0:T(8,128)(2,1)}), bf16[64,8,128]{2,1,0:T(8,128)(2,1)S(1)}, u32[]{:S(2)}, u32[]{:S(2)}) %all-to-all-start.1) | async-done | bytes 131104 | tf_op jit(solution)/shard_map/all_to_all | solution.py:30
  52.2 1.5 %fusion.14 = f32[4,8192]{1,0:T(4,128)S(1)} fusion(bf16[64,8192]{1,0:T(8,128)(2,1)} %bitcast.69, pred[]{:T(512)S(6)} %eq.2, bf16[8,128]{1,0:T(8,128)(2,1)S(1)} %shard_map.123), kind=kOutput, calls=%fused_computation.44 | convolution fusion | flops 4194560 | bytes 1181697 | tf_op jit(solution)/shard_map/dot_general | solution.py:219
  53.7 0.9 fusion.1
  54.6 4.7 %all-to-all-start.2 = ((bf16[64,4,128]{2,1,0:T(4,128)(2,1)}), bf16[64,4,128]{2,1,0:T(4,128)(2,1)S(1)}, u32[]{:S(2)}, u32[]{:S(2)}) async-start(bf16[64,4,128]{2,1,0:T(4,128)(2,1)} %fusion.1), calls=%async_computation.2 | async-start | bytes 131072 | tf_op jit(solution)/shard_map/all_to_all | solution.py:30
  59.3 0.7 fusion.11
  60.1 10.4 %all-to-all-done.2 = bf16[64,4,128]{2,1,0:T(4,128)(2,1)S(1)} async-done(((bf16[64,4,128]{2,1,0:T(4,128)(2,1)}), bf16[64,4,128]{2,1,0:T(4,128)(2,1)S(1)}, u32[]{:S(2)}, u32[]{:S(2)}) %all-to-all-start.2) | async-done | bytes 65568 | tf_op jit(solution)/shard_map/all_to_all | solution.py:30
  71.2 4.6 %all-to-all-start.3 = ((bf16[64,4,128]{2,1,0:T(4,128)(2,1)}), bf16[64,4,128]{2,1,0:T(4,128)(2,1)S(1)}, u32[]{:S(2)}, u32[]{:S(2)}) async-start(bf16[64,4,128]{2,1,0:T(4,128)(2,1)} %broadcast_in_dim.15), calls=%async_computation.3 | async-start | bytes 131072 | tf_op jit(solution)/shard_map/all_to_all | solution.py:30
  75.8 0.7 fusion.22.action_ref
  76.5 10.3 %all-to-all-done.3 = bf16[64,4,128]{2,1,0:T(4,128)(2,1)S(1)} async-done(((bf16[64,4,128]{2,1,0:T(4,128)(2,1)}), bf16[64,4,128]{2,1,0:T(4,128)(2,1)S(1)}, u32[]{:S(2)}, u32[]{:S(2)}) %all-to-all-start.3) | async-done | bytes 65568 | tf_op jit(solution)/shard_map/all_to_all | solution.py:30
  86.8 4.0 %collective-permute-start.6 = (bf16[64,4,128]{2,1,0:T(4,128)(2,1)S(1)}, bf16[64,4,128]{2,1,0:T(4,128)(2,1)S(1)}, u32[]{:S(2)}, u32[]{:S(2)}) collective-permute-start(bf16[64,4,128]{2,1,0:T(4,128)(2,1)S(1)} %all-to-all-done.3), channel_id=1, source_target_pairs={{0,1},{1,0},{2,3},{3,2},{4,5},{5,4},{6,7},{7,6},{8,9},{9,8},{10,11... | collective-permute-start | bytes 196616 | tf_op jit(solution)/shard_map/ppermute | solution.py:26
  92.1 3.3 %copy-done = bf16[8192,501]{0,1:T(8,128)(2,1)S(1)} copy-done((bf16[8192,501]{0,1:T(8,128)(2,1)S(1)}, bf16[8192,501]{0,1:T(8,128)(2,1)}, u32[]{:S(2)}) %copy-start) | copy-done | bytes 8208408
  95.5 2.4 %shard_map.124 = f32[3,8]{1,0:T(4,128)S(1)} custom-call(bf16[64,8,128]{2,1,0:T(8,128)(2,1)S(1)} %fusion.4.u_ref, bf16[501,8192]{1,0:T(8,128)(2,1)S(1)} %bitcast.66, s32[1,8]{1,0:T(1,128)S(1)} %fusion.22.action_ref), custom_call_target="tpu_custom_call" | custom-call | flops 65667072 | bytes 4104192 | tf_op jit(solution)/shard_map/pallas_call | solution.py:53
  98.5 0.8 collective-permute-done.7
  99.4 0.7 broadcast_in_dim.16
  100.0 6.1 %all-to-all-start.4 = ((f32[128,1,32]{2,1,0:T(1,128)}), f32[128,1,32]{2,1,0:T(1,128)S(1)}, u32[]{:S(2)}, u32[]{:S(2)}) async-start(f32[128,1,32]{2,1,0:T(1,128)} %broadcast_in_dim.16), calls=%async_computation.4 | async-start | bytes 131072 | tf_op jit(solution)/shard_map/all_to_all | solution.py:30
  106.3 0.9 collective-permute-start.8
  107.2 1.8 %collective-permute-done.8 = bf16[8,64]{1,0:T(8,128)(2,1)S(1)} collective-permute-done((bf16[8,64]{1,0:T(8,128)(2,1)S(1)}, bf16[8,64]{1,0:T(8,128)(2,1)S(1)}, u32[]{:S(2)}, u32[]{:S(2)}) %collective-permute-start.8) | collective-permute-done | bytes 1056 | tf_op jit(solution)/shard_map/ppermute | solution.py:233
  109.0 7.7 %all-to-all-done.4 = f32[128,1,32]{2,1,0:T(1,128)S(1)} async-done(((f32[128,1,32]{2,1,0:T(1,128)}), f32[128,1,32]{2,1,0:T(1,128)S(1)}, u32[]{:S(2)}, u32[]{:S(2)}) %all-to-all-start.4) | async-done | bytes 16416 | tf_op jit(solution)/shard_map/all_to_all | solution.py:30
  (51 shorter events, 6.5 us)
Async XLA Ops:
  0.6 4.9 %collective-permute-start = (bf16[2,8,64]{2,1,0:T(8,128)(2,1)}, bf16[2,8,64]{2,1,0:T(8,128)(2,1)S(1)}, u32[]{:S(2)}, u32[]{:S(2)}) collective-permute-start(bf16[2,8,64]{2,1,0:T(8,128)(2,1)} %param.11), channel_id=1, source_target_pairs={{0,1},{1,0},{2,3},{3,2},{4,5},{5,4},{6,7},{7,6},{8,9},{9,8},{10,11... | collective-permute-start | bytes 6152 | tf_op jit(solution)/shard_map/ppermute | solution.py:26
  6.2 23.6 %all-to-all-start = ((bf16[64,4,128]{2,1,0:T(4,128)(2,1)}), bf16[64,4,128]{2,1,0:T(4,128)(2,1)S(1)}, u32[]{:S(2)}, u32[]{:S(2)}) async-start(bf16[64,4,128]{2,1,0:T(4,128)(2,1)} %broadcast_in_dim.14), calls=%async_computation | async-start | bytes 131072 | tf_op jit(solution)/shard_map/all_to_all | solution.py:30
  18.8 11.1 %collective-permute-start.1 = (bf16[8,32,1024]{2,1,0:T(8,128)(2,1)}, bf16[8,32,1024]{2,1,0:T(8,128)(2,1)S(1)}, u32[]{:S(2)}, u32[]{:S(2)}) collective-permute-start(bf16[8,32,1024]{2,1,0:T(8,128)(2,1)} %k_ref), channel_id=1, source_target_pairs={{0,1},{1,0},{2,3},{3,2},{4,5},{5,4},{6,7},{7,6},{8,9},{9,8},{10,11... | collective-permute-start | bytes 1572872 | tf_op jit(solution)/shard_map/ppermute | solution.py:26
  19.2 10.6 %collective-permute-start.2 = (bf16[8,32,1024]{2,1,0:T(8,128)(2,1)}, bf16[8,32,1024]{2,1,0:T(8,128)(2,1)S(1)}, u32[]{:S(2)}, u32[]{:S(2)}) collective-permute-start(bf16[8,32,1024]{2,1,0:T(8,128)(2,1)} %v_ref), channel_id=1, source_target_pairs={{0,1},{1,0},{2,3},{3,2},{4,5},{5,4},{6,7},{7,6},{8,9},{9,8},{10,11... | collective-permute-start | bytes 1572872 | tf_op jit(solution)/shard_map/ppermute | solution.py:26
  20.1 1.6 %collective-permute-start.3 = (f32[64]{0:T(128)}, f32[64]{0:T(128)S(1)}, u32[]{:S(2)}, u32[]{:S(2)}) collective-permute-start(f32[64]{0:T(128)} %bitcast.73), channel_id=1, source_target_pairs={{0,1},{1,0},{2,3},{3,2},{4,5},{5,4},{6,7},{7,6},{8,9},{9,8},{10,11... | collective-permute-start | bytes 776 | tf_op jit(solution)/shard_map/ppermute | solution.py:26
  20.6 33.1 %collective-permute-start.4 = (bf16[64,8192]{1,0:T(8,128)(2,1)}, bf16[64,8192]{1,0:T(8,128)(2,1)S(1)}, u32[]{:S(2)}, u32[]{:S(2)}) collective-permute-start(bf16[64,8192]{1,0:T(8,128)(2,1)} %bitcast.68), channel_id=1, source_target_pairs={{0,1},{1,0},{2,3},{3,2},{4,5},{5,4},{6,7},{7,6},{8,9},{9,8},{10,11... | collective-permute-start | bytes 3145736 | tf_op jit(solution)/shard_map/ppermute | solution.py:26
  29.9 1.0 copy-start.1
  30.9 1.0 copy-start.2
  34.6 17.2 %all-to-all-start.1 = ((bf16[64,8,128]{2,1,0:T(8,128)(2,1)}), bf16[64,8,128]{2,1,0:T(8,128)(2,1)S(1)}, u32[]{:S(2)}, u32[]{:S(2)}) async-start(bf16[64,8,128]{2,1,0:T(8,128)(2,1)} %shard_map.122), calls=%async_computation.1 | async-start | bytes 262144 | tf_op jit(solution)/shard_map/all_to_all | solution.py:30
  40.1 20.0 %collective-permute-start.5 = (bf16[2,8,64]{2,1,0:T(8,128)(2,1)}, bf16[2,8,64]{2,1,0:T(8,128)(2,1)S(1)}, u32[]{:S(2)}, u32[]{:S(2)}) collective-permute-start(bf16[2,8,64]{2,1,0:T(8,128)(2,1)} %param.20), channel_id=1, source_target_pairs={{0,1},{1,0},{2,3},{3,2},{4,5},{5,4},{6,7},{7,6},{8,9},{9,8},{10,11... | collective-permute-start | bytes 6152 | tf_op jit(solution)/shard_map/ppermute | solution.py:26
  54.6 15.8 %all-to-all-start.2 = ((bf16[64,4,128]{2,1,0:T(4,128)(2,1)}), bf16[64,4,128]{2,1,0:T(4,128)(2,1)S(1)}, u32[]{:S(2)}, u32[]{:S(2)}) async-start(bf16[64,4,128]{2,1,0:T(4,128)(2,1)} %fusion.1), calls=%async_computation.2 | async-start | bytes 131072 | tf_op jit(solution)/shard_map/all_to_all | solution.py:30
  71.2 15.6 %all-to-all-start.3 = ((bf16[64,4,128]{2,1,0:T(4,128)(2,1)}), bf16[64,4,128]{2,1,0:T(4,128)(2,1)S(1)}, u32[]{:S(2)}, u32[]{:S(2)}) async-start(bf16[64,4,128]{2,1,0:T(4,128)(2,1)} %broadcast_in_dim.15), calls=%async_computation.3 | async-start | bytes 131072 | tf_op jit(solution)/shard_map/all_to_all | solution.py:30
  86.8 4.9 %collective-permute-start.6 = (bf16[64,4,128]{2,1,0:T(4,128)(2,1)S(1)}, bf16[64,4,128]{2,1,0:T(4,128)(2,1)S(1)}, u32[]{:S(2)}, u32[]{:S(2)}) collective-permute-start(bf16[64,4,128]{2,1,0:T(4,128)(2,1)S(1)} %all-to-all-done.3), channel_id=1, source_target_pairs={{0,1},{1,0},{2,3},{3,2},{4,5},{5,4},{6,7},{7,6},{8,9},{9,8},{10,11... | collective-permute-start | bytes 196616 | tf_op jit(solution)/shard_map/ppermute | solution.py:26
  92.1 3.3 %copy-start = (bf16[8192,501]{0,1:T(8,128)(2,1)S(1)}, bf16[8192,501]{0,1:T(8,128)(2,1)}, u32[]{:S(2)}) copy-start(bf16[8192,501]{0,1:T(8,128)(2,1)} %param.19) | copy-start | bytes 24625156
  97.8 1.4 %collective-permute-start.7 = (f32[3,8]{1,0:T(4,128)S(1)}, f32[3,8]{1,0:T(4,128)S(1)}, u32[]{:S(2)}, u32[]{:S(2)}) collective-permute-start(f32[3,8]{1,0:T(4,128)S(1)} %shard_map.124), channel_id=1, source_target_pairs={{0,1},{1,0},{2,3},{3,2},{4,5},{5,4},{6,7},{7,6},{8,9},{9,8},{10,11... | collective-permute-start | bytes 296 | tf_op jit(solution)/shard_map/ppermute | solution.py:26
  100.0 16.7 %all-to-all-start.4 = ((f32[128,1,32]{2,1,0:T(1,128)}), f32[128,1,32]{2,1,0:T(1,128)S(1)}, u32[]{:S(2)}, u32[]{:S(2)}) async-start(f32[128,1,32]{2,1,0:T(1,128)} %broadcast_in_dim.16), calls=%async_computation.4 | async-start | bytes 131072 | tf_op jit(solution)/shard_map/all_to_all | solution.py:30
  106.3 2.8 %collective-permute-start.8 = (bf16[8,64]{1,0:T(8,128)(2,1)S(1)}, bf16[8,64]{1,0:T(8,128)(2,1)S(1)}, u32[]{:S(2)}, u32[]{:S(2)}) collective-permute-start(bf16[8,64]{1,0:T(8,128)(2,1)S(1)} %slice_select_fusion), channel_id=1, source_target_pairs={{0,128},{128,0},{1,129},{129,1},{2,130},{130,2},{3,131},{131,3},{4... | collective-permute-start | bytes 3080 | tf_op jit(solution)/shard_map/ppermute | solution.py:233

commit v3 on v2

--- a/solution.py
+++ b/solution.py
@@ -15,6 +15,7 @@
 CHIP = ("grp", "tp_0", "tp_1")
 CORE = "tp_2"
 GRP_TP = CHIP + (CORE,)
+WITHIN = (CORE, "tp_0", "tp_1")
 CHIPS = 64
 HALF = 4
 LOW = -(2.0**100)
@@ -62,42 +63,66 @@
     )(*operands)
 
 
-def attend_kernel(core_ref, q_ref, k_ref, kf_ref, v_ref, vf_ref, ok_ref, pack_ref, out_ref):
-    base = core_ref[0] * HALF
-    row = lax.broadcasted_iota(jnp.int32, (32, 256), 0)
-    col = lax.broadcasted_iota(jnp.int32, (32, 256), 1)
-    valid = ((row % HALF) == (col // 64)) & (ok_ref[...] > 0)
-    lane = lax.broadcasted_iota(jnp.int32, (32, 128), 1)
-    upper = lax.broadcasted_iota(jnp.int32, (4, 8, 128), 1) < HALF
-    pack = jnp.concatenate([pack_ref[...]] * 4, 0)
-    for kv in range(KV_HEADS):
+def load_kernel(w_ref, out_ref):
+    out_ref[...] = w_ref[...]
+
+
+def attend_kernel(q_ref, k_ref, v_ref, kf_ref, vf_ref, ok_ref, pack_ref, out_ref):
+    x = q_ref[...].astype(F32)
+    x0, x1 = x[:128], x[128:]
+    left = lax.broadcasted_iota(jnp.int32, (128, 128), 1) < 64
+    halves = (
+        jnp.where(left, x0, pltpu.roll(x1, 64, 1)).astype(BF),
+        jnp.where(left, pltpu.roll(x0, 64, 1), x1).astype(BF),
+    )
+    row = lax.broadcasted_iota(jnp.int32, (128, 256), 0)
+    col = lax.broadcasted_iota(jnp.int32, (128, 256), 1)
+    same = (row % HALF) == (col // 64)
+
+    def both(near, far, half, kv):
         cols = slice(kv * HEAD_SIZE, (kv + 1) * HEAD_SIZE)
-
-        def both(near, far):
-            parts = []
-            for r in range(HALF):
-                parts += [near[base + r, :, cols], far[base + r, :, cols]]
-            return jnp.concatenate(parts, 0)
-
-        q = q_ref[kv * 32 : (kv + 1) * 32, :]
-        s = lax.dot_general(q, both(k_ref, kf_ref), NT, preferred_element_type=F32)
-        s = jnp.where(valid, s * (1.0 / math.sqrt(HEAD_SIZE)), LOW)
-        top = jnp.max(s, 1, keepdims=True).astype(BF).astype(F32)
-        p = jnp.where(valid, jnp.exp(s - top), 0.0)
-        total = jnp.sum(p, 1, keepdims=True)
-        total_hi = total.astype(BF).astype(F32)
-        acc = jnp.dot(p.astype(BF), both(v_ref, vf_ref), preferred_element_type=F32)
-        stats = jnp.where(lane < 32, total_hi, total - total_hi)
-        stats = jnp.where(lane < 16, top, jnp.where(lane < 64, stats, pack))
-        acc, stats = acc.reshape(4, 8, 128), stats.reshape(4, 8, 128)
-        even = jnp.where(upper, acc, pltpu.roll(stats, HALF, 1)).astype(BF)
-        odd = jnp.where(upper, pltpu.roll(acc, HALF, 1), stats).astype(BF)
-        for t in range(4):
-            out_ref[kv * 8 + 2 * t] = even[t]
-            out_ref[kv * 8 + 2 * t + 1] = odd[t]
-
-
-def merge_kernel(step_ref, got_ref, q_ref, fk_ref, fv_ref, out_ref):
+        parts = []
+        for r in range(half * HALF, half * HALF + HALF):
+            parts += [near[r, :, cols], far[r, :, cols]]
+        return jnp.concatenate(parts, 0)
+
+    scores, valid = [], []
+    for half in range(2):
+        for kv in range(4):
+            q = halves[half][kv * 32 : (kv + 1) * 32]
+            scores.append(
+                lax.dot_general(q, both(k_ref, kf_ref, half, kv), NT, preferred_element_type=F32)
+            )
+        valid.append(same & (ok_ref[half : half + 1, :] > 0))
+    valid = jnp.concatenate(valid, 0)
+    s = jnp.concatenate(scores, 0)
+    s = jnp.where(valid, s * (1.0 / math.sqrt(HEAD_SIZE)), LOW)
+    top = jnp.max(s, 1, keepdims=True).astype(BF).astype(F32)
+    p = jnp.where(valid, jnp.exp(s - top), 0.0)
+    total = jnp.sum(p, 1, keepdims=True)
+    p = p.astype(BF)
+    total_hi = total.astype(BF).astype(F32)
+    lane = lax.broadcasted_iota(jnp.int32, (256, 128), 1)
+    stats = jnp.where(lane < 32, total_hi, total - total_hi)
+    stats = jnp.where(lane < 16, top, stats)
+    acc = []
+    for half in range(2):
+        for kv in range(4):
+            n = (half * 4 + kv) * 32
+            acc.append(
+                jnp.dot(p[n : n + 32], both(v_ref, vf_ref, half, kv), preferred_element_type=F32)
+            )
+    acc = jnp.concatenate(acc, 0).reshape(32, 8, 128)
+    stats = jnp.where(lane.reshape(32, 8, 128) < 64, stats.reshape(32, 8, 128), pack_ref[...][None])
+    upper = lax.broadcasted_iota(jnp.int32, (32, 8, 128), 1) < HALF
+    even = jnp.where(upper, acc, pltpu.roll(stats, HALF, 1)).astype(BF)
+    odd = jnp.where(upper, pltpu.roll(acc, HALF, 1), stats).astype(BF)
+    for t in range(32):
+        out_ref[2 * t] = even[t]
+        out_ref[2 * t + 1] = odd[t]
+
+
+def merge_kernel(at_ref, got_ref, q_ref, fk_ref, fv_ref, w_ref, far_ref, out_ref):
     x = got_ref[...].astype(F32)
     stats = pltpu.roll(x, HALF, 1)
     tops = stats[:, :, 0:1]
@@ -106,7 +131,7 @@
     scale = 1.0 / math.sqrt(HEAD_SIZE)
     s0 = jnp.sum(fk_ref[0] * q, 1, keepdims=True) * scale
     s1 = jnp.sum(fk_ref[1] * q, 1, keepdims=True) * scale
-    second = step_ref[0] >= 1
+    second = at_ref[0] >= 1
     s1 = jnp.where(second, s1, LOW)
     peak = jnp.maximum(jnp.max(tops, 0), jnp.maximum(s0, s1))
     factor = jnp.exp(tops - peak[None])
@@ -115,7 +140,15 @@
     below = jnp.sum(totals * factor, 0) + p0 + p1
     above = jnp.sum(x * factor, 0) + p0 * fv_ref[0] + p1 * fv_ref[1]
     row = lax.broadcasted_iota(jnp.int32, (8, 128), 0)
-    out_ref[...] = jnp.where(row < HALF, above / below, 0.0).astype(BF)
+    attended = jnp.where(row < HALF, above / below, 0.0)
+    turned = pltpu.roll(attended, 64, 1)
+    turned = jnp.where(at_ref[1] == 0, attended, turned).astype(BF)
+    wide = 1024
+    for n in range(0, D, wide):
+        w = jnp.concatenate([w_ref[:, n : n + wide], far_ref[:, n : n + wide]], 0)
+        share = jnp.dot(turned, w, preferred_element_type=F32)
+        for i in range(wide // 128):
+            out_ref[n // 128 + i] = share[:HALF, i * 128 : (i + 1) * 128].astype(BF)
 
 
 def head_kernel(u_ref, head_ref, action_ref, out_ref):
@@ -159,67 +192,94 @@
         far = rows_of(lax.dynamic_index_in_dim(far, step, 0, keepdims=False), row0)
         return by_core(core, near, far, 1)
 
+    grp = lax.axis_index("grp")
+    sides = [(0, 1), (1, 0)]
+    away = (1 - grp) * 512
+    keys_out = lax.dynamic_slice_in_dim(stored_key_cache, away, 512, 2)
+    values_out = lax.dynamic_slice_in_dim(stored_value_cache, away, 512, 2)
+    keys_far = lax.ppermute(keys_out, "grp", sides)
+    values_far = lax.ppermute(values_out, "grp", sides)
+    q_now = lax.dynamic_index_in_dim(queries, step, 0, keepdims=False)
+    q_packed = jnp.concatenate([q_now[:HALF], q_now[HALF:]], 1)
+    q_packed, _, _ = lax.optimization_barrier((q_packed, keys_out, values_out))
+    q = to_every(q_packed, WITHIN, CHIPS).reshape(CHIPS * HALF, HEAD_SIZE)
+
+    keys, values, w_side, gain, resid, queries, lengths, head, _ = lax.optimization_barrier(
+        (
+            stored_key_cache,
+            stored_value_cache,
+            wo_sides[0],
+            gain_sides,
+            resid,
+            queries,
+            lengths,
+            head,
+            q_packed,
+        )
+    )
+    keys = lax.dynamic_slice_in_dim(keys, grp * 512, 512, 2)
+    values = lax.dynamic_slice_in_dim(values, grp * 512, 512, 2)
+    w_mine = call(
+        load_kernel,
+        jax.ShapeDtypeStruct(w_side.shape, BF),
+        [VMEM],
+        4,
+        1 << 20,
+        w_side,
+    )
+    w_far = swap(w_side)
+    head_far = swap(head)
+    gain_peer = lax.ppermute(gain, "grp", sides)
     q_chip = chip_rows(queries, swap(queries))
-    q = to_every(q_chip, CHIP, CHIPS).reshape(CHIPS * HALF, HEAD_SIZE)
-
-    keys, values, w_mine, gain, resid, lengths, _ = lax.optimization_barrier(
-        (stored_key_cache, stored_value_cache, wo_sides[0], gain_sides[0], resid, lengths, q_chip)
-    )
-    keys_far, values_far, w_far = swap(keys), swap(values), swap(w_mine)
-    gain_chip = by_core(core, gain, swap(gain), 0)
     r_chip = chip_rows(resid, swap(resid)).astype(F32)
 
-    lens = rows_of(lengths, row0)
     at = jnp.arange(slots, dtype=jnp.int32)
-    position = jnp.concatenate([place * slots + at, (place + 1 - 2 * core) * slots + at])
-    valid = (position[None, :] < lens[:, None]).astype(F32).reshape(1, 4 * 2 * slots)
-    gain_hi = rounded(gain_chip)
-    pack = jnp.concatenate([gain_hi, gain_chip - gain_hi]).reshape(HALF, 64)
+    position = jnp.concatenate([place * slots + at, (place + CHIPS - 2 * CHIPS * grp) * slots + at])
+    valid = (position[None, :] < lengths[:, None]).astype(F32).reshape(2, 4 * 2 * slots)
+    gain_two = jnp.concatenate([gain, gain_peer], 0)
+    gain_hi = rounded(gain_two)
+    pack = jnp.concatenate([gain_hi, gain_two - gain_hi], 0)
     pack = jnp.concatenate([jnp.zeros_like(pack), pack], 1)
     pack = jnp.concatenate([pack, pack], 0)
     sent = call(
         attend_kernel,
         jax.ShapeDtypeStruct((CHIPS, 8, HEAD_SIZE), BF),
-        [SMEM] + [VMEM] * 7,
+        [VMEM] * 7,
         16,
         2 * 2 * 256 * 256 * 128,
-        core[None],
         q,
         keys,
+        values,
         keys_far,
-        values,
         values_far,
         valid,
         pack,
     )
-    got = exchange(sent, CHIP)
-    gains = got[:, HALF:, 64:].astype(F32).reshape(CHIPS, 2, HEAD_SIZE).sum(1)
+    got = exchange(sent, WITHIN)
+    gains = got[:, HALF:, 64:].astype(F32)
+    gains = (gains[:, :2] + gains[:, 2:]).reshape(2, 32, 2, 64)
+    gains = gains.transpose(2, 1, 0, 3).reshape(2, 32, HEAD_SIZE)
+    gains = jnp.where(grp == 0, gains, gains[::-1]).reshape(CHIPS, HEAD_SIZE)
     kv = chip // GROUP
 
     def fresh(x):
         x = lax.dynamic_slice(x, (0, row0, kv * HEAD_SIZE), (2, HALF, HEAD_SIZE))
         return jnp.pad(x.astype(F32), ((0, 0), (0, HALF), (0, 0)))
 
-    attended = call(
+    share = call(
         merge_kernel,
-        jax.ShapeDtypeStruct((8, HEAD_SIZE), BF),
-        [SMEM] + [VMEM] * 4,
-        8,
-        CHIPS * 8 * HEAD_SIZE * 8,
-        step[None],
+        jax.ShapeDtypeStruct((CHIPS, HALF, HEAD_SIZE), BF),
+        [SMEM] + [VMEM] * 6,
+        16,
+        2 * 8 * HEAD_SIZE * D,
+        jnp.stack([step, core]),
         got,
         jnp.pad(q_chip.astype(F32), ((0, HALF), (0, 0))),
         fresh(step_token_keys),
         fresh(step_token_values),
-    )[:HALF]
-
-    a0, a1 = attended[:, :64], attended[:, 64:]
-    a_mine = jnp.where(core == 0, a0, a1)
-    a_far = jnp.where(core == 0, a1, a0)
-    share = jnp.dot(a_mine, w_mine, preferred_element_type=F32) + jnp.dot(
-        a_far, w_far, preferred_element_type=F32
-    )
-    share = share.astype(BF).reshape(HALF, CHIPS, HEAD_SIZE).transpose(1, 0, 2)
+        w_mine,
+        w_far,
+    )
     state = jnp.sum(exchange(share, CHIP).astype(F32), 0) + r_chip
 
     mine = to_every(state.astype(BF), CHIP, CHIPS)
@@ -240,8 +300,8 @@
         24,
         2 * 8 * D * width,
         normed,
-        head.T,
-        action - place * width,
+        head_far.T,
+        action - (place + 1 - 2 * core) * width,
     )
     far = swap(local)
     both = jnp.maximum(local[0], far[0])

time: 119 us -> 121 us (1.017)
  starting transfers between devices: 44.1 us -> 49.9 us
  waiting for transfers between devices: 50.7 us -> 45.4 us
  Pallas kernels: 5.43 us -> 8.96 us
  matrix products: 2.47 us -> 0 us
    all_to_all x5, waiting for transfers between devices: 46.5 us -> 41.4 us  [exchange(): return lax.all_to_all(x, axes, split_axis=0, concat_axis=0, tiled=True)]
    dynamic_slice x0 -> x4, local copies, waits for them, and re-layouts: none -> 4.43 us  [the longest x1 1.7 us: on_device(): keys_out = lax.dynamic_slice_in_dim(stored_key_cache, away, 512, 2)]
    unnamed x7 -> x3, local copies, waits for them, and re-layouts: 6 us -> 1.8 us
    ppermute x0 -> x3, starting transfers between devices: none -> 4 us  [the longest x1 1.96 us: on_device(): values_far = lax.ppermute(values_out, 'grp', sides)]
    pallas_call x3 -> x4, Pallas kernels: 5.43 us -> 8.96 us  [call(): pl.pallas_call(kernel, out_shape=shapes, in_specs=specs, out_specs=jax.tr...]
    all_to_all x5, starting transfers between devices: 33.4 us -> 36.8 us  [exchange(): return lax.all_to_all(x, axes, split_axis=0, concat_axis=0, tiled=True)]
    dot_general x2 -> x0, matrix products: 2.47 us -> none  [the longest x1 1.53 us: on_device(): jnp.dot(a_mine, w_mine, preferred_element_type=F32)]
    ppermute x8 -> x6, starting transfers between devices: 9.77 us -> 8.1 us  [swap(): return lax.ppermute(x, CORE, [(0, 1), (1, 0)])]
  transfers between devices with their start and end apart: 14 -> 15, of which waited for: 9 -> 9; matrix products, arithmetic and copies ran while one was open for 6% -> 7% of each run, Pallas kernels for 3% -> 3%
where the time goes in v3:
time: 121 us; the launch traced here: 120 us
  starting transfers between devices  49.9 us (41%)
  waiting for transfers between devices  45.4 us (38%)
  local copies, waits for them, and re-layouts  11.7 us (10%)
  Pallas kernels  8.96 us (7%)
  other arithmetic  3.52 us (3%)
    all_to_all x5, waiting for transfers between devices, exchange(): return lax.all_to_all(x, axes, split_axis=0, concat_axis=0, tiled=True)  41.4 us
    all_to_all x5, starting transfers between devices, exchange(): return lax.all_to_all(x, axes, split_axis=0, concat_axis=0, tiled=True)  36.8 us
    pallas_call x4, Pallas kernels, call(): pl.pallas_call(kernel, out_shape=shapes, in_specs=specs, out_specs=jax.tr...  8.96 us
    ppermute x6, starting transfers between devices, swap(): return lax.ppermute(x, CORE, [(0, 1), (1, 0)])  8.1 us
  transfers between devices with their start and end apart: 15, of which 9 were waited for; matrix products, arithmetic and copies ran while one was open for 7% of the time, Pallas kernels for 3%

profile of v3, /device:TPU:1, one launch (start us, length us, event | category | flops | bytes accessed | tf_op | source)
XLA Modules:
  0.0 120.2 jit_solution(5825062388100724016)
XLA Ops:
  0.6 0.7 constant_dynamic-slice_fusion.13
  1.3 1.0 constant_dynamic-slice_fusion.11
  2.3 1.7 %constant_dynamic-slice_fusion.12 = bf16[8,32,512]{2,1,0:T(8,128)(2,1)} fusion(bf16[8,32,1024]{2,1,0:T(8,128)(2,1)} %param.14, s32[]{:T(128)S(6)} %select_n.87), kind=kLoop, calls=%fused_computation.34 | loop fusion | bytes 524292 | tf_op jit(solution)/shard_map/dynamic_slice | solution.py:198
  4.1 3.3 %collective-permute-start.7 = (bf16[8192,501]{0,1:T(8,128)(2,1)}, bf16[8192,501]{0,1:T(8,128)(2,1)}, u32[]{:S(2)}, u32[]{:S(2)}) collective-permute-start(bf16[8192,501]{0,1:T(8,128)(2,1)} %param.19), channel_id=1, source_target_pairs={{0,1},{1,0},{2,3},{3,2},{4,5},{5,4},{6,7},{7,6},{8,9},{9,8},{10,11... | collective-permute-start | bytes 24625160 | tf_op jit(solution)/shard_map/ppermute | solution.py:27
  7.3 1.0 collective-permute-start
  8.4 2.0 %collective-permute-start.1 = (bf16[8,32,512]{2,1,0:T(8,128)(2,1)S(1)}, bf16[8,32,512]{2,1,0:T(8,128)(2,1)S(1)}, u32[]{:S(2)}, u32[]{:S(2)}) collective-permute-start(bf16[8,32,512]{2,1,0:T(8,128)(2,1)S(1)} %constant_dynamic-slice_fusion.11), channel_id=1, source_target_pairs={{0,64},{64,0},{1,65},{65,1},{2,66},{66,2},{3,67},{67,3},{4,68},{68... | collective-permute-start | bytes 786440 | tf_op jit(solution)/shard_map/ppermute | solution.py:201
  10.3 1.0 collective-permute-start.2
  12.0 12.7 %all-to-all-start = ((bf16[64,4,128]{2,1,0:T(4,128)(2,1)}), bf16[64,4,128]{2,1,0:T(4,128)(2,1)S(1)}, u32[]{:S(2)}, u32[]{:S(2)}) async-start(bf16[64,4,128]{2,1,0:T(4,128)(2,1)} %broadcast_in_dim.8), calls=%async_computation | async-start | bytes 131072 | tf_op jit(solution)/shard_map/all_to_all | solution.py:31
  25.3 0.7 fusion.7
  26.0 0.7 fusion.9
  26.7 0.8 constant_dynamic-slice_fusion.5
  27.4 1.1 constant_dynamic-slice_fusion.9
  28.5 0.7 fusion.11.action_ref
  29.3 0.7 lt.62
  30.2 1.2 %copy-done = bf16[1,64,8192]{2,1,0:T(8,128)(2,1)S(1)} copy-done((bf16[1,64,8192]{2,1,0:T(8,128)(2,1)S(1)}, bf16[1,64,8192]{2,1,0:T(8,128)(2,1)}, u32[]{:S(2)}) %copy-start) | copy-done | bytes 1048600
  33.2 1.3 %all-to-all-done = bf16[64,4,128]{2,1,0:T(4,128)(2,1)S(1)} async-done(((bf16[64,4,128]{2,1,0:T(4,128)(2,1)}), bf16[64,4,128]{2,1,0:T(4,128)(2,1)S(1)}, u32[]{:S(2)}, u32[]{:S(2)}) %all-to-all-start) | async-done | bytes 65568 | tf_op jit(solution)/shard_map/all_to_all | solution.py:31
  34.5 1.2 %shard_map.122 = bf16[64,8,128]{2,1,0:T(8,128)(2,1)} custom-call(bf16[256,128]{1,0:T(8,128)(2,1)S(1)} %bitcast.70, bf16[8,32,512]{2,1,0:T(8,128)(2,1)S(1)} %get-tuple-element.29.k_ref, bf16[8,32,512]{2,1,0:T(8,128)(2,1)S(1)} %get-tuple-element.28.v_ref, bf16[8,32,512]{2,1,0:T(8,128)(2,1)S(1)} %collective-permute-done.kf_ref, ...), custom_call_target="tpu_custom_call" | custom-call | flops 33554432 | bytes 2097152 | tf_op jit(solution)/shard_map/pallas_call | solution.py:54
  35.7 8.9 %all-to-all-start.1 = ((bf16[64,8,128]{2,1,0:T(8,128)(2,1)}), bf16[64,8,128]{2,1,0:T(8,128)(2,1)S(1)}, u32[]{:S(2)}, u32[]{:S(2)}) async-start(bf16[64,8,128]{2,1,0:T(8,128)(2,1)} %shard_map.122), calls=%async_computation.1 | async-start | bytes 262144 | tf_op jit(solution)/shard_map/all_to_all | solution.py:31
  44.7 10.6 %all-to-all-done.1.got_ref = bf16[64,8,128]{2,1,0:T(8,128)(2,1)S(1)} async-done(((bf16[64,8,128]{2,1,0:T(8,128)(2,1)}), bf16[64,8,128]{2,1,0:T(8,128)(2,1)S(1)}, u32[]{:S(2)}, u32[]{:S(2)}) %all-to-all-start.1) | async-done | bytes 131104 | tf_op jit(solution)/shard_map/all_to_all | solution.py:31
  55.3 2.0 %shard_map.124 = bf16[64,4,128]{2,1,0:T(4,128)(2,1)} custom-call(s32[2]{0:T(128)S(1)} %pad_add_fusion.at_ref, bf16[64,8,128]{2,1,0:T(8,128)(2,1)S(1)} %all-to-all-done.1.got_ref, f32[8,128]{1,0:T(8,128)S(1)} %pad_convert_fusion.2.q_ref, f32[2,8,128]{2,1,0:T(8,128)S(1)} %pad_convert_fusion.1.fk_ref, f32[2,8,128]{2,1,0:T(8,128)S(1)} %pad_convert_fusion.fv_ref, ...), custom_call_target="tpu_custom_call" | custom-call | flops 16777216 | bytes 1048576 | tf_op jit(solution)/shard_map/pallas_call | solution.py:54
  57.3 4.6 %all-to-all-start.2 = ((bf16[64,4,128]{2,1,0:T(4,128)(2,1)}), bf16[64,4,128]{2,1,0:T(4,128)(2,1)S(1)}, u32[]{:S(2)}, u32[]{:S(2)}) async-start(bf16[64,4,128]{2,1,0:T(4,128)(2,1)} %shard_map.124), calls=%async_computation.2 | async-start | bytes 131072 | tf_op jit(solution)/shard_map/all_to_all | solution.py:31
  62.0 10.9 %all-to-all-done.2 = bf16[64,4,128]{2,1,0:T(4,128)(2,1)S(1)} async-done(((bf16[64,4,128]{2,1,0:T(4,128)(2,1)}), bf16[64,4,128]{2,1,0:T(4,128)(2,1)S(1)}, u32[]{:S(2)}, u32[]{:S(2)}) %all-to-all-start.2) | async-done | bytes 65568 | tf_op jit(solution)/shard_map/all_to_all | solution.py:31
  73.7 4.6 %all-to-all-start.3 = ((bf16[64,4,128]{2,1,0:T(4,128)(2,1)}), bf16[64,4,128]{2,1,0:T(4,128)(2,1)S(1)}, u32[]{:S(2)}, u32[]{:S(2)}) async-start(bf16[64,4,128]{2,1,0:T(4,128)(2,1)} %broadcast_in_dim.9), calls=%async_computation.3 | async-start | bytes 131072 | tf_op jit(solution)/shard_map/all_to_all | solution.py:31
  78.5 10.8 %all-to-all-done.3 = bf16[64,4,128]{2,1,0:T(4,128)(2,1)S(1)} async-done(((bf16[64,4,128]{2,1,0:T(4,128)(2,1)}), bf16[64,4,128]{2,1,0:T(4,128)(2,1)S(1)}, u32[]{:S(2)}, u32[]{:S(2)}) %all-to-all-start.3) | async-done | bytes 65568 | tf_op jit(solution)/shard_map/all_to_all | solution.py:31
  89.3 3.5 %collective-permute-start.6 = (bf16[64,4,128]{2,1,0:T(4,128)(2,1)S(1)}, bf16[64,4,128]{2,1,0:T(4,128)(2,1)S(1)}, u32[]{:S(2)}, u32[]{:S(2)}) collective-permute-start(bf16[64,4,128]{2,1,0:T(4,128)(2,1)S(1)} %all-to-all-done.3), channel_id=1, source_target_pairs={{0,1},{1,0},{2,3},{3,2},{4,5},{5,4},{6,7},{7,6},{8,9},{9,8},{10,11... | collective-permute-start | bytes 196616 | tf_op jit(solution)/shard_map/ppermute | solution.py:27
  92.8 0.9 collective-permute-done.6
  94.1 5.7 %shard_map.125 = f32[3,8]{1,0:T(4,128)S(1)} custom-call(bf16[64,8,128]{2,1,0:T(8,128)(2,1)S(1)} %fusion.2.u_ref, bf16[501,8192]{1,0:T(8,128)(2,1)} %bitcast.13.head_ref, s32[1,8]{1,0:T(1,128)S(1)} %fusion.11.action_ref), custom_call_target="tpu_custom_call" | custom-call | flops 65667072 | bytes 4104192 | tf_op jit(solution)/shard_map/pallas_call | solution.py:54
  100.3 0.8 collective-permute-done.8
  101.9 6.1 %all-to-all-start.4 = ((f32[128,1,32]{2,1,0:T(1,128)}), f32[128,1,32]{2,1,0:T(1,128)S(1)}, u32[]{:S(2)}, u32[]{:S(2)}) async-start(f32[128,1,32]{2,1,0:T(1,128)} %broadcast_in_dim.10), calls=%async_computation.4 | async-start | bytes 131072 | tf_op jit(solution)/shard_map/all_to_all | solution.py:31
  108.1 0.9 collective-permute-start.9
  109.0 1.8 %collective-permute-done.9 = bf16[8,64]{1,0:T(8,128)(2,1)S(1)} collective-permute-done((bf16[8,64]{1,0:T(8,128)(2,1)S(1)}, bf16[8,64]{1,0:T(8,128)(2,1)S(1)}, u32[]{:S(2)}, u32[]{:S(2)}) %collective-permute-start.9) | collective-permute-done | bytes 1056 | tf_op jit(solution)/shard_map/ppermute | solution.py:293
  110.8 7.7 %all-to-all-done.4 = f32[128,1,32]{2,1,0:T(1,128)S(1)} async-done(((f32[128,1,32]{2,1,0:T(1,128)}), f32[128,1,32]{2,1,0:T(1,128)S(1)}, u32[]{:S(2)}, u32[]{:S(2)}) %all-to-all-start.4) | async-done | bytes 16416 | tf_op jit(solution)/shard_map/all_to_all | solution.py:31
  (58 shorter events, 7.8 us)
Async XLA Ops:
  4.1 90.1 %collective-permute-start.7 = (bf16[8192,501]{0,1:T(8,128)(2,1)}, bf16[8192,501]{0,1:T(8,128)(2,1)}, u32[]{:S(2)}, u32[]{:S(2)}) collective-permute-start(bf16[8192,501]{0,1:T(8,128)(2,1)} %param.19), channel_id=1, source_target_pairs={{0,1},{1,0},{2,3},{3,2},{4,5},{5,4},{6,7},{7,6},{8,9},{9,8},{10,11... | collective-permute-start | bytes 24625160 | tf_op jit(solution)/shard_map/ppermute | solution.py:27
  7.3 27.1 %collective-permute-start = (bf16[8,32,512]{2,1,0:T(8,128)(2,1)}, bf16[8,32,512]{2,1,0:T(8,128)(2,1)S(1)}, u32[]{:S(2)}, u32[]{:S(2)}) collective-permute-start(bf16[8,32,512]{2,1,0:T(8,128)(2,1)} %constant_dynamic-slice_fusion.12), channel_id=1, source_target_pairs={{0,64},{64,0},{1,65},{65,1},{2,66},{66,2},{3,67},{67,3},{4,68},{68... | collective-permute-start | bytes 786440 | tf_op jit(solution)/shard_map/ppermute | solution.py:200
  8.4 26.1 %collective-permute-start.1 = (bf16[8,32,512]{2,1,0:T(8,128)(2,1)S(1)}, bf16[8,32,512]{2,1,0:T(8,128)(2,1)S(1)}, u32[]{:S(2)}, u32[]{:S(2)}) collective-permute-start(bf16[8,32,512]{2,1,0:T(8,128)(2,1)S(1)} %constant_dynamic-slice_fusion.11), channel_id=1, source_target_pairs={{0,64},{64,0},{1,65},{65,1},{2,66},{66,2},{3,67},{67,3},{4,68},{68... | collective-permute-start | bytes 786440 | tf_op jit(solution)/shard_map/ppermute | solution.py:201
  10.3 21.2 %collective-permute-start.2 = (f32[1,64]{1,0:T(1,128)}, f32[1,64]{1,0:T(1,128)S(1)}, u32[]{:S(2)}, u32[]{:S(2)}) collective-permute-start(f32[1,64]{1,0:T(1,128)} %param.18), channel_id=1, source_target_pairs={{0,64},{64,0},{1,65},{65,1},{2,66},{66,2},{3,67},{67,3},{4,68},{68... | collective-permute-start | bytes 776 | tf_op jit(solution)/shard_map/ppermute | solution.py:232
  12.0 22.5 %all-to-all-start = ((bf16[64,4,128]{2,1,0:T(4,128)(2,1)}), bf16[64,4,128]{2,1,0:T(4,128)(2,1)S(1)}, u32[]{:S(2)}, u32[]{:S(2)}) async-start(bf16[64,4,128]{2,1,0:T(4,128)(2,1)} %broadcast_in_dim.8), calls=%async_computation | async-start | bytes 131072 | tf_op jit(solution)/shard_map/all_to_all | solution.py:31
  24.7 30.6 %collective-permute-start.4 = (bf16[64,8192]{1,0:T(8,128)(2,1)}, bf16[64,8192]{1,0:T(8,128)(2,1)S(1)}, u32[]{:S(2)}, u32[]{:S(2)}) collective-permute-start(bf16[64,8192]{1,0:T(8,128)(2,1)} %bitcast.68), channel_id=1, source_target_pairs={{0,1},{1,0},{2,3},{3,2},{4,5},{5,4},{6,7},{7,6},{8,9},{9,8},{10,11... | collective-permute-start | bytes 3145736 | tf_op jit(solution)/shard_map/ppermute | solution.py:27
  30.2 1.2 %copy-start = (bf16[1,64,8192]{2,1,0:T(8,128)(2,1)S(1)}, bf16[1,64,8192]{2,1,0:T(8,128)(2,1)}, u32[]{:S(2)}) copy-start(bf16[1,64,8192]{2,1,0:T(8,128)(2,1)} %param.17) | copy-start | bytes 3145732
  31.5 1.5 %collective-permute-start.3 = (bf16[2,8,64]{2,1,0:T(8,128)(2,1)}, bf16[2,8,64]{2,1,0:T(8,128)(2,1)S(1)}, u32[]{:S(2)}, u32[]{:S(2)}) collective-permute-start(bf16[2,8,64]{2,1,0:T(8,128)(2,1)} %param.11), channel_id=1, source_target_pairs={{0,1},{1,0},{2,3},{3,2},{4,5},{5,4},{6,7},{7,6},{8,9},{9,8},{10,11... | collective-permute-start | bytes 6152 | tf_op jit(solution)/shard_map/ppermute | solution.py:27
  33.0 11.7 %collective-permute-start.5 = (bf16[2,8,64]{2,1,0:T(8,128)(2,1)}, bf16[2,8,64]{2,1,0:T(8,128)(2,1)S(1)}, u32[]{:S(2)}, u32[]{:S(2)}) collective-permute-start(bf16[2,8,64]{2,1,0:T(8,128)(2,1)} %param.20), channel_id=1, source_target_pairs={{0,1},{1,0},{2,3},{3,2},{4,5},{5,4},{6,7},{7,6},{8,9},{9,8},{10,11... | collective-permute-start | bytes 6152 | tf_op jit(solution)/shard_map/ppermute | solution.py:27
  35.7 19.6 %all-to-all-start.1 = ((bf16[64,8,128]{2,1,0:T(8,128)(2,1)}), bf16[64,8,128]{2,1,0:T(8,128)(2,1)S(1)}, u32[]{:S(2)}, u32[]{:S(2)}) async-start(bf16[64,8,128]{2,1,0:T(8,128)(2,1)} %shard_map.122), calls=%async_computation.1 | async-start | bytes 262144 | tf_op jit(solution)/shard_map/all_to_all | solution.py:31
  57.3 15.6 %all-to-all-start.2 = ((bf16[64,4,128]{2,1,0:T(4,128)(2,1)}), bf16[64,4,128]{2,1,0:T(4,128)(2,1)S(1)}, u32[]{:S(2)}, u32[]{:S(2)}) async-start(bf16[64,4,128]{2,1,0:T(4,128)(2,1)} %shard_map.124), calls=%async_computation.2 | async-start | bytes 131072 | tf_op jit(solution)/shard_map/all_to_all | solution.py:31
  73.7 15.6 %all-to-all-start.3 = ((bf16[64,4,128]{2,1,0:T(4,128)(2,1)}), bf16[64,4,128]{2,1,0:T(4,128)(2,1)S(1)}, u32[]{:S(2)}, u32[]{:S(2)}) async-start(bf16[64,4,128]{2,1,0:T(4,128)(2,1)} %broadcast_in_dim.9), calls=%async_computation.3 | async-start | bytes 131072 | tf_op jit(solution)/shard_map/all_to_all | solution.py:31
  89.3 4.5 %collective-permute-start.6 = (bf16[64,4,128]{2,1,0:T(4,128)(2,1)S(1)}, bf16[64,4,128]{2,1,0:T(4,128)(2,1)S(1)}, u32[]{:S(2)}, u32[]{:S(2)}) collective-permute-start(bf16[64,4,128]{2,1,0:T(4,128)(2,1)S(1)} %all-to-all-done.3), channel_id=1, source_target_pairs={{0,1},{1,0},{2,3},{3,2},{4,5},{5,4},{6,7},{7,6},{8,9},{9,8},{10,11... | collective-permute-start | bytes 196616 | tf_op jit(solution)/shard_map/ppermute | solution.py:27
  99.9 1.3 %collective-permute-start.8 = (f32[3,8]{1,0:T(4,128)S(1)}, f32[3,8]{1,0:T(4,128)S(1)}, u32[]{:S(2)}, u32[]{:S(2)}) collective-permute-start(f32[3,8]{1,0:T(4,128)S(1)} %shard_map.125), channel_id=1, source_target_pairs={{0,1},{1,0},{2,3},{3,2},{4,5},{5,4},{6,7},{7,6},{8,9},{9,8},{10,11... | collective-permute-start | bytes 296 | tf_op jit(solution)/shard_map/ppermute | solution.py:27
  101.9 16.7 %all-to-all-start.4 = ((f32[128,1,32]{2,1,0:T(1,128)}), f32[128,1,32]{2,1,0:T(1,128)S(1)}, u32[]{:S(2)}, u32[]{:S(2)}) async-start(f32[128,1,32]{2,1,0:T(1,128)} %broadcast_in_dim.10), calls=%async_computation.4 | async-start | bytes 131072 | tf_op jit(solution)/shard_map/all_to_all | solution.py:31
  108.1 2.8 %collective-permute-start.9 = (bf16[8,64]{1,0:T(8,128)(2,1)S(1)}, bf16[8,64]{1,0:T(8,128)(2,1)S(1)}, u32[]{:S(2)}, u32[]{:S(2)}) collective-permute-start(bf16[8,64]{1,0:T(8,128)(2,1)S(1)} %slice_select_fusion), channel_id=1, source_target_pairs={{0,128},{128,0},{1,129},{129,1},{2,130},{130,2},{3,131},{131,3},{4... | collective-permute-start | bytes 3080 | tf_op jit(solution)/shard_map/ppermute | solution.py:293

commit v4 on v2

v4 whole, which is shorter than its diff:
```python
import math

import jax
import jax.numpy as jnp
from jax import lax
from jax.experimental import pallas as pl
from jax.experimental.pallas import tpu as pltpu
from jax.sharding import Mesh
from jax.sharding import PartitionSpec as P

D = 8192
KV_HEADS = 8
GROUP = 8
HEAD_SIZE = 128
CHIP = ("grp", "tp_0", "tp_1")
CORE = "tp_2"
GRP_TP = CHIP + (CORE,)
CHIPS = 64
HALF = 4
LOW = -(2.0**100)
BF = jnp.bfloat16
F32 = jnp.float32


def swap(x):
    return lax.ppermute(x, CORE, [(0, 1), (1, 0)])


def exchange(x, axes):
    return lax.all_to_all(x, axes, split_axis=0, concat_axis=0, tiled=True)


def to_every(x, axes, count):
    return exchange(jnp.broadcast_to(x[None], (count, *x.shape)), axes)


def rounded(x):
    return lax.reduce_precision(x, 8, 7)


def by_core(core, mine, other, axis):
    first = jnp.concatenate([mine, other], axis)
    second = jnp.concatenate([other, mine], axis)
    return jnp.where(core == 0, first, second)


NT = (((1,), (1,)), ((), ()))
VMEM = pl.BlockSpec(memory_space=pltpu.VMEM)
SMEM = pl.BlockSpec(memory_space=pltpu.SMEM)


def call(kernel, shapes, specs, limit, cost, *operands):
    return pl.pallas_call(
        kernel,
        out_shape=shapes,
        in_specs=specs,
        out_specs=jax.tree.map(lambda _: VMEM, shapes),
        compiler_params=pltpu.CompilerParams(vmem_limit_bytes=limit * 2**20),
        cost_estimate=pl.CostEstimate(
            flops=cost, bytes_accessed=cost // 16, transcendentals=0
        ),
    )(*operands)


def first_kernel(at_ref, near_ref, far_ref, out_ref, chip_ref):
    step, first = at_ref[0], at_ref[1] == 0
    near = near_ref[step].astype(F32)
    far = far_ref[step].astype(F32)
    x = jnp.concatenate([near, far], 1)
    x = jnp.where(first, x, pltpu.roll(x, 64, 1))
    x = jnp.where(first, x, pltpu.roll(x, HALF, 0))
    row = lax.broadcasted_iota(jnp.int32, (8, 128), 0)
    chip_ref[...] = jnp.where(row < HALF, x, 0.0)
    out_ref[...] = jnp.broadcast_to(x[:HALF].astype(BF)[None], out_ref.shape)


def load_kernel(x_ref, out_ref):
    out_ref[...] = x_ref[...]


def attend_kernel(core_ref, q_ref, k_ref, v_ref, kf_ref, vf_ref, ok_ref, pack_ref, out_ref):
    base = core_ref[0] * HALF
    row = lax.broadcasted_iota(jnp.int32, (256, 256), 0)
    col = lax.broadcasted_iota(jnp.int32, (256, 256), 1)
    valid = ((row % HALF) == (col // 64)) & (ok_ref[...] > 0)

    def both(near, far, kv):
        cols = slice(kv * HEAD_SIZE, (kv + 1) * HEAD_SIZE)
        parts = []
        for r in range(HALF):
            parts += [near[r, :, cols], far[base + r, :, cols]]
        return jnp.concatenate(parts, 0)

    s = jnp.concatenate(
        [
            lax.dot_general(
                q_ref[kv * 32 : (kv + 1) * 32, :],
                both(k_ref, kf_ref, kv),
                NT,
                preferred_element_type=F32,
            )
            for kv in range(KV_HEADS)
        ],
        0,
    )
    s = jnp.where(valid, s * (1.0 / math.sqrt(HEAD_SIZE)), LOW)
    top = jnp.max(s, 1, keepdims=True).astype(BF).astype(F32)
    p = jnp.where(valid, jnp.exp(s - top), 0.0)
    total = jnp.sum(p, 1, keepdims=True)
    p = p.astype(BF)
    total_hi = total.astype(BF).astype(F32)
    lane = lax.broadcasted_iota(jnp.int32, (256, 128), 1)
    stats = jnp.where(lane < 32, total_hi, total - total_hi)
    stats = jnp.where(lane < 16, top, stats)
    acc = jnp.concatenate(
        [
            jnp.dot(
                p[kv * 32 : (kv + 1) * 32],
                both(v_ref, vf_ref, kv),
                preferred_element_type=F32,
            )
            for kv in range(KV_HEADS)
        ],
        0,
    ).reshape(32, 8, 128)
    stats = jnp.where(lane.reshape(32, 8, 128) < 64, stats.reshape(32, 8, 128), pack_ref[...][None])
    upper = lax.broadcasted_iota(jnp.int32, (32, 8, 128), 1) < HALF
    even = jnp.where(upper, acc, pltpu.roll(stats, HALF, 1)).astype(BF)
    odd = jnp.where(upper, pltpu.roll(acc, HALF, 1), stats).astype(BF)
    for t in range(32):
        out_ref[2 * t] = even[t]
        out_ref[2 * t + 1] = odd[t]


def merge_kernel(at_ref, got_ref, q_ref, fk_ref, fv_ref, w_ref, far_ref, out_ref):
    x = got_ref[...].astype(F32)
    stats = pltpu.roll(x, HALF, 1)
    tops = stats[:, :, 0:1]
    totals = stats[:, :, 16:17] + stats[:, :, 32:33]
    q = q_ref[...]
    scale = 1.0 / math.sqrt(HEAD_SIZE)
    s0 = jnp.sum(fk_ref[0] * q, 1, keepdims=True) * scale
    s1 = jnp.sum(fk_ref[1] * q, 1, keepdims=True) * scale
    second = at_ref[0] >= 1
    s1 = jnp.where(second, s1, LOW)
    peak = jnp.maximum(jnp.max(tops, 0), jnp.maximum(s0, s1))
    factor = jnp.exp(tops - peak[None])
    p0 = jnp.exp(s0 - peak)
    p1 = jnp.where(second, jnp.exp(s1 - peak), 0.0)
    below = jnp.sum(totals * factor, 0) + p0 + p1
    above = jnp.sum(x * factor, 0) + p0 * fv_ref[0] + p1 * fv_ref[1]
    row = lax.broadcasted_iota(jnp.int32, (8, 128), 0)
    attended = jnp.where(row < HALF, above / below, 0.0)
    turned = pltpu.roll(attended, 64, 1)
    turned = jnp.where(at_ref[1] == 0, attended, turned).astype(BF)
    wide = 1024
    for n in range(0, D, wide):
        w = jnp.concatenate([w_ref[:, n : n + wide], far_ref[:, n : n + wide]], 0)
        share = jnp.dot(turned, w, preferred_element_type=F32)
        for i in range(wide // 128):
            out_ref[n // 128 + i] = share[:HALF, i * 128 : (i + 1) * 128].astype(BF)


def state_kernel(got_ref, resid_ref, out_ref):
    state = jnp.sum(got_ref[...].astype(F32), 0) + resid_ref[...]
    out_ref[...] = jnp.broadcast_to(state.astype(BF)[None], out_ref.shape)


def head_kernel(u_ref, head_ref, action_ref, out_ref):
    u = jnp.concatenate([u_ref[i] for i in range(CHIPS)], 1)
    logits = lax.dot_general(head_ref[...], u, NT, preferred_element_type=F32)
    ids = lax.broadcasted_iota(jnp.int32, logits.shape, 0)
    high = jnp.max(logits, 0, keepdims=True)
    out_ref[...] = jnp.zeros_like(out_ref)
    out_ref[0:1, 0:8] = high
    out_ref[1:2, 0:8] = jnp.sum(jnp.exp(logits - high), 0, keepdims=True)
    out_ref[2:3, 0:8] = jnp.sum(
        jnp.where(ids == action_ref[...], logits, 0.0), 0, keepdims=True
    )


def pack_kernel(near_ref, far_ref, out_ref):
    a, b = near_ref[...], far_ref[...]
    high = jnp.maximum(a[0:1], b[0:1])
    total = a[1:2] * jnp.exp(a[0:1] - high) + b[1:2] * jnp.exp(b[0:1] - high)
    x = high + pltpu.roll(total, 8, 1) + pltpu.roll(a[2:3] + b[2:3], 16, 1)
    out_ref[...] = jnp.broadcast_to(x[None], out_ref.shape)


def final_kernel(start_ref, heard_ref, out_ref):
    x = heard_ref[pl.ds(start_ref[0], CHIPS)]
    high = jnp.max(x, 0, keepdims=True)
    total = jnp.sum(pltpu.roll(x, 120, 2) * jnp.exp(x - high), 0)
    target = jnp.sum(pltpu.roll(x, 112, 2), 0)
    out_ref[...] = (target - high[0] - jnp.log(total))[:, 0:8]


def on_device(
    queries,
    step_token_keys,
    step_token_values,
    stored_key_cache,
    stored_value_cache,
    lengths,
    wo_sides,
    gain_sides,
    head,
    resid,
    actions,
):
    place = lax.axis_index(GRP_TP)
    chip = lax.axis_index(CHIP)
    core = lax.axis_index(CORE)
    side = lax.axis_index("role")
    step = 1 - side
    slots = stored_key_cache.shape[1]
    row0 = core * HALF

    def rows_of(x, start, axis=0):
        return lax.dynamic_slice_in_dim(x, start, HALF, axis)

    def chip_rows(x, far):
        near = rows_of(lax.dynamic_index_in_dim(x, step, 0, keepdims=False), row0)
        far = rows_of(lax.dynamic_index_in_dim(far, step, 0, keepdims=False), row0)
        return by_core(core, near, far, 1)

    spot = jnp.stack([step, core])
    sent, q_chip = call(
        first_kernel,
        (
            jax.ShapeDtypeStruct((CHIPS, HALF, HEAD_SIZE), BF),
            jax.ShapeDtypeStruct((8, HEAD_SIZE), F32),
        ),
        [SMEM, VMEM, VMEM],
        4,
        1 << 16,
        spot,
        queries,
        swap(queries),
    )
    q = exchange(sent, CHIP).reshape(CHIPS * HALF, HEAD_SIZE)

    keys, values, gain, lengths, _ = lax.optimization_barrier(
        (stored_key_cache, stored_value_cache, gain_sides[0], lengths, q_chip)
    )
    keys_far, values_far = swap(keys), swap(values)
    keys, values = rows_of(keys, row0), rows_of(values, row0)
    gain_chip = by_core(core, gain, swap(gain), 0)

    lens = rows_of(lengths, row0)
    at = jnp.arange(slots, dtype=jnp.int32)
    position = jnp.concatenate([place * slots + at, (place + 1 - 2 * core) * slots + at])
    valid = (position[None, :] < lens[:, None]).astype(F32).reshape(1, 4 * 2 * slots)
    gain_hi = rounded(gain_chip)
    pack = jnp.concatenate([gain_hi, gain_chip - gain_hi]).reshape(HALF, 64)
    pack = jnp.concatenate([jnp.zeros_like(pack), pack], 1)
    pack = jnp.concatenate([pack, pack], 0)
    sent = call(
        attend_kernel,
        jax.ShapeDtypeStruct((CHIPS, 8, HEAD_SIZE), BF),
        [SMEM] + [VMEM] * 7,
        16,
        2 * 2 * 256 * 256 * 128,
        core[None],
        q,
        keys,
        values,
        keys_far,
        values_far,
        valid,
        pack,
    )
    got = exchange(sent, CHIP)
    w_side, resid, new_keys, new_values, _ = lax.optimization_barrier(
        (wo_sides[0], resid, step_token_keys, step_token_values, sent)
    )
    w_far = swap(w_side)
    w_mine = call(load_kernel, jax.ShapeDtypeStruct(w_side.shape, BF), [VMEM], 8, 1 << 20, w_side)
    r_chip = chip_rows(resid, swap(resid)).astype(F32)
    gains = got[:, HALF:, 64:].astype(F32).reshape(CHIPS, 2, HEAD_SIZE).sum(1)
    kv = chip // GROUP

    def fresh(x):
        x = lax.dynamic_slice(x, (0, row0, kv * HEAD_SIZE), (2, HALF, HEAD_SIZE))
        return jnp.pad(x.astype(F32), ((0, 0), (0, HALF), (0, 0)))

    share = call(
        merge_kernel,
        jax.ShapeDtypeStruct((CHIPS, HALF, HEAD_SIZE), BF),
        [SMEM] + [VMEM] * 6,
        16,
        2 * 8 * HEAD_SIZE * D,
        spot,
        got,
        q_chip,
        fresh(new_keys),
        fresh(new_values),
        w_mine,
        w_far,
    )
    shares = exchange(share, CHIP)
    head_t, actions, _ = lax.optimization_barrier((head.T, actions, share))
    head_t = call(load_kernel, jax.ShapeDtypeStruct(head_t.shape, BF), [VMEM], 24, 1 << 24, head_t)
    sent = call(
        state_kernel,
        jax.ShapeDtypeStruct((CHIPS, HALF, HEAD_SIZE), BF),
        [VMEM, VMEM],
        4,
        1 << 16,
        shares,
        r_chip,
    )
    mine = exchange(sent, CHIP)
    whole = by_core(core, mine, swap(mine), 1).astype(F32)
    square = jnp.sum(jnp.sum(whole * whole, 0), -1, keepdims=True)
    inverse = lax.rsqrt(square / D + 1e-05)
    normed = (whole * inverse[None] * gains[:, None, :]).astype(BF)
    own = lax.dynamic_index_in_dim(normed, chip, 0, keepdims=False)
    own = jnp.where(core == 0, own[:, :64], own[:, 64:])
    to_side = [(0, 1), (1, 0)]
    peer_normed = lax.ppermute(own, "role", to_side)
    width = head.shape[1]
    action = lax.dynamic_index_in_dim(actions, step, 0, keepdims=True)
    local = call(
        head_kernel,
        jax.ShapeDtypeStruct((8, 128), F32),
        [VMEM] * 3,
        24,
        2 * 8 * D * width,
        normed,
        head_t,
        action - place * width,
    )
    packed = call(
        pack_kernel,
        jax.ShapeDtypeStruct((2 * CHIPS, 1, HEAD_SIZE), F32),
        [VMEM, VMEM],
        4,
        1 << 16,
        local,
        swap(local),
    )
    heard = exchange(packed, ("role",) + CHIP)
    prob = call(
        final_kernel,
        jax.ShapeDtypeStruct((1, 8), F32),
        [SMEM, VMEM],
        4,
        1 << 16,
        ((1 - side) * CHIPS)[None],
        heard,
    )
    return prob, peer_normed[None]


def solution(mesh):
    split = Mesh(
        mesh.devices.reshape(mesh.shape["role"], mesh.shape["grp"], 4, 8, 2),
        ("role", "grp", "tp_0", "tp_1", "tp_2"),
    )
    return jax.shard_map(
        on_device,
        mesh=split,
        in_specs=(
            P(None, None, GRP_TP),
            P(),
            P(),
            P(None, GRP_TP, None),
            P(None, GRP_TP, None),
            P(),
            P("role", GRP_TP, None),
            P("role", GRP_TP),
            P(None, GRP_TP),
            P(None, None, GRP_TP),
            P(),
        ),
        out_specs=(P("role", None), P("role", None, GRP_TP)),
        check_vma=False,
    )
```

time: 119 us -> 119 us (level)
  waiting for transfers between devices: 50.7 us -> 41.9 us
  local copies, waits for them, and re-layouts: 11.3 us -> 16 us
  Pallas kernels: 5.43 us -> 9.62 us
  starting transfers between devices: 44.1 us -> 48 us
  matrix products: 2.47 us -> 0 us
  other arithmetic: 3.62 us -> 1.89 us
    all_to_all x5, waiting for transfers between devices: 46.5 us -> 36.6 us  [exchange(): return lax.all_to_all(x, axes, split_axis=0, concat_axis=0, tiled=True)]
    unnamed x7 -> x15, local copies, waits for them, and re-layouts: 6 us -> 12.4 us
    pallas_call x3 -> x9, Pallas kernels: 5.43 us -> 9.62 us  [call(): pl.pallas_call(kernel, out_shape=shapes, in_specs=specs, out_specs=jax.tr...]
    all_to_all x5, starting transfers between devices: 33.4 us -> 36 us  [exchange(): return lax.all_to_all(x, axes, split_axis=0, concat_axis=0, tiled=True)]
    dot_general x2 -> x0, matrix products: 2.47 us -> none  [the longest x1 1.53 us: on_device(): jnp.dot(a_mine, w_mine, preferred_element_type=F32)]
    broadcast_in_dim x3 -> x0, local copies, waits for them, and re-layouts: 1.94 us -> none  [to_every(): return exchange(jnp.broadcast_to(x[None], (count, *x.shape)), axes)]
    dynamic_slice x1 -> x4, local copies, waits for them, and re-layouts: 0.73 us -> 2.51 us  [rows_of(): return lax.dynamic_slice_in_dim(x, start, HALF, axis)]
    concatenate x4 -> x0, local copies, waits for them, and re-layouts: 1.4 us -> none  [by_core(): first = jnp.concatenate([mine, other], axis)]
  transfers between devices with their start and end apart: 14 -> 14, of which waited for: 9 -> 10; matrix products, arithmetic and copies ran while one was open for 6% -> 4% of each run, Pallas kernels for 3% -> 2%
where the time goes in v4:
time: 119 us; the launch traced here: 118 us
  starting transfers between devices  48 us (40%)
  waiting for transfers between devices  41.9 us (35%)
  local copies, waits for them, and re-layouts  16 us (13%)
  Pallas kernels  9.62 us (8%)
  other arithmetic  1.89 us (2%)
    all_to_all x5, waiting for transfers between devices, exchange(): return lax.all_to_all(x, axes, split_axis=0, concat_axis=0, tiled=True)  36.6 us
    all_to_all x5, starting transfers between devices, exchange(): return lax.all_to_all(x, axes, split_axis=0, concat_axis=0, tiled=True)  36 us
    unnamed x15, local copies, waits for them, and re-layouts  12.4 us
    ppermute x8, starting transfers between devices, swap(): return lax.ppermute(x, CORE, [(0, 1), (1, 0)])  11.2 us
    pallas_call x9, Pallas kernels, call(): pl.pallas_call(kernel, out_shape=shapes, in_specs=specs, out_specs=jax.tr...  9.62 us
    ppermute x8, waiting for transfers between devices, swap(): return lax.ppermute(x, CORE, [(0, 1), (1, 0)])  3.4 us
    dynamic_slice x4, local copies, waits for them, and re-layouts, rows_of(): return lax.dynamic_slice_in_dim(x, start, HALF, axis)  2.51 us
  transfers between devices with their start and end apart: 14, of which 10 were waited for; matrix products, arithmetic and copies ran while one was open for 4% of the time, Pallas kernels for 2%

profile of v4, /device:TPU:1, one launch (start us, length us, event | category | flops | bytes accessed | tf_op | source)
XLA Modules:
  0.0 118.2 jit_solution(9353139188212035849)
XLA Ops:
  0.6 3.3 %collective-permute-start = (bf16[2,8,64]{2,1,0:T(8,128)(2,1)}, bf16[2,8,64]{2,1,0:T(8,128)(2,1)S(1)}, u32[]{:S(2)}, u32[]{:S(2)}) collective-permute-start(bf16[2,8,64]{2,1,0:T(8,128)(2,1)} %near_ref.1), channel_id=1, source_target_pairs={{0,1},{1,0},{2,3},{3,2},{4,5},{5,4},{6,7},{7,6},{8,9},{9,8},{10,11... | collective-permute-start | bytes 6152 | tf_op jit(solution)/shard_map/ppermute | solution.py:26
  4.1 0.9 collective-permute-done.far_ref
  5.7 1.3 %shard_map.122 = (bf16[64,4,128]{2,1,0:T(4,128)(2,1)}, f32[8,128]{1,0:T(8,128)S(1)}) custom-call(s32[2]{0:T(128)S(1)} %pad_add_fusion.at_ref, bf16[2,8,64]{2,1,0:T(8,128)(2,1)S(1)} %copy-done.5, bf16[2,8,64]{2,1,0:T(8,128)(2,1)S(1)} %collective-permute-done.far_ref), custom_call_target="tpu_custom_call" | custom-call | flops 65536 | bytes 4096 | tf_op jit(solution)/shard_map/pallas_call | solution.py:53
  7.0 12.6 %all-to-all-start = ((bf16[64,4,128]{2,1,0:T(4,128)(2,1)}), bf16[64,4,128]{2,1,0:T(4,128)(2,1)S(1)}, u32[]{:S(2)}, u32[]{:S(2)}) async-start(bf16[64,4,128]{2,1,0:T(4,128)(2,1)} %get-tuple-element.14), calls=%async_computation | async-start | bytes 131072 | tf_op jit(solution)/shard_map/all_to_all | solution.py:30
  20.4 1.1 constant_dynamic-slice_fusion.5
  21.5 0.7 dynamic_slice.38
  22.8 0.8 collective-permute-done.3
  23.6 0.8 broadcast_select_fusion
  24.6 6.1 %all-to-all-done = bf16[64,4,128]{2,1,0:T(4,128)(2,1)S(1)} async-done(((bf16[64,4,128]{2,1,0:T(4,128)(2,1)}), bf16[64,4,128]{2,1,0:T(4,128)(2,1)S(1)}, u32[]{:S(2)}, u32[]{:S(2)}) %all-to-all-start) | async-done | bytes 65568 | tf_op jit(solution)/shard_map/all_to_all | solution.py:30
  30.7 1.2 %shard_map.123 = bf16[64,8,128]{2,1,0:T(8,128)(2,1)} custom-call(s32[1]{0:T(128)} %bitcast.2.core_ref, bf16[256,128]{1,0:T(8,128)(2,1)S(1)} %bitcast.17, bf16[4,32,1024]{2,1,0:T(8,128)(2,1)S(1)} %get-tuple-element.29.k_ref, bf16[4,32,1024]{2,1,0:T(8,128)(2,1)S(1)} %get-tuple-element.28.v_ref, bf16[8,32,1024]{2,1,0:T(8,128)(2,1)S(1)} %collective-permute-done.1.kf_ref, ...), custom_call_target="tpu_custom_call" | custom-call | flops 33554432 | bytes 2097152 | tf_op jit(solution)/shard_map/pallas_call | solution.py:53
  31.9 1.7 %collective-permute-start.4 = (bf16[64,8192]{1,0:T(8,128)(2,1)}, bf16[64,8192]{1,0:T(8,128)(2,1)S(1)}, u32[]{:S(2)}, u32[]{:S(2)}) collective-permute-start(bf16[64,8192]{1,0:T(8,128)(2,1)} %bitcast.15), channel_id=1, source_target_pairs={{0,1},{1,0},{2,3},{3,2},{4,5},{5,4},{6,7},{7,6},{8,9},{9,8},{10,11... | collective-permute-start | bytes 3145736 | tf_op jit(solution)/shard_map/ppermute | solution.py:26
  33.5 5.1 %all-to-all-start.1 = ((bf16[64,8,128]{2,1,0:T(8,128)(2,1)}), bf16[64,8,128]{2,1,0:T(8,128)(2,1)S(1)}, u32[]{:S(2)}, u32[]{:S(2)}) async-start(bf16[64,8,128]{2,1,0:T(8,128)(2,1)} %shard_map.123), calls=%async_computation.1 | async-start | bytes 262144 | tf_op jit(solution)/shard_map/all_to_all | solution.py:30
  38.7 0.8 constant_dynamic-slice_fusion.3
  40.7 1.2 %copy-done.4 = bf16[1,64,8192]{2,1,0:T(8,128)(2,1)S(1)} copy-done((bf16[1,64,8192]{2,1,0:T(8,128)(2,1)S(1)}, bf16[1,64,8192]{2,1,0:T(8,128)(2,1)}, u32[]{:S(2)}) %copy-start.4) | copy-done | bytes 1048600
  42.0 8.2 %all-to-all-done.1.got_ref = bf16[64,8,128]{2,1,0:T(8,128)(2,1)S(1)} async-done(((bf16[64,8,128]{2,1,0:T(8,128)(2,1)}), bf16[64,8,128]{2,1,0:T(8,128)(2,1)S(1)}, u32[]{:S(2)}, u32[]{:S(2)}) %all-to-all-start.1) | async-done | bytes 131104 | tf_op jit(solution)/shard_map/all_to_all | solution.py:30
  50.2 1.9 %shard_map.125 = bf16[64,4,128]{2,1,0:T(4,128)(2,1)} custom-call(s32[2]{0:T(128)S(1)} %pad_add_fusion.at_ref, bf16[64,8,128]{2,1,0:T(8,128)(2,1)S(1)} %all-to-all-done.1.got_ref, f32[8,128]{1,0:T(8,128)S(1)} %get-tuple-element.15.q_ref, f32[2,8,128]{2,1,0:T(8,128)S(1)} %pad_convert_fusion.1.fk_ref, f32[2,8,128]{2,1,0:T(8,128)S(1)} %pad_convert_fusion.fv_ref, ...), custom_call_target="tpu_custom_call" | custom-call | flops 16777216 | bytes 1048576 | tf_op jit(solution)/shard_map/pallas_call | solution.py:53
  52.1 4.8 %all-to-all-start.2 = ((bf16[64,4,128]{2,1,0:T(4,128)(2,1)}), bf16[64,4,128]{2,1,0:T(4,128)(2,1)S(1)}, u32[]{:S(2)}, u32[]{:S(2)}) async-start(bf16[64,4,128]{2,1,0:T(4,128)(2,1)} %shard_map.125), calls=%async_computation.2 | async-start | bytes 131072 | tf_op jit(solution)/shard_map/all_to_all | solution.py:30
  57.1 10.9 %all-to-all-done.2.got_ref = bf16[64,4,128]{2,1,0:T(4,128)(2,1)S(1)} async-done(((bf16[64,4,128]{2,1,0:T(4,128)(2,1)}), bf16[64,4,128]{2,1,0:T(4,128)(2,1)S(1)}, u32[]{:S(2)}, u32[]{:S(2)}) %all-to-all-start.2) | async-done | bytes 65568 | tf_op jit(solution)/shard_map/all_to_all | solution.py:30
  68.7 4.6 %all-to-all-start.3 = ((bf16[64,4,128]{2,1,0:T(4,128)(2,1)}), bf16[64,4,128]{2,1,0:T(4,128)(2,1)S(1)}, u32[]{:S(2)}, u32[]{:S(2)}) async-start(bf16[64,4,128]{2,1,0:T(4,128)(2,1)} %shard_map.126), calls=%async_computation.3 | async-start | bytes 131072 | tf_op jit(solution)/shard_map/all_to_all | solution.py:30
  73.6 3.3 %copy-done.3 = bf16[8192,501]{0,1:T(8,128)(2,1)S(1)} copy-done((bf16[8192,501]{0,1:T(8,128)(2,1)S(1)}, bf16[8192,501]{0,1:T(8,128)(2,1)}, u32[]{:S(2)}) %copy-start.3) | copy-done | bytes 8208408
  77.5 3.2 %copy-done.1 = bf16[501,8192]{1,0:T(8,128)(2,1)} copy-done((bf16[501,8192]{1,0:T(8,128)(2,1)}, bf16[501,8192]{1,0:T(8,128)(2,1)S(1)}, u32[]{:S(2)}) %copy-start.1) | copy-done | bytes 8208408
  80.7 3.6 %all-to-all-done.3 = bf16[64,4,128]{2,1,0:T(4,128)(2,1)S(1)} async-done(((bf16[64,4,128]{2,1,0:T(4,128)(2,1)}), bf16[64,4,128]{2,1,0:T(4,128)(2,1)S(1)}, u32[]{:S(2)}, u32[]{:S(2)}) %all-to-all-start.3) | async-done | bytes 65568 | tf_op jit(solution)/shard_map/all_to_all | solution.py:30
  84.3 4.0 %collective-permute-start.6 = (bf16[64,4,128]{2,1,0:T(4,128)(2,1)S(1)}, bf16[64,4,128]{2,1,0:T(4,128)(2,1)S(1)}, u32[]{:S(2)}, u32[]{:S(2)}) collective-permute-start(bf16[64,4,128]{2,1,0:T(4,128)(2,1)S(1)} %all-to-all-done.3), channel_id=1, source_target_pairs={{0,1},{1,0},{2,3},{3,2},{4,5},{5,4},{6,7},{7,6},{8,9},{9,8},{10,11... | collective-permute-start | bytes 196616 | tf_op jit(solution)/shard_map/ppermute | solution.py:26
  88.3 0.9 collective-permute-done.6
  89.6 3.3 %copy-done.2 = bf16[501,8192]{1,0:T(8,128)(2,1)S(1)} copy-done((bf16[501,8192]{1,0:T(8,128)(2,1)S(1)}, bf16[501,8192]{1,0:T(8,128)(2,1)}, u32[]{:S(2)}) %copy-start.2) | copy-done | bytes 8208408
  93.0 2.4 %shard_map.128.near_ref = f32[8,128]{1,0:T(8,128)S(1)} custom-call(bf16[64,8,128]{2,1,0:T(8,128)(2,1)S(1)} %fusion.2.u_ref, bf16[501,8192]{1,0:T(8,128)(2,1)S(1)} %copy-done.2, s32[1,8]{1,0:T(1,128)S(1)} %fusion.6.action_ref), custom_call_target="tpu_custom_call" | custom-call | flops 65667072 | bytes 4104192 | tf_op jit(solution)/shard_map/pallas_call | solution.py:53
  95.8 0.8 collective-permute-done.7.far_ref
  96.6 0.7 shard_map.129
  97.3 9.0 %all-to-all-start.4 = ((f32[128,1,128]{2,1,0:T(1,128)}), f32[128,1,128]{2,1,0:T(1,128)S(1)}, u32[]{:S(2)}, u32[]{:S(2)}) async-start(f32[128,1,128]{2,1,0:T(1,128)} %shard_map.129), calls=%async_computation.4 | async-start | bytes 131072 | tf_op jit(solution)/shard_map/all_to_all | solution.py:30
  106.4 0.9 collective-permute-start.8
  107.3 1.8 %collective-permute-done.8 = bf16[8,64]{1,0:T(8,128)(2,1)S(1)} collective-permute-done((bf16[8,64]{1,0:T(8,128)(2,1)S(1)}, bf16[8,64]{1,0:T(8,128)(2,1)S(1)}, u32[]{:S(2)}, u32[]{:S(2)}) %collective-permute-start.8) | collective-permute-done | bytes 1056 | tf_op jit(solution)/shard_map/ppermute | solution.py:321
  109.2 7.7 %all-to-all-done.4.heard_ref = f32[128,1,128]{2,1,0:T(1,128)S(1)} async-done(((f32[128,1,128]{2,1,0:T(1,128)}), f32[128,1,128]{2,1,0:T(1,128)S(1)}, u32[]{:S(2)}, u32[]{:S(2)}) %all-to-all-start.4) | async-done | bytes 65568 | tf_op jit(solution)/shard_map/all_to_all | solution.py:30
  (48 shorter events, 7.6 us)
Async XLA Ops:
  0.6 38.0 %copy-start = (bf16[2,8,1024]{2,1,0:T(8,128)(2,1)S(1)}, bf16[2,8,1024]{2,1,0:T(8,128)(2,1)}, u32[]{:S(2)}) copy-start(bf16[2,8,1024]{2,1,0:T(8,128)(2,1)} %param.12) | copy-start | bytes 98308
  0.6 4.4 %collective-permute-start = (bf16[2,8,64]{2,1,0:T(8,128)(2,1)}, bf16[2,8,64]{2,1,0:T(8,128)(2,1)S(1)}, u32[]{:S(2)}, u32[]{:S(2)}) collective-permute-start(bf16[2,8,64]{2,1,0:T(8,128)(2,1)} %near_ref.1), channel_id=1, source_target_pairs={{0,1},{1,0},{2,3},{3,2},{4,5},{5,4},{6,7},{7,6},{8,9},{9,8},{10,11... | collective-permute-start | bytes 6152 | tf_op jit(solution)/shard_map/ppermute | solution.py:26
  5.0 0.7 copy-start.5
  7.0 23.7 %all-to-all-start = ((bf16[64,4,128]{2,1,0:T(4,128)(2,1)}), bf16[64,4,128]{2,1,0:T(4,128)(2,1)S(1)}, u32[]{:S(2)}, u32[]{:S(2)}) async-start(bf16[64,4,128]{2,1,0:T(4,128)(2,1)} %get-tuple-element.14), calls=%async_computation | async-start | bytes 131072 | tf_op jit(solution)/shard_map/all_to_all | solution.py:30
  19.6 11.1 %collective-permute-start.1 = (bf16[8,32,1024]{2,1,0:T(8,128)(2,1)}, bf16[8,32,1024]{2,1,0:T(8,128)(2,1)S(1)}, u32[]{:S(2)}, u32[]{:S(2)}) collective-permute-start(bf16[8,32,1024]{2,1,0:T(8,128)(2,1)} %param.14), channel_id=1, source_target_pairs={{0,1},{1,0},{2,3},{3,2},{4,5},{5,4},{6,7},{7,6},{8,9},{9,8},{10,11... | collective-permute-start | bytes 1572872 | tf_op jit(solution)/shard_map/ppermute | solution.py:26
  20.3 10.4 %collective-permute-start.2 = (bf16[8,32,1024]{2,1,0:T(8,128)(2,1)}, bf16[8,32,1024]{2,1,0:T(8,128)(2,1)S(1)}, u32[]{:S(2)}, u32[]{:S(2)}) collective-permute-start(bf16[8,32,1024]{2,1,0:T(8,128)(2,1)} %param.15), channel_id=1, source_target_pairs={{0,1},{1,0},{2,3},{3,2},{4,5},{5,4},{6,7},{7,6},{8,9},{9,8},{10,11... | collective-permute-start | bytes 1572872 | tf_op jit(solution)/shard_map/ppermute | solution.py:26
  22.2 1.4 %collective-permute-start.3 = (f32[64]{0:T(128)}, f32[64]{0:T(128)S(1)}, u32[]{:S(2)}, u32[]{:S(2)}) collective-permute-start(f32[64]{0:T(128)} %bitcast.19), channel_id=1, source_target_pairs={{0,1},{1,0},{2,3},{3,2},{4,5},{5,4},{6,7},{7,6},{8,9},{9,8},{10,11... | collective-permute-start | bytes 776 | tf_op jit(solution)/shard_map/ppermute | solution.py:26
  31.9 18.3 %collective-permute-start.4 = (bf16[64,8192]{1,0:T(8,128)(2,1)}, bf16[64,8192]{1,0:T(8,128)(2,1)S(1)}, u32[]{:S(2)}, u32[]{:S(2)}) collective-permute-start(bf16[64,8192]{1,0:T(8,128)(2,1)} %bitcast.15), channel_id=1, source_target_pairs={{0,1},{1,0},{2,3},{3,2},{4,5},{5,4},{6,7},{7,6},{8,9},{9,8},{10,11... | collective-permute-start | bytes 3145736 | tf_op jit(solution)/shard_map/ppermute | solution.py:26
  33.5 16.7 %all-to-all-start.1 = ((bf16[64,8,128]{2,1,0:T(8,128)(2,1)}), bf16[64,8,128]{2,1,0:T(8,128)(2,1)S(1)}, u32[]{:S(2)}, u32[]{:S(2)}) async-start(bf16[64,8,128]{2,1,0:T(8,128)(2,1)} %shard_map.123), calls=%async_computation.1 | async-start | bytes 262144 | tf_op jit(solution)/shard_map/all_to_all | solution.py:30
  39.5 17.5 %collective-permute-start.5 = (bf16[2,8,64]{2,1,0:T(8,128)(2,1)}, bf16[2,8,64]{2,1,0:T(8,128)(2,1)S(1)}, u32[]{:S(2)}, u32[]{:S(2)}) collective-permute-start(bf16[2,8,64]{2,1,0:T(8,128)(2,1)} %param.20), channel_id=1, source_target_pairs={{0,1},{1,0},{2,3},{3,2},{4,5},{5,4},{6,7},{7,6},{8,9},{9,8},{10,11... | collective-permute-start | bytes 6152 | tf_op jit(solution)/shard_map/ppermute | solution.py:26
  40.7 1.2 %copy-start.4 = (bf16[1,64,8192]{2,1,0:T(8,128)(2,1)S(1)}, bf16[1,64,8192]{2,1,0:T(8,128)(2,1)}, u32[]{:S(2)}) copy-start(bf16[1,64,8192]{2,1,0:T(8,128)(2,1)} %param.17) | copy-start | bytes 3145732
  52.1 15.9 %all-to-all-start.2 = ((bf16[64,4,128]{2,1,0:T(4,128)(2,1)}), bf16[64,4,128]{2,1,0:T(4,128)(2,1)S(1)}, u32[]{:S(2)}, u32[]{:S(2)}) async-start(bf16[64,4,128]{2,1,0:T(4,128)(2,1)} %shard_map.125), calls=%async_computation.2 | async-start | bytes 131072 | tf_op jit(solution)/shard_map/all_to_all | solution.py:30
  68.7 15.6 %all-to-all-start.3 = ((bf16[64,4,128]{2,1,0:T(4,128)(2,1)}), bf16[64,4,128]{2,1,0:T(4,128)(2,1)S(1)}, u32[]{:S(2)}, u32[]{:S(2)}) async-start(bf16[64,4,128]{2,1,0:T(4,128)(2,1)} %shard_map.126), calls=%async_computation.3 | async-start | bytes 131072 | tf_op jit(solution)/shard_map/all_to_all | solution.py:30
  73.6 3.3 %copy-start.3 = (bf16[8192,501]{0,1:T(8,128)(2,1)S(1)}, bf16[8192,501]{0,1:T(8,128)(2,1)}, u32[]{:S(2)}) copy-start(bf16[8192,501]{0,1:T(8,128)(2,1)} %param.19) | copy-start | bytes 24625156
  77.0 11.3 %copy-start.6 = (s32[2,8]{1,0:T(2,128)S(1)}, s32[2,8]{1,0:T(2,128)}, u32[]{:S(2)}) copy-start(s32[2,8]{1,0:T(2,128)} %param.21) | copy-start | bytes 196
  77.5 3.2 %copy-start.1 = (bf16[501,8192]{1,0:T(8,128)(2,1)}, bf16[501,8192]{1,0:T(8,128)(2,1)S(1)}, u32[]{:S(2)}) copy-start(bf16[501,8192]{1,0:T(8,128)(2,1)S(1)} %shard_map.127.head_ref) | copy-start | bytes 24625156
  84.3 4.9 %collective-permute-start.6 = (bf16[64,4,128]{2,1,0:T(4,128)(2,1)S(1)}, bf16[64,4,128]{2,1,0:T(4,128)(2,1)S(1)}, u32[]{:S(2)}, u32[]{:S(2)}) collective-permute-start(bf16[64,4,128]{2,1,0:T(4,128)(2,1)S(1)} %all-to-all-done.3), channel_id=1, source_target_pairs={{0,1},{1,0},{2,3},{3,2},{4,5},{5,4},{6,7},{7,6},{8,9},{9,8},{10,11... | collective-permute-start | bytes 196616 | tf_op jit(solution)/shard_map/ppermute | solution.py:26
  89.6 3.3 %copy-start.2 = (bf16[501,8192]{1,0:T(8,128)(2,1)S(1)}, bf16[501,8192]{1,0:T(8,128)(2,1)}, u32[]{:S(2)}) copy-start(bf16[501,8192]{1,0:T(8,128)(2,1)} %copy-done.1) | copy-start | bytes 24625156
  95.3 1.3 %collective-permute-start.7 = (f32[8,128]{1,0:T(8,128)S(1)}, f32[8,128]{1,0:T(8,128)S(1)}, u32[]{:S(2)}, u32[]{:S(2)}) collective-permute-start(f32[8,128]{1,0:T(8,128)S(1)} %shard_map.128.near_ref), channel_id=1, source_target_pairs={{0,1},{1,0},{2,3},{3,2},{4,5},{5,4},{6,7},{7,6},{8,9},{9,8},{10,11... | collective-permute-start | bytes 12296 | tf_op jit(solution)/shard_map/ppermute | solution.py:26
  97.3 19.6 %all-to-all-start.4 = ((f32[128,1,128]{2,1,0:T(1,128)}), f32[128,1,128]{2,1,0:T(1,128)S(1)}, u32[]{:S(2)}, u32[]{:S(2)}) async-start(f32[128,1,128]{2,1,0:T(1,128)} %shard_map.129), calls=%async_computation.4 | async-start | bytes 131072 | tf_op jit(solution)/shard_map/all_to_all | solution.py:30
  106.4 2.8 %collective-permute-start.8 = (bf16[8,64]{1,0:T(8,128)(2,1)S(1)}, bf16[8,64]{1,0:T(8,128)(2,1)S(1)}, u32[]{:S(2)}, u32[]{:S(2)}) collective-permute-start(bf16[8,64]{1,0:T(8,128)(2,1)S(1)} %slice_select_fusion), channel_id=1, source_target_pairs={{0,128},{128,0},{1,129},{129,1},{2,130},{130,2},{3,131},{131,3},{4... | collective-permute-start | bytes 3080 | tf_op jit(solution)/shard_map/ppermute | solution.py:321

commit v5 on v4

--- a/solution.py
+++ b/solution.py
@@ -30,10 +30,6 @@
     return lax.all_to_all(x, axes, split_axis=0, concat_axis=0, tiled=True)
 
 
-def to_every(x, axes, count):
-    return exchange(jnp.broadcast_to(x[None], (count, *x.shape)), axes)
-
-
 def rounded(x):
     return lax.reduce_precision(x, 8, 7)
 
@@ -60,18 +56,6 @@
             flops=cost, bytes_accessed=cost // 16, transcendentals=0
         ),
     )(*operands)
-
-
-def first_kernel(at_ref, near_ref, far_ref, out_ref, chip_ref):
-    step, first = at_ref[0], at_ref[1] == 0
-    near = near_ref[step].astype(F32)
-    far = far_ref[step].astype(F32)
-    x = jnp.concatenate([near, far], 1)
-    x = jnp.where(first, x, pltpu.roll(x, 64, 1))
-    x = jnp.where(first, x, pltpu.roll(x, HALF, 0))
-    row = lax.broadcasted_iota(jnp.int32, (8, 128), 0)
-    chip_ref[...] = jnp.where(row < HALF, x, 0.0)
-    out_ref[...] = jnp.broadcast_to(x[:HALF].astype(BF)[None], out_ref.shape)
 
 
 def load_kernel(x_ref, out_ref):
@@ -225,23 +209,13 @@
         return by_core(core, near, far, 1)
 
     spot = jnp.stack([step, core])
-    sent, q_chip = call(
-        first_kernel,
-        (
-            jax.ShapeDtypeStruct((CHIPS, HALF, HEAD_SIZE), BF),
-            jax.ShapeDtypeStruct((8, HEAD_SIZE), F32),
-        ),
-        [SMEM, VMEM, VMEM],
-        4,
-        1 << 16,
-        spot,
-        queries,
-        swap(queries),
-    )
-    q = exchange(sent, CHIP).reshape(CHIPS * HALF, HEAD_SIZE)
+    q_half = chip_rows(queries, swap(queries))
+    q_chip = jnp.pad(q_half.astype(F32), ((0, HALF), (0, 0)))
+    q = exchange(jnp.broadcast_to(q_half[None], (CHIPS, *q_half.shape)), CHIP)
+    q = q.reshape(CHIPS * HALF, HEAD_SIZE)
 
     keys, values, gain, lengths, _ = lax.optimization_barrier(
-        (stored_key_cache, stored_value_cache, gain_sides[0], lengths, q_chip)
+        (stored_key_cache, stored_value_cache, gain_sides[0], lengths, q_half)
     )
     keys_far, values_far = swap(keys), swap(values)
     keys, values = rows_of(keys, row0), rows_of(values, row0)
@@ -290,7 +264,7 @@
         [SMEM] + [VMEM] * 6,
         16,
         2 * 8 * HEAD_SIZE * D,
-        spot,
+        jnp.stack([step, core]),
         got,
         q_chip,
         fresh(new_keys),
@@ -299,8 +273,6 @@
         w_far,
     )
     shares = exchange(share, CHIP)
-    head_t, actions, _ = lax.optimization_barrier((head.T, actions, share))
-    head_t = call(load_kernel, jax.ShapeDtypeStruct(head_t.shape, BF), [VMEM], 24, 1 << 24, head_t)
     sent = call(
         state_kernel,
         jax.ShapeDtypeStruct((CHIPS, HALF, HEAD_SIZE), BF),
@@ -328,7 +300,7 @@
         24,
         2 * 8 * D * width,
         normed,
-        head_t,
+        head.T,
         action - place * width,
     )
     packed = call(

time: 119 us -> 118 us (level)
  waiting for transfers between devices: 41.9 us -> 52.9 us
  local copies, waits for them, and re-layouts: 16 us -> 10.9 us
  starting transfers between devices: 48 us -> 43.3 us
  Pallas kernels: 9.62 us -> 7.82 us
    all_to_all x5, waiting for transfers between devices: 36.6 us -> 49.4 us  [exchange(): return lax.all_to_all(x, axes, split_axis=0, concat_axis=0, tiled=True)]
    unnamed x15 -> x7, local copies, waits for them, and re-layouts: 12.4 us -> 5.15 us
    all_to_all x5, starting transfers between devices: 36 us -> 32.6 us  [exchange(): return lax.all_to_all(x, axes, split_axis=0, concat_axis=0, tiled=True)]
    pallas_call x9 -> x7, Pallas kernels: 9.62 us -> 7.82 us  [call(): pl.pallas_call(kernel, out_shape=shapes, in_specs=specs, out_specs=jax.tr...]
    ppermute x8, waiting for transfers between devices: 3.4 us -> 1.68 us  [swap(): return lax.ppermute(x, CORE, [(0, 1), (1, 0)])]
    ppermute x8, starting transfers between devices: 11.2 us -> 9.86 us  [swap(): return lax.ppermute(x, CORE, [(0, 1), (1, 0)])]
    dynamic_slice x4 -> x5, local copies, waits for them, and re-layouts: 2.51 us -> 3.37 us  [rows_of(): return lax.dynamic_slice_in_dim(x, start, HALF, axis)]
  transfers between devices with their start and end apart: 14 -> 14, of which waited for: 10 -> 9; matrix products, arithmetic and copies ran while one was open for 4% -> 5% of each run, Pallas kernels for 2% -> 2%
where the time goes in v5:
time: 118 us
  waiting for transfers between devices  52.9 us (45%)
  starting transfers between devices  43.3 us (37%)
  local copies, waits for them, and re-layouts  10.9 us (9%)
  Pallas kernels  7.82 us (7%)
  other arithmetic  1.98 us (2%)
    all_to_all x5, waiting for transfers between devices, exchange(): return lax.all_to_all(x, axes, split_axis=0, concat_axis=0, tiled=True)  49.4 us
    all_to_all x5, starting transfers between devices, exchange(): return lax.all_to_all(x, axes, split_axis=0, concat_axis=0, tiled=True)  32.6 us
    ppermute x8, starting transfers between devices, swap(): return lax.ppermute(x, CORE, [(0, 1), (1, 0)])  9.86 us
    pallas_call x7, Pallas kernels, call(): pl.pallas_call(kernel, out_shape=shapes, in_specs=specs, out_specs=jax.tr...  7.82 us
    unnamed x7, local copies, waits for them, and re-layouts  5.15 us
    dynamic_slice x5, local copies, waits for them, and re-layouts, rows_of(): return lax.dynamic_slice_in_dim(x, start, HALF, axis)  3.37 us
  transfers between devices with their start and end apart: 14, of which 9 were waited for; matrix products, arithmetic and copies ran while one was open for 5% of the time, Pallas kernels for 2%

profile of v5, /device:TPU:1, one launch (start us, length us, event | category | flops | bytes accessed | tf_op | source)
XLA Modules:
  0.0 117.8 jit_solution(14698839882520045683)
XLA Ops:
  0.6 3.3 %collective-permute-start = (bf16[2,8,64]{2,1,0:T(8,128)(2,1)}, bf16[2,8,64]{2,1,0:T(8,128)(2,1)S(1)}, u32[]{:S(2)}, u32[]{:S(2)}) collective-permute-start(bf16[2,8,64]{2,1,0:T(8,128)(2,1)} %param.11), channel_id=1, source_target_pairs={{0,1},{1,0},{2,3},{3,2},{4,5},{5,4},{6,7},{7,6},{8,9},{9,8},{10,11... | collective-permute-start | bytes 6152 | tf_op jit(solution)/shard_map/ppermute | solution.py:26
  4.0 0.7 fusion.4
  5.1 1.0 constant_dynamic-slice_fusion.7.k_ref
  6.5 1.0 constant_dynamic-slice_fusion.6.v_ref
  7.7 0.7 dynamic_slice.48
  8.9 0.7 broadcast_in_dim.7
  9.6 12.6 %all-to-all-start = ((bf16[64,4,128]{2,1,0:T(4,128)(2,1)}), bf16[64,4,128]{2,1,0:T(4,128)(2,1)S(1)}, u32[]{:S(2)}, u32[]{:S(2)}) async-start(bf16[64,4,128]{2,1,0:T(4,128)(2,1)} %broadcast_in_dim.7), calls=%async_computation | async-start | bytes 131072 | tf_op jit(solution)/shard_map/all_to_all | solution.py:30
  22.2 0.8 broadcast_select_fusion
  23.2 10.3 %all-to-all-done = bf16[64,4,128]{2,1,0:T(4,128)(2,1)S(1)} async-done(((bf16[64,4,128]{2,1,0:T(4,128)(2,1)}), bf16[64,4,128]{2,1,0:T(4,128)(2,1)S(1)}, u32[]{:S(2)}, u32[]{:S(2)}) %all-to-all-start) | async-done | bytes 65568 | tf_op jit(solution)/shard_map/all_to_all | solution.py:30
  33.4 1.2 %shard_map.122 = bf16[64,8,128]{2,1,0:T(8,128)(2,1)} custom-call(s32[1]{0:T(128)} %bitcast.2.core_ref, bf16[256,128]{1,0:T(8,128)(2,1)S(1)} %bitcast.21, bf16[4,32,1024]{2,1,0:T(8,128)(2,1)S(1)} %constant_dynamic-slice_fusion.7.k_ref, bf16[4,32,1024]{2,1,0:T(8,128)(2,1)S(1)} %constant_dynamic-slice_fusion.6.v_ref, ...), custom_call_target="tpu_custom_call" | custom-call | flops 33554432 | bytes 2097152 | tf_op jit(solution)/shard_map/pallas_call | solution.py:49
  34.7 1.3 %collective-permute-start.4 = (bf16[64,8192]{1,0:T(8,128)(2,1)}, bf16[64,8192]{1,0:T(8,128)(2,1)S(1)}, u32[]{:S(2)}, u32[]{:S(2)}) collective-permute-start(bf16[64,8192]{1,0:T(8,128)(2,1)} %bitcast.19), channel_id=1, source_target_pairs={{0,1},{1,0},{2,3},{3,2},{4,5},{5,4},{6,7},{7,6},{8,9},{9,8},{10,11... | collective-permute-start | bytes 3145736 | tf_op jit(solution)/shard_map/ppermute | solution.py:26
  36.0 4.6 %all-to-all-start.1 = ((bf16[64,8,128]{2,1,0:T(8,128)(2,1)}), bf16[64,8,128]{2,1,0:T(8,128)(2,1)S(1)}, u32[]{:S(2)}, u32[]{:S(2)}) async-start(bf16[64,8,128]{2,1,0:T(8,128)(2,1)} %shard_map.122), calls=%async_computation.1 | async-start | bytes 262144 | tf_op jit(solution)/shard_map/all_to_all | solution.py:30
  40.7 0.8 constant_dynamic-slice_fusion.4
  41.6 0.7 fusion.6
  42.3 1.2 %copy-done.1 = bf16[1,64,8192]{2,1,0:T(8,128)(2,1)S(1)} copy-done((bf16[1,64,8192]{2,1,0:T(8,128)(2,1)S(1)}, bf16[1,64,8192]{2,1,0:T(8,128)(2,1)}, u32[]{:S(2)}) %copy-start.1) | copy-done | bytes 1048600
  43.6 9.5 %all-to-all-done.1.got_ref = bf16[64,8,128]{2,1,0:T(8,128)(2,1)S(1)} async-done(((bf16[64,8,128]{2,1,0:T(8,128)(2,1)}), bf16[64,8,128]{2,1,0:T(8,128)(2,1)S(1)}, u32[]{:S(2)}, u32[]{:S(2)}) %all-to-all-start.1) | async-done | bytes 131104 | tf_op jit(solution)/shard_map/all_to_all | solution.py:30
  53.0 2.0 %shard_map.124 = bf16[64,4,128]{2,1,0:T(4,128)(2,1)} custom-call(s32[2]{0:T(128)S(1)} %pad_add_fusion.at_ref, bf16[64,8,128]{2,1,0:T(8,128)(2,1)S(1)} %all-to-all-done.1.got_ref, f32[8,128]{1,0:T(8,128)S(1)} %pad_convert_fusion.2.q_ref, f32[2,8,128]{2,1,0:T(8,128)S(1)} %pad_convert_fusion.1.fk_ref, f32[2,8,128]{2,1,0:T(8,128)S(1)} %pad_convert_fusion.fv_ref, ...), custom_call_target="tpu_custom_call" | custom-call | flops 16777216 | bytes 1048576 | tf_op jit(solution)/shard_map/pallas_call | solution.py:49
  55.0 4.6 %all-to-all-start.2 = ((bf16[64,4,128]{2,1,0:T(4,128)(2,1)}), bf16[64,4,128]{2,1,0:T(4,128)(2,1)S(1)}, u32[]{:S(2)}, u32[]{:S(2)}) async-start(bf16[64,4,128]{2,1,0:T(4,128)(2,1)} %shard_map.124), calls=%async_computation.2 | async-start | bytes 131072 | tf_op jit(solution)/shard_map/all_to_all | solution.py:30
  59.7 10.9 %all-to-all-done.2.got_ref = bf16[64,4,128]{2,1,0:T(4,128)(2,1)S(1)} async-done(((bf16[64,4,128]{2,1,0:T(4,128)(2,1)}), bf16[64,4,128]{2,1,0:T(4,128)(2,1)S(1)}, u32[]{:S(2)}, u32[]{:S(2)}) %all-to-all-start.2) | async-done | bytes 65568 | tf_op jit(solution)/shard_map/all_to_all | solution.py:30
  70.6 0.7 shard_map.125
  71.3 4.6 %all-to-all-start.3 = ((bf16[64,4,128]{2,1,0:T(4,128)(2,1)}), bf16[64,4,128]{2,1,0:T(4,128)(2,1)S(1)}, u32[]{:S(2)}, u32[]{:S(2)}) async-start(bf16[64,4,128]{2,1,0:T(4,128)(2,1)} %shard_map.125), calls=%async_computation.3 | async-start | bytes 131072 | tf_op jit(solution)/shard_map/all_to_all | solution.py:30
  76.0 11.0 %all-to-all-done.3 = bf16[64,4,128]{2,1,0:T(4,128)(2,1)S(1)} async-done(((bf16[64,4,128]{2,1,0:T(4,128)(2,1)}), bf16[64,4,128]{2,1,0:T(4,128)(2,1)S(1)}, u32[]{:S(2)}, u32[]{:S(2)}) %all-to-all-start.3) | async-done | bytes 65568 | tf_op jit(solution)/shard_map/all_to_all | solution.py:30
  87.0 3.5 %collective-permute-start.6 = (bf16[64,4,128]{2,1,0:T(4,128)(2,1)S(1)}, bf16[64,4,128]{2,1,0:T(4,128)(2,1)S(1)}, u32[]{:S(2)}, u32[]{:S(2)}) collective-permute-start(bf16[64,4,128]{2,1,0:T(4,128)(2,1)S(1)} %all-to-all-done.3), channel_id=1, source_target_pairs={{0,1},{1,0},{2,3},{3,2},{4,5},{5,4},{6,7},{7,6},{8,9},{9,8},{10,11... | collective-permute-start | bytes 196616 | tf_op jit(solution)/shard_map/ppermute | solution.py:26
  91.8 3.3 %copy-done = bf16[8192,501]{0,1:T(8,128)(2,1)S(1)} copy-done((bf16[8192,501]{0,1:T(8,128)(2,1)S(1)}, bf16[8192,501]{0,1:T(8,128)(2,1)}, u32[]{:S(2)}) %copy-start) | copy-done | bytes 8208408
  95.1 2.4 %shard_map.126.near_ref = f32[8,128]{1,0:T(8,128)S(1)} custom-call(bf16[64,8,128]{2,1,0:T(8,128)(2,1)S(1)} %fusion.2.u_ref, bf16[501,8192]{1,0:T(8,128)(2,1)S(1)} %bitcast.18, s32[1,8]{1,0:T(1,128)S(1)} %fusion.9.action_ref), custom_call_target="tpu_custom_call" | custom-call | flops 65667072 | bytes 4104192 | tf_op jit(solution)/shard_map/pallas_call | solution.py:49
  98.1 0.8 collective-permute-done.7.far_ref
  99.0 0.8 shard_map.127
  99.7 6.2 %all-to-all-start.4 = ((f32[128,1,128]{2,1,0:T(1,128)}), f32[128,1,128]{2,1,0:T(1,128)S(1)}, u32[]{:S(2)}, u32[]{:S(2)}) async-start(f32[128,1,128]{2,1,0:T(1,128)} %shard_map.127), calls=%async_computation.4 | async-start | bytes 131072 | tf_op jit(solution)/shard_map/all_to_all | solution.py:30
  106.0 0.9 collective-permute-start.8
  106.9 1.8 %collective-permute-done.8 = bf16[8,64]{1,0:T(8,128)(2,1)S(1)} collective-permute-done((bf16[8,64]{1,0:T(8,128)(2,1)S(1)}, bf16[8,64]{1,0:T(8,128)(2,1)S(1)}, u32[]{:S(2)}, u32[]{:S(2)}) %collective-permute-start.8) | collective-permute-done | bytes 1056 | tf_op jit(solution)/shard_map/ppermute | solution.py:293
  108.7 7.7 %all-to-all-done.4.heard_ref = f32[128,1,128]{2,1,0:T(1,128)S(1)} async-done(((f32[128,1,128]{2,1,0:T(1,128)}), f32[128,1,128]{2,1,0:T(1,128)S(1)}, u32[]{:S(2)}, u32[]{:S(2)}) %all-to-all-start.4) | async-done | bytes 65568 | tf_op jit(solution)/shard_map/all_to_all | solution.py:30
  116.5 0.7 shard_map.128
  (44 shorter events, 4.7 us)
Async XLA Ops:
  0.6 75.3 %copy-start.2 = (s32[2,8]{1,0:T(2,128)S(1)}, s32[2,8]{1,0:T(2,128)}, u32[]{:S(2)}) copy-start(s32[2,8]{1,0:T(2,128)} %param.21) | copy-start | bytes 196
  0.6 4.4 %collective-permute-start = (bf16[2,8,64]{2,1,0:T(8,128)(2,1)}, bf16[2,8,64]{2,1,0:T(8,128)(2,1)S(1)}, u32[]{:S(2)}, u32[]{:S(2)}) collective-permute-start(bf16[2,8,64]{2,1,0:T(8,128)(2,1)} %param.11), channel_id=1, source_target_pairs={{0,1},{1,0},{2,3},{3,2},{4,5},{5,4},{6,7},{7,6},{8,9},{9,8},{10,11... | collective-permute-start | bytes 6152 | tf_op jit(solution)/shard_map/ppermute | solution.py:26
  6.1 27.4 %collective-permute-start.1 = (bf16[8,32,1024]{2,1,0:T(8,128)(2,1)}, bf16[8,32,1024]{2,1,0:T(8,128)(2,1)S(1)}, u32[]{:S(2)}, u32[]{:S(2)}) collective-permute-start(bf16[8,32,1024]{2,1,0:T(8,128)(2,1)} %param.14), channel_id=1, source_target_pairs={{0,1},{1,0},{2,3},{3,2},{4,5},{5,4},{6,7},{7,6},{8,9},{9,8},{10,11... | collective-permute-start | bytes 1572872 | tf_op jit(solution)/shard_map/ppermute | solution.py:26
  7.5 26.0 %collective-permute-start.2 = (bf16[8,32,1024]{2,1,0:T(8,128)(2,1)}, bf16[8,32,1024]{2,1,0:T(8,128)(2,1)S(1)}, u32[]{:S(2)}, u32[]{:S(2)}) collective-permute-start(bf16[8,32,1024]{2,1,0:T(8,128)(2,1)} %param.15), channel_id=1, source_target_pairs={{0,1},{1,0},{2,3},{3,2},{4,5},{5,4},{6,7},{7,6},{8,9},{9,8},{10,11... | collective-permute-start | bytes 1572872 | tf_op jit(solution)/shard_map/ppermute | solution.py:26
  8.4 13.7 %collective-permute-start.3 = (f32[64]{0:T(128)}, f32[64]{0:T(128)S(1)}, u32[]{:S(2)}, u32[]{:S(2)}) collective-permute-start(f32[64]{0:T(128)} %bitcast.23), channel_id=1, source_target_pairs={{0,1},{1,0},{2,3},{3,2},{4,5},{5,4},{6,7},{7,6},{8,9},{9,8},{10,11... | collective-permute-start | bytes 776 | tf_op jit(solution)/shard_map/ppermute | solution.py:26
  9.6 23.8 %all-to-all-start = ((bf16[64,4,128]{2,1,0:T(4,128)(2,1)}), bf16[64,4,128]{2,1,0:T(4,128)(2,1)S(1)}, u32[]{:S(2)}, u32[]{:S(2)}) async-start(bf16[64,4,128]{2,1,0:T(4,128)(2,1)} %broadcast_in_dim.7), calls=%async_computation | async-start | bytes 131072 | tf_op jit(solution)/shard_map/all_to_all | solution.py:30
  34.7 18.4 %collective-permute-start.4 = (bf16[64,8192]{1,0:T(8,128)(2,1)}, bf16[64,8192]{1,0:T(8,128)(2,1)S(1)}, u32[]{:S(2)}, u32[]{:S(2)}) collective-permute-start(bf16[64,8192]{1,0:T(8,128)(2,1)} %bitcast.19), channel_id=1, source_target_pairs={{0,1},{1,0},{2,3},{3,2},{4,5},{5,4},{6,7},{7,6},{8,9},{9,8},{10,11... | collective-permute-start | bytes 3145736 | tf_op jit(solution)/shard_map/ppermute | solution.py:26
  36.0 17.0 %all-to-all-start.1 = ((bf16[64,8,128]{2,1,0:T(8,128)(2,1)}), bf16[64,8,128]{2,1,0:T(8,128)(2,1)S(1)}, u32[]{:S(2)}, u32[]{:S(2)}) async-start(bf16[64,8,128]{2,1,0:T(8,128)(2,1)} %shard_map.122), calls=%async_computation.1 | async-start | bytes 262144 | tf_op jit(solution)/shard_map/all_to_all | solution.py:30
  41.5 18.1 %collective-permute-start.5 = (bf16[2,8,64]{2,1,0:T(8,128)(2,1)}, bf16[2,8,64]{2,1,0:T(8,128)(2,1)S(1)}, u32[]{:S(2)}, u32[]{:S(2)}) collective-permute-start(bf16[2,8,64]{2,1,0:T(8,128)(2,1)} %param.20), channel_id=1, source_target_pairs={{0,1},{1,0},{2,3},{3,2},{4,5},{5,4},{6,7},{7,6},{8,9},{9,8},{10,11... | collective-permute-start | bytes 6152 | tf_op jit(solution)/shard_map/ppermute | solution.py:26
  42.3 1.2 %copy-start.1 = (bf16[1,64,8192]{2,1,0:T(8,128)(2,1)S(1)}, bf16[1,64,8192]{2,1,0:T(8,128)(2,1)}, u32[]{:S(2)}) copy-start(bf16[1,64,8192]{2,1,0:T(8,128)(2,1)} %param.17) | copy-start | bytes 3145732
  55.0 15.6 %all-to-all-start.2 = ((bf16[64,4,128]{2,1,0:T(4,128)(2,1)}), bf16[64,4,128]{2,1,0:T(4,128)(2,1)S(1)}, u32[]{:S(2)}, u32[]{:S(2)}) async-start(bf16[64,4,128]{2,1,0:T(4,128)(2,1)} %shard_map.124), calls=%async_computation.2 | async-start | bytes 131072 | tf_op jit(solution)/shard_map/all_to_all | solution.py:30
  71.3 15.6 %all-to-all-start.3 = ((bf16[64,4,128]{2,1,0:T(4,128)(2,1)}), bf16[64,4,128]{2,1,0:T(4,128)(2,1)S(1)}, u32[]{:S(2)}, u32[]{:S(2)}) async-start(bf16[64,4,128]{2,1,0:T(4,128)(2,1)} %shard_map.125), calls=%async_computation.3 | async-start | bytes 131072 | tf_op jit(solution)/shard_map/all_to_all | solution.py:30
  87.0 4.4 %collective-permute-start.6 = (bf16[64,4,128]{2,1,0:T(4,128)(2,1)S(1)}, bf16[64,4,128]{2,1,0:T(4,128)(2,1)S(1)}, u32[]{:S(2)}, u32[]{:S(2)}) collective-permute-start(bf16[64,4,128]{2,1,0:T(4,128)(2,1)S(1)} %all-to-all-done.3), channel_id=1, source_target_pairs={{0,1},{1,0},{2,3},{3,2},{4,5},{5,4},{6,7},{7,6},{8,9},{9,8},{10,11... | collective-permute-start | bytes 196616 | tf_op jit(solution)/shard_map/ppermute | solution.py:26
  91.8 3.3 %copy-start = (bf16[8192,501]{0,1:T(8,128)(2,1)S(1)}, bf16[8192,501]{0,1:T(8,128)(2,1)}, u32[]{:S(2)}) copy-start(bf16[8192,501]{0,1:T(8,128)(2,1)} %param.19) | copy-start | bytes 24625156
  97.5 1.4 %collective-permute-start.7 = (f32[8,128]{1,0:T(8,128)S(1)}, f32[8,128]{1,0:T(8,128)S(1)}, u32[]{:S(2)}, u32[]{:S(2)}) collective-permute-start(f32[8,128]{1,0:T(8,128)S(1)} %shard_map.126.near_ref), channel_id=1, source_target_pairs={{0,1},{1,0},{2,3},{3,2},{4,5},{5,4},{6,7},{7,6},{8,9},{9,8},{10,11... | collective-permute-start | bytes 12296 | tf_op jit(solution)/shard_map/ppermute | solution.py:26
  99.7 16.7 %all-to-all-start.4 = ((f32[128,1,128]{2,1,0:T(1,128)}), f32[128,1,128]{2,1,0:T(1,128)S(1)}, u32[]{:S(2)}, u32[]{:S(2)}) async-start(f32[128,1,128]{2,1,0:T(1,128)} %shard_map.127), calls=%async_computation.4 | async-start | bytes 131072 | tf_op jit(solution)/shard_map/all_to_all | solution.py:30
  106.0 2.8 %collective-permute-start.8 = (bf16[8,64]{1,0:T(8,128)(2,1)S(1)}, bf16[8,64]{1,0:T(8,128)(2,1)S(1)}, u32[]{:S(2)}, u32[]{:S(2)}) collective-permute-start(bf16[8,64]{1,0:T(8,128)(2,1)S(1)} %slice_select_fusion), channel_id=1, source_target_pairs={{0,128},{128,0},{1,129},{129,1},{2,130},{130,2},{3,131},{131,3},{4... | collective-permute-start | bytes 3080 | tf_op jit(solution)/shard_map/ppermute | solution.py:293

commit v6 on v5

--- a/solution.py
+++ b/solution.py
@@ -116,7 +116,7 @@
         out_ref[2 * t + 1] = odd[t]
 
 
-def merge_kernel(at_ref, got_ref, q_ref, fk_ref, fv_ref, w_ref, far_ref, out_ref):
+def merge_kernel(at_ref, got_ref, q_ref, fk_ref, fv_ref, near_ref, far_ref):
     x = got_ref[...].astype(F32)
     stats = pltpu.roll(x, HALF, 1)
     tops = stats[:, :, 0:1]
@@ -136,13 +136,9 @@
     row = lax.broadcasted_iota(jnp.int32, (8, 128), 0)
     attended = jnp.where(row < HALF, above / below, 0.0)
     turned = pltpu.roll(attended, 64, 1)
-    turned = jnp.where(at_ref[1] == 0, attended, turned).astype(BF)
-    wide = 1024
-    for n in range(0, D, wide):
-        w = jnp.concatenate([w_ref[:, n : n + wide], far_ref[:, n : n + wide]], 0)
-        share = jnp.dot(turned, w, preferred_element_type=F32)
-        for i in range(wide // 128):
-            out_ref[n // 128 + i] = share[:HALF, i * 128 : (i + 1) * 128].astype(BF)
+    first = at_ref[1] == 0
+    near_ref[...] = jnp.where(first, attended, turned)[:HALF, :64].astype(BF)
+    far_ref[...] = jnp.where(first, turned, attended)[:HALF, :64].astype(BF)
 
 
 def state_kernel(got_ref, resid_ref, out_ref):
@@ -171,7 +167,8 @@
     out_ref[...] = jnp.broadcast_to(x[None], out_ref.shape)
 
 
-def final_kernel(start_ref, heard_ref, out_ref):
+def final_kernel(start_ref, heard_ref, normed_ref, out_ref, normed_out):
+    normed_out[...] = normed_ref[...][None]
     x = heard_ref[pl.ds(start_ref[0], CHIPS)]
     high = jnp.max(x, 0, keepdims=True)
     total = jnp.sum(pltpu.roll(x, 120, 2) * jnp.exp(x - high), 0)
@@ -211,11 +208,13 @@
     spot = jnp.stack([step, core])
     q_half = chip_rows(queries, swap(queries))
     q_chip = jnp.pad(q_half.astype(F32), ((0, HALF), (0, 0)))
-    q = exchange(jnp.broadcast_to(q_half[None], (CHIPS, *q_half.shape)), CHIP)
-    q = q.reshape(CHIPS * HALF, HEAD_SIZE)
+    sent = lax.optimization_barrier(
+        jnp.broadcast_to(q_half[None], (CHIPS, *q_half.shape))
+    )
+    q = exchange(sent, CHIP).reshape(CHIPS * HALF, HEAD_SIZE)
 
     keys, values, gain, lengths, _ = lax.optimization_barrier(
-        (stored_key_cache, stored_value_cache, gain_sides[0], lengths, q_half)
+        (stored_key_cache, stored_value_cache, gain_sides[0], lengths, sent)
     )
     keys_far, values_far = swap(keys), swap(values)
     keys, values = rows_of(keys, row0), rows_of(values, row0)
@@ -245,8 +244,8 @@
         pack,
     )
     got = exchange(sent, CHIP)
-    w_side, resid, new_keys, new_values, _ = lax.optimization_barrier(
-        (wo_sides[0], resid, step_token_keys, step_token_values, sent)
+    w_side, resid, actions, new_keys, new_values, _ = lax.optimization_barrier(
+        (wo_sides[0], resid, actions, step_token_keys, step_token_values, sent)
     )
     w_far = swap(w_side)
     w_mine = call(load_kernel, jax.ShapeDtypeStruct(w_side.shape, BF), [VMEM], 8, 1 << 20, w_side)
@@ -258,20 +257,25 @@
         x = lax.dynamic_slice(x, (0, row0, kv * HEAD_SIZE), (2, HALF, HEAD_SIZE))
         return jnp.pad(x.astype(F32), ((0, 0), (0, HALF), (0, 0)))
 
-    share = call(
+    part = jax.ShapeDtypeStruct((HALF, 64), BF)
+    near, far = call(
         merge_kernel,
-        jax.ShapeDtypeStruct((CHIPS, HALF, HEAD_SIZE), BF),
-        [SMEM] + [VMEM] * 6,
+        (part, part),
+        [SMEM] + [VMEM] * 4,
         16,
-        2 * 8 * HEAD_SIZE * D,
+        CHIPS * 8 * HEAD_SIZE * 8,
         jnp.stack([step, core]),
         got,
         q_chip,
         fresh(new_keys),
         fresh(new_values),
-        w_mine,
-        w_far,
-    )
+    )
+    share = jnp.dot(near, w_mine, preferred_element_type=F32)
+    share = share + jnp.dot(far, w_far, preferred_element_type=F32)
+    share = share.astype(BF).reshape(HALF, CHIPS, HEAD_SIZE).transpose(1, 0, 2)
+    action = lax.dynamic_index_in_dim(actions, step, 0, keepdims=True)
+    action = action - place * head.shape[1]
+    share, gains, r_chip, action = lax.optimization_barrier((share, gains, r_chip, action))
     shares = exchange(share, CHIP)
     sent = call(
         state_kernel,
@@ -283,6 +287,8 @@
         r_chip,
     )
     mine = exchange(sent, CHIP)
+    head_t, _ = lax.optimization_barrier((head.T, mine))
+    head_t = call(load_kernel, jax.ShapeDtypeStruct(head_t.shape, BF), [VMEM], 24, 1 << 24, head_t)
     whole = by_core(core, mine, swap(mine), 1).astype(F32)
     square = jnp.sum(jnp.sum(whole * whole, 0), -1, keepdims=True)
     inverse = lax.rsqrt(square / D + 1e-05)
@@ -292,7 +298,6 @@
     to_side = [(0, 1), (1, 0)]
     peer_normed = lax.ppermute(own, "role", to_side)
     width = head.shape[1]
-    action = lax.dynamic_index_in_dim(actions, step, 0, keepdims=True)
     local = call(
         head_kernel,
         jax.ShapeDtypeStruct((8, 128), F32),
@@ -300,8 +305,8 @@
         24,
         2 * 8 * D * width,
         normed,
-        head.T,
-        action - place * width,
+        head_t,
+        action,
     )
     packed = call(
         pack_kernel,
@@ -313,16 +318,19 @@
         swap(local),
     )
     heard = exchange(packed, ("role",) + CHIP)
-    prob = call(
+    return call(
         final_kernel,
-        jax.ShapeDtypeStruct((1, 8), F32),
-        [SMEM, VMEM],
+        (
+            jax.ShapeDtypeStruct((1, 8), F32),
+            jax.ShapeDtypeStruct((1, *peer_normed.shape), BF),
+        ),
+        [SMEM, VMEM, VMEM],
         4,
         1 << 16,
         ((1 - side) * CHIPS)[None],
         heard,
-    )
-    return prob, peer_normed[None]
+        peer_normed,
+    )
 
 
 def solution(mesh):

time: 118 us -> 113 us (0.958)
  blocking collectives: 0 us -> 30.7 us
  waiting for transfers between devices: 52.9 us -> 24.4 us
  starting transfers between devices: 43.3 us -> 36 us
    all_to_all x0 -> x2, blocking collectives: none -> 30.7 us  [exchange(): return lax.all_to_all(x, axes, split_axis=0, concat_axis=0, tiled=True)]
    all_to_all x5 -> x3, waiting for transfers between devices: 49.4 us -> 20.4 us  [exchange(): return lax.all_to_all(x, axes, split_axis=0, concat_axis=0, tiled=True)]
    all_to_all x5 -> x3, starting transfers between devices: 32.6 us -> 24.7 us  [exchange(): return lax.all_to_all(x, axes, split_axis=0, concat_axis=0, tiled=True)]
    pallas_call x7 -> x8, Pallas kernels: 7.82 us -> 6.7 us  [call(): pl.pallas_call(kernel, out_shape=shapes, in_specs=specs, out_specs=jax.tr...]
    unnamed x7 -> x4, local copies, waits for them, and re-layouts: 5.15 us -> 4.57 us
  transfers between devices with their start and end apart: 14 -> 12, of which waited for: 9 -> 7; matrix products, arithmetic and copies ran while one was open for 5% -> 7% of each run, Pallas kernels for 2% -> 1%
where the time goes in v6:
time: 113 us; the launch traced here: 112 us
  starting transfers between devices  36 us (32%)
  blocking collectives  30.7 us (27%)
  waiting for transfers between devices  24.4 us (22%)
  local copies, waits for them, and re-layouts  10.3 us (9%)
  Pallas kernels  6.7 us (6%)
  other arithmetic  2.66 us (2%)
    all_to_all x2, blocking collectives, exchange(): return lax.all_to_all(x, axes, split_axis=0, concat_axis=0, tiled=True)  30.7 us
    all_to_all x3, starting transfers between devices, exchange(): return lax.all_to_all(x, axes, split_axis=0, concat_axis=0, tiled=True)  24.7 us
    all_to_all x3, waiting for transfers between devices, exchange(): return lax.all_to_all(x, axes, split_axis=0, concat_axis=0, tiled=True)  20.4 us
    ppermute x8, starting transfers between devices, swap(): return lax.ppermute(x, CORE, [(0, 1), (1, 0)])  10.4 us
    pallas_call x8, Pallas kernels, call(): pl.pallas_call(kernel, out_shape=shapes, in_specs=specs, out_specs=jax.tr...  6.7 us
    unnamed x4, local copies, waits for them, and re-layouts  4.57 us
    dynamic_slice x5, local copies, waits for them, and re-layouts, rows_of(): return lax.dynamic_slice_in_dim(x, start, HALF, axis)  3.37 us
  transfers between devices with their start and end apart: 12, of which 7 were waited for; matrix products, arithmetic and copies ran while one was open for 7% of the time, Pallas kernels for 1%

profile of v6, /device:TPU:1, one launch (start us, length us, event | category | flops | bytes accessed | tf_op | source)
XLA Modules:
  0.0 112.0 jit_solution(7906444222597803770)
XLA Ops:
  0.6 3.3 %collective-permute-start = (bf16[2,8,64]{2,1,0:T(8,128)(2,1)}, bf16[2,8,64]{2,1,0:T(8,128)(2,1)S(1)}, u32[]{:S(2)}, u32[]{:S(2)}) collective-permute-start(bf16[2,8,64]{2,1,0:T(8,128)(2,1)} %param.11), channel_id=1, source_target_pairs={{0,1},{1,0},{2,3},{3,2},{4,5},{5,4},{6,7},{7,6},{8,9},{9,8},{10,11... | collective-permute-start | bytes 6152 | tf_op jit(solution)/shard_map/ppermute | solution.py:26
  4.0 0.7 fusion.6
  5.1 0.6 broadcast_in_dim.5
  5.7 12.6 %all-to-all-start = ((bf16[64,4,128]{2,1,0:T(4,128)(2,1)}), bf16[64,4,128]{2,1,0:T(4,128)(2,1)S(1)}, u32[]{:S(2)}, u32[]{:S(2)}) async-start(bf16[64,4,128]{2,1,0:T(4,128)(2,1)} %broadcast_in_dim.5), calls=%async_computation | async-start | bytes 131072 | tf_op jit(solution)/shard_map/all_to_all | solution.py:30
  18.3 1.0 constant_dynamic-slice_fusion.7.k_ref
  19.3 0.7 collective-permute-start.1
  20.0 1.0 constant_dynamic-slice_fusion.6.v_ref
  21.0 0.7 dynamic_slice.48
  22.4 0.8 collective-permute-done.3
  23.2 0.8 broadcast_select_fusion
  24.2 5.2 %all-to-all-done = bf16[64,4,128]{2,1,0:T(4,128)(2,1)S(1)} async-done(((bf16[64,4,128]{2,1,0:T(4,128)(2,1)}), bf16[64,4,128]{2,1,0:T(4,128)(2,1)S(1)}, u32[]{:S(2)}, u32[]{:S(2)}) %all-to-all-start) | async-done | bytes 65568 | tf_op jit(solution)/shard_map/all_to_all | solution.py:30
  29.4 1.2 %shard_map.122 = bf16[64,8,128]{2,1,0:T(8,128)(2,1)} custom-call(s32[1]{0:T(128)} %bitcast.2.core_ref, bf16[256,128]{1,0:T(8,128)(2,1)S(1)} %bitcast.28, bf16[4,32,1024]{2,1,0:T(8,128)(2,1)S(1)} %constant_dynamic-slice_fusion.7.k_ref, bf16[4,32,1024]{2,1,0:T(8,128)(2,1)S(1)} %constant_dynamic-slice_fusion.6.v_ref, ...), custom_call_target="tpu_custom_call" | custom-call | flops 33554432 | bytes 2097152 | tf_op jit(solution)/shard_map/pallas_call | solution.py:49
  30.6 1.7 %collective-permute-start.4 = (bf16[64,8192]{1,0:T(8,128)(2,1)}, bf16[64,8192]{1,0:T(8,128)(2,1)S(1)}, u32[]{:S(2)}, u32[]{:S(2)}) collective-permute-start(bf16[64,8192]{1,0:T(8,128)(2,1)} %bitcast.26), channel_id=1, source_target_pairs={{0,1},{1,0},{2,3},{3,2},{4,5},{5,4},{6,7},{7,6},{8,9},{9,8},{10,11... | collective-permute-start | bytes 3145736 | tf_op jit(solution)/shard_map/ppermute | solution.py:26
  32.3 6.0 %all-to-all-start.1 = ((bf16[64,8,128]{2,1,0:T(8,128)(2,1)}), bf16[64,8,128]{2,1,0:T(8,128)(2,1)S(1)}, u32[]{:S(2)}, u32[]{:S(2)}) async-start(bf16[64,8,128]{2,1,0:T(8,128)(2,1)} %shard_map.122), calls=%async_computation.1 | async-start | bytes 262144 | tf_op jit(solution)/shard_map/all_to_all | solution.py:30
  38.8 0.7 fusion.8
  39.5 0.8 constant_dynamic-slice_fusion.4
  40.3 0.7 fusion.11.action_ref
  41.0 1.2 %copy-done.1 = bf16[1,64,8192]{2,1,0:T(8,128)(2,1)S(1)} copy-done((bf16[1,64,8192]{2,1,0:T(8,128)(2,1)S(1)}, bf16[1,64,8192]{2,1,0:T(8,128)(2,1)}, u32[]{:S(2)}) %copy-start.1) | copy-done | bytes 1048600
  42.4 7.4 %all-to-all-done.1.got_ref = bf16[64,8,128]{2,1,0:T(8,128)(2,1)S(1)} async-done(((bf16[64,8,128]{2,1,0:T(8,128)(2,1)}), bf16[64,8,128]{2,1,0:T(8,128)(2,1)S(1)}, u32[]{:S(2)}, u32[]{:S(2)}) %all-to-all-start.1) | async-done | bytes 131104 | tf_op jit(solution)/shard_map/all_to_all | solution.py:30
  50.2 1.0 shard_map.123
  51.7 15.9 %all_to_all.25.got_ref = bf16[64,4,128]{2,1,0:T(4,128)(2,1)S(1)} all-to-all(bf16[64,4,128]{2,1,0:T(4,128)(2,1)S(1)} %fusion.1), channel_id=1, replica_groups=mesh['role'=2,'grp'=2,'tp_0'=4,'tp_1'=8,'tp_2'=2] {'grp','tp_0','tp_1'}, dimensions={0} | all-to-all | bytes 131072 | tf_op jit(solution)/shard_map/all_to_all | solution.py:30
  67.7 14.8 %all_to_all.26 = bf16[64,4,128]{2,1,0:T(4,128)(2,1)S(1)} all-to-all(bf16[64,4,128]{2,1,0:T(4,128)(2,1)S(1)} %shard_map.125), channel_id=1, replica_groups=mesh['role'=2,'grp'=2,'tp_0'=4,'tp_1'=8,'tp_2'=2] {'grp','tp_0','tp_1'}, dimensions={0} | all-to-all | bytes 131072 | tf_op jit(solution)/shard_map/all_to_all | solution.py:30
  82.5 3.4 %collective-permute-start.6 = (bf16[64,4,128]{2,1,0:T(4,128)(2,1)S(1)}, bf16[64,4,128]{2,1,0:T(4,128)(2,1)S(1)}, u32[]{:S(2)}, u32[]{:S(2)}) collective-permute-start(bf16[64,4,128]{2,1,0:T(4,128)(2,1)S(1)} %all_to_all.26), channel_id=1, source_target_pairs={{0,1},{1,0},{2,3},{3,2},{4,5},{5,4},{6,7},{7,6},{8,9},{9,8},{10,11... | collective-permute-start | bytes 196616 | tf_op jit(solution)/shard_map/ppermute | solution.py:26
  85.8 3.3 %copy-done = bf16[8192,501]{0,1:T(8,128)(2,1)S(1)} copy-done((bf16[8192,501]{0,1:T(8,128)(2,1)S(1)}, bf16[8192,501]{0,1:T(8,128)(2,1)}, u32[]{:S(2)}) %copy-start) | copy-done | bytes 8208408
  90.2 2.4 %shard_map.127.near_ref = f32[8,128]{1,0:T(8,128)S(1)} custom-call(bf16[64,8,128]{2,1,0:T(8,128)(2,1)S(1)} %fusion.4.u_ref, bf16[501,8192]{1,0:T(8,128)(2,1)S(1)} %shard_map.126.head_ref, s32[1,8]{1,0:T(1,128)S(1)} %fusion.11.action_ref), custom_call_target="tpu_custom_call" | custom-call | flops 65667072 | bytes 4104192 | tf_op jit(solution)/shard_map/pallas_call | solution.py:49
  92.7 1.1 %collective-permute-done.7.far_ref = f32[8,128]{1,0:T(8,128)S(1)} collective-permute-done((f32[8,128]{1,0:T(8,128)S(1)}, f32[8,128]{1,0:T(8,128)S(1)}, u32[]{:S(2)}, u32[]{:S(2)}) %collective-permute-start.7) | collective-permute-done | bytes 4128 | tf_op jit(solution)/shard_map/ppermute | solution.py:26
  93.8 0.7 shard_map.128
  94.5 6.1 %all-to-all-start.4 = ((f32[128,1,128]{2,1,0:T(1,128)}), f32[128,1,128]{2,1,0:T(1,128)S(1)}, u32[]{:S(2)}, u32[]{:S(2)}) async-start(f32[128,1,128]{2,1,0:T(1,128)} %shard_map.128), calls=%async_computation.4 | async-start | bytes 131072 | tf_op jit(solution)/shard_map/all_to_all | solution.py:30
  100.7 0.9 collective-permute-start.8
  101.7 1.8 %collective-permute-done.8.normed_ref = bf16[8,64]{1,0:T(8,128)(2,1)S(1)} collective-permute-done((bf16[8,64]{1,0:T(8,128)(2,1)S(1)}, bf16[8,64]{1,0:T(8,128)(2,1)S(1)}, u32[]{:S(2)}, u32[]{:S(2)}) %collective-permute-start.8) | collective-permute-done | bytes 1056 | tf_op jit(solution)/shard_map/ppermute | solution.py:299
  103.5 7.8 %all-to-all-done.4.heard_ref = f32[128,1,128]{2,1,0:T(1,128)S(1)} async-done(((f32[128,1,128]{2,1,0:T(1,128)}), f32[128,1,128]{2,1,0:T(1,128)S(1)}, u32[]{:S(2)}, u32[]{:S(2)}) %all-to-all-start.4) | async-done | bytes 65568 | tf_op jit(solution)/shard_map/all_to_all | solution.py:30
  111.3 0.7 shard_map.129
  (42 shorter events, 4.2 us)
Async XLA Ops:
  0.6 4.4 %collective-permute-start = (bf16[2,8,64]{2,1,0:T(8,128)(2,1)}, bf16[2,8,64]{2,1,0:T(8,128)(2,1)S(1)}, u32[]{:S(2)}, u32[]{:S(2)}) collective-permute-start(bf16[2,8,64]{2,1,0:T(8,128)(2,1)} %param.11), channel_id=1, source_target_pairs={{0,1},{1,0},{2,3},{3,2},{4,5},{5,4},{6,7},{7,6},{8,9},{9,8},{10,11... | collective-permute-start | bytes 6152 | tf_op jit(solution)/shard_map/ppermute | solution.py:26
  5.7 23.7 %all-to-all-start = ((bf16[64,4,128]{2,1,0:T(4,128)(2,1)}), bf16[64,4,128]{2,1,0:T(4,128)(2,1)S(1)}, u32[]{:S(2)}, u32[]{:S(2)}) async-start(bf16[64,4,128]{2,1,0:T(4,128)(2,1)} %broadcast_in_dim.5), calls=%async_computation | async-start | bytes 131072 | tf_op jit(solution)/shard_map/all_to_all | solution.py:30
  19.3 10.1 %collective-permute-start.1 = (bf16[8,32,1024]{2,1,0:T(8,128)(2,1)}, bf16[8,32,1024]{2,1,0:T(8,128)(2,1)S(1)}, u32[]{:S(2)}, u32[]{:S(2)}) collective-permute-start(bf16[8,32,1024]{2,1,0:T(8,128)(2,1)} %param.14), channel_id=1, source_target_pairs={{0,1},{1,0},{2,3},{3,2},{4,5},{5,4},{6,7},{7,6},{8,9},{9,8},{10,11... | collective-permute-start | bytes 1572872 | tf_op jit(solution)/shard_map/ppermute | solution.py:26
  20.9 8.4 %collective-permute-start.2 = (bf16[8,32,1024]{2,1,0:T(8,128)(2,1)}, bf16[8,32,1024]{2,1,0:T(8,128)(2,1)S(1)}, u32[]{:S(2)}, u32[]{:S(2)}) collective-permute-start(bf16[8,32,1024]{2,1,0:T(8,128)(2,1)} %param.15), channel_id=1, source_target_pairs={{0,1},{1,0},{2,3},{3,2},{4,5},{5,4},{6,7},{7,6},{8,9},{9,8},{10,11... | collective-permute-start | bytes 1572872 | tf_op jit(solution)/shard_map/ppermute | solution.py:26
  21.8 1.4 %collective-permute-start.3 = (f32[64]{0:T(128)}, f32[64]{0:T(128)S(1)}, u32[]{:S(2)}, u32[]{:S(2)}) collective-permute-start(f32[64]{0:T(128)} %bitcast.29), channel_id=1, source_target_pairs={{0,1},{1,0},{2,3},{3,2},{4,5},{5,4},{6,7},{7,6},{8,9},{9,8},{10,11... | collective-permute-start | bytes 776 | tf_op jit(solution)/shard_map/ppermute | solution.py:26
  30.6 20.6 %collective-permute-start.4 = (bf16[64,8192]{1,0:T(8,128)(2,1)}, bf16[64,8192]{1,0:T(8,128)(2,1)S(1)}, u32[]{:S(2)}, u32[]{:S(2)}) collective-permute-start(bf16[64,8192]{1,0:T(8,128)(2,1)} %bitcast.26), channel_id=1, source_target_pairs={{0,1},{1,0},{2,3},{3,2},{4,5},{5,4},{6,7},{7,6},{8,9},{9,8},{10,11... | collective-permute-start | bytes 3145736 | tf_op jit(solution)/shard_map/ppermute | solution.py:26
  32.3 17.6 %all-to-all-start.1 = ((bf16[64,8,128]{2,1,0:T(8,128)(2,1)}), bf16[64,8,128]{2,1,0:T(8,128)(2,1)S(1)}, u32[]{:S(2)}, u32[]{:S(2)}) async-start(bf16[64,8,128]{2,1,0:T(8,128)(2,1)} %shard_map.122), calls=%async_computation.1 | async-start | bytes 262144 | tf_op jit(solution)/shard_map/all_to_all | solution.py:30
  38.3 4.0 %collective-permute-start.5 = (bf16[2,8,64]{2,1,0:T(8,128)(2,1)}, bf16[2,8,64]{2,1,0:T(8,128)(2,1)S(1)}, u32[]{:S(2)}, u32[]{:S(2)}) collective-permute-start(bf16[2,8,64]{2,1,0:T(8,128)(2,1)} %param.20), channel_id=1, source_target_pairs={{0,1},{1,0},{2,3},{3,2},{4,5},{5,4},{6,7},{7,6},{8,9},{9,8},{10,11... | collective-permute-start | bytes 6152 | tf_op jit(solution)/shard_map/ppermute | solution.py:26
  41.0 1.2 %copy-start.1 = (bf16[1,64,8192]{2,1,0:T(8,128)(2,1)S(1)}, bf16[1,64,8192]{2,1,0:T(8,128)(2,1)}, u32[]{:S(2)}) copy-start(bf16[1,64,8192]{2,1,0:T(8,128)(2,1)} %param.17) | copy-start | bytes 3145732
  82.5 7.3 %collective-permute-start.6 = (bf16[64,4,128]{2,1,0:T(4,128)(2,1)S(1)}, bf16[64,4,128]{2,1,0:T(4,128)(2,1)S(1)}, u32[]{:S(2)}, u32[]{:S(2)}) collective-permute-start(bf16[64,4,128]{2,1,0:T(4,128)(2,1)S(1)} %all_to_all.26), channel_id=1, source_target_pairs={{0,1},{1,0},{2,3},{3,2},{4,5},{5,4},{6,7},{7,6},{8,9},{9,8},{10,11... | collective-permute-start | bytes 196616 | tf_op jit(solution)/shard_map/ppermute | solution.py:26
  85.8 3.3 %copy-start = (bf16[8192,501]{0,1:T(8,128)(2,1)S(1)}, bf16[8192,501]{0,1:T(8,128)(2,1)}, u32[]{:S(2)}) copy-start(bf16[8192,501]{0,1:T(8,128)(2,1)} %param.19) | copy-start | bytes 24625156
  92.5 1.3 %collective-permute-start.7 = (f32[8,128]{1,0:T(8,128)S(1)}, f32[8,128]{1,0:T(8,128)S(1)}, u32[]{:S(2)}, u32[]{:S(2)}) collective-permute-start(f32[8,128]{1,0:T(8,128)S(1)} %shard_map.127.near_ref), channel_id=1, source_target_pairs={{0,1},{1,0},{2,3},{3,2},{4,5},{5,4},{6,7},{7,6},{8,9},{9,8},{10,11... | collective-permute-start | bytes 12296 | tf_op jit(solution)/shard_map/ppermute | solution.py:26
  94.5 16.8 %all-to-all-start.4 = ((f32[128,1,128]{2,1,0:T(1,128)}), f32[128,1,128]{2,1,0:T(1,128)S(1)}, u32[]{:S(2)}, u32[]{:S(2)}) async-start(f32[128,1,128]{2,1,0:T(1,128)} %shard_map.128), calls=%async_computation.4 | async-start | bytes 131072 | tf_op jit(solution)/shard_map/all_to_all | solution.py:30
  100.7 2.8 %collective-permute-start.8 = (bf16[8,64]{1,0:T(8,128)(2,1)S(1)}, bf16[8,64]{1,0:T(8,128)(2,1)S(1)}, u32[]{:S(2)}, u32[]{:S(2)}) collective-permute-start(bf16[8,64]{1,0:T(8,128)(2,1)S(1)} %slice_select_fusion), channel_id=1, source_target_pairs={{0,128},{128,0},{1,129},{129,1},{2,130},{130,2},{3,131},{131,3},{4... | collective-permute-start | bytes 3080 | tf_op jit(solution)/shard_map/ppermute | solution.py:299

commit v7 on v6

--- a/solution.py
+++ b/solution.py
@@ -60,6 +60,10 @@
 
 def load_kernel(x_ref, out_ref):
     out_ref[...] = x_ref[...]
+
+
+def touch_kernel(x_ref, out_ref):
+    out_ref[...] = x_ref[0:16, 0:128][0:8]
 
 
 def attend_kernel(core_ref, q_ref, k_ref, v_ref, kf_ref, vf_ref, ok_ref, pack_ref, out_ref):
@@ -146,7 +150,7 @@
     out_ref[...] = jnp.broadcast_to(state.astype(BF)[None], out_ref.shape)
 
 
-def head_kernel(u_ref, head_ref, action_ref, out_ref):
+def head_kernel(u_ref, head_ref, action_ref, touched_ref, out_ref):
     u = jnp.concatenate([u_ref[i] for i in range(CHIPS)], 1)
     logits = lax.dot_general(head_ref[...], u, NT, preferred_element_type=F32)
     ids = lax.broadcasted_iota(jnp.int32, logits.shape, 0)
@@ -213,19 +217,19 @@
     )
     q = exchange(sent, CHIP).reshape(CHIPS * HALF, HEAD_SIZE)
 
-    keys, values, gain, lengths, _ = lax.optimization_barrier(
-        (stored_key_cache, stored_value_cache, gain_sides[0], lengths, sent)
+    keys, values, gain, gain_far, _ = lax.optimization_barrier(
+        (stored_key_cache, stored_value_cache, gain_sides, swap(gain_sides), sent)
     )
     keys_far, values_far = swap(keys), swap(values)
     keys, values = rows_of(keys, row0), rows_of(values, row0)
-    gain_chip = by_core(core, gain, swap(gain), 0)
+    gain_chip = by_core(core, gain, gain_far, 0)
 
     lens = rows_of(lengths, row0)
     at = jnp.arange(slots, dtype=jnp.int32)
     position = jnp.concatenate([place * slots + at, (place + 1 - 2 * core) * slots + at])
     valid = (position[None, :] < lens[:, None]).astype(F32).reshape(1, 4 * 2 * slots)
     gain_hi = rounded(gain_chip)
-    pack = jnp.concatenate([gain_hi, gain_chip - gain_hi]).reshape(HALF, 64)
+    pack = jnp.concatenate([gain_hi, gain_chip - gain_hi])
     pack = jnp.concatenate([jnp.zeros_like(pack), pack], 1)
     pack = jnp.concatenate([pack, pack], 0)
     sent = call(
@@ -250,7 +254,6 @@
     w_far = swap(w_side)
     w_mine = call(load_kernel, jax.ShapeDtypeStruct(w_side.shape, BF), [VMEM], 8, 1 << 20, w_side)
     r_chip = chip_rows(resid, swap(resid)).astype(F32)
-    gains = got[:, HALF:, 64:].astype(F32).reshape(CHIPS, 2, HEAD_SIZE).sum(1)
     kv = chip // GROUP
 
     def fresh(x):
@@ -275,7 +278,7 @@
     share = share.astype(BF).reshape(HALF, CHIPS, HEAD_SIZE).transpose(1, 0, 2)
     action = lax.dynamic_index_in_dim(actions, step, 0, keepdims=True)
     action = action - place * head.shape[1]
-    share, gains, r_chip, action = lax.optimization_barrier((share, gains, r_chip, action))
+    share, r_chip, action = lax.optimization_barrier((share, r_chip, action))
     shares = exchange(share, CHIP)
     sent = call(
         state_kernel,
@@ -287,8 +290,9 @@
         r_chip,
     )
     mine = exchange(sent, CHIP)
-    head_t, _ = lax.optimization_barrier((head.T, mine))
-    head_t = call(load_kernel, jax.ShapeDtypeStruct(head_t.shape, BF), [VMEM], 24, 1 << 24, head_t)
+    head_t, got, _ = lax.optimization_barrier((head.T, got, mine))
+    touched = call(touch_kernel, jax.ShapeDtypeStruct((8, 128), BF), [VMEM], 24, 1 << 24, head_t)
+    gains = got[:, HALF:, 64:].astype(F32).reshape(CHIPS, 2, HEAD_SIZE).sum(1)
     whole = by_core(core, mine, swap(mine), 1).astype(F32)
     square = jnp.sum(jnp.sum(whole * whole, 0), -1, keepdims=True)
     inverse = lax.rsqrt(square / D + 1e-05)
@@ -301,12 +305,13 @@
     local = call(
         head_kernel,
         jax.ShapeDtypeStruct((8, 128), F32),
-        [VMEM] * 3,
+        [VMEM] * 4,
         24,
         2 * 8 * D * width,
         normed,
         head_t,
         action,
+        touched,
     )
     packed = call(
         pack_kernel,

time: 113 us -> 113 us (level)
  blocking collectives: 30.7 us -> 14.9 us
  waiting for transfers between devices: 24.4 us -> 37.8 us
  starting transfers between devices: 36 us -> 38.9 us
    all_to_all x2 -> x1, blocking collectives: 30.7 us -> 14.9 us  [exchange(): return lax.all_to_all(x, axes, split_axis=0, concat_axis=0, tiled=True)]
    all_to_all x3 -> x4, waiting for transfers between devices: 20.4 us -> 34.8 us  [exchange(): return lax.all_to_all(x, axes, split_axis=0, concat_axis=0, tiled=True)]
    all_to_all x3 -> x4, starting transfers between devices: 24.7 us -> 27.9 us  [exchange(): return lax.all_to_all(x, axes, split_axis=0, concat_axis=0, tiled=True)]
  transfers between devices with their start and end apart: 12 -> 13, of which waited for: 7 -> 6; matrix products, arithmetic and copies ran while one was open for 7% -> 7% of each run, Pallas kernels for 1% -> 1%
where the time goes in v7:
time: 113 us
  starting transfers between devices  38.9 us (34%)
  waiting for transfers between devices  37.8 us (33%)
  blocking collectives  14.9 us (13%)
  local copies, waits for them, and re-layouts  10.3 us (9%)
  Pallas kernels  6.79 us (6%)
  other arithmetic  2.58 us (2%)
    all_to_all x4, waiting for transfers between devices, exchange(): return lax.all_to_all(x, axes, split_axis=0, concat_axis=0, tiled=True)  34.8 us
    all_to_all x4, starting transfers between devices, exchange(): return lax.all_to_all(x, axes, split_axis=0, concat_axis=0, tiled=True)  27.9 us
    all_to_all x1, blocking collectives, exchange(): return lax.all_to_all(x, axes, split_axis=0, concat_axis=0, tiled=True)  14.9 us
    ppermute x8, starting transfers between devices, swap(): return lax.ppermute(x, CORE, [(0, 1), (1, 0)])  10.1 us
    pallas_call x8, Pallas kernels, call(): pl.pallas_call(kernel, out_shape=shapes, in_specs=specs, out_specs=jax.tr...  6.79 us
    unnamed x4, local copies, waits for them, and re-layouts  4.56 us
    dynamic_slice x5, local copies, waits for them, and re-layouts, rows_of(): return lax.dynamic_slice_in_dim(x, start, HALF, axis)  3.38 us
  transfers between devices with their start and end apart: 13, of which 6 were waited for; matrix products, arithmetic and copies ran while one was open for 7% of the time, Pallas kernels for 1%

profile of v7, /device:TPU:1, one launch (start us, length us, event | category | flops | bytes accessed | tf_op | source)
XLA Modules:
  0.0 112.5 jit_solution(10371439711198227172)
XLA Ops:
  0.6 3.3 %collective-permute-start = (bf16[2,8,64]{2,1,0:T(8,128)(2,1)}, bf16[2,8,64]{2,1,0:T(8,128)(2,1)S(1)}, u32[]{:S(2)}, u32[]{:S(2)}) collective-permute-start(bf16[2,8,64]{2,1,0:T(8,128)(2,1)} %param.11), channel_id=1, source_target_pairs={{0,1},{1,0},{2,3},{3,2},{4,5},{5,4},{6,7},{7,6},{8,9},{9,8},{10,11... | collective-permute-start | bytes 6152 | tf_op jit(solution)/shard_map/ppermute | solution.py:26
  4.1 0.7 dynamic_slice.48
  4.9 0.7 fusion.6
  6.4 12.6 %all-to-all-start = ((bf16[64,4,128]{2,1,0:T(4,128)(2,1)}), bf16[64,4,128]{2,1,0:T(4,128)(2,1)S(1)}, u32[]{:S(2)}, u32[]{:S(2)}) async-start(bf16[64,4,128]{2,1,0:T(4,128)(2,1)} %broadcast_in_dim.5), calls=%async_computation | async-start | bytes 131072 | tf_op jit(solution)/shard_map/all_to_all | solution.py:30
  19.0 0.8 collective-permute-start.2
  19.9 0.7 fusion.12
  20.7 1.0 constant_dynamic-slice_fusion.6.v_ref
  21.7 1.0 constant_dynamic-slice_fusion.7.k_ref
  22.7 7.3 %all-to-all-done = bf16[64,4,128]{2,1,0:T(4,128)(2,1)S(1)} async-done(((bf16[64,4,128]{2,1,0:T(4,128)(2,1)}), bf16[64,4,128]{2,1,0:T(4,128)(2,1)S(1)}, u32[]{:S(2)}, u32[]{:S(2)}) %all-to-all-start) | async-done | bytes 65568 | tf_op jit(solution)/shard_map/all_to_all | solution.py:30
  30.0 1.2 %shard_map.122 = bf16[64,8,128]{2,1,0:T(8,128)(2,1)} custom-call(s32[1]{0:T(128)} %bitcast.2.core_ref, bf16[256,128]{1,0:T(8,128)(2,1)S(1)} %bitcast.28, bf16[4,32,1024]{2,1,0:T(8,128)(2,1)S(1)} %constant_dynamic-slice_fusion.7.k_ref, bf16[4,32,1024]{2,1,0:T(8,128)(2,1)S(1)} %constant_dynamic-slice_fusion.6.v_ref, ...), custom_call_target="tpu_custom_call" | custom-call | flops 33554432 | bytes 2097152 | tf_op jit(solution)/shard_map/pallas_call | solution.py:49
  31.2 1.8 %collective-permute-start.4 = (bf16[64,8192]{1,0:T(8,128)(2,1)}, bf16[64,8192]{1,0:T(8,128)(2,1)S(1)}, u32[]{:S(2)}, u32[]{:S(2)}) collective-permute-start(bf16[64,8192]{1,0:T(8,128)(2,1)} %bitcast.26), channel_id=1, source_target_pairs={{0,1},{1,0},{2,3},{3,2},{4,5},{5,4},{6,7},{7,6},{8,9},{9,8},{10,11... | collective-permute-start | bytes 3145736 | tf_op jit(solution)/shard_map/ppermute | solution.py:26
  33.1 4.6 %all-to-all-start.1 = ((bf16[64,8,128]{2,1,0:T(8,128)(2,1)}), bf16[64,8,128]{2,1,0:T(8,128)(2,1)S(1)}, u32[]{:S(2)}, u32[]{:S(2)}) async-start(bf16[64,8,128]{2,1,0:T(8,128)(2,1)} %shard_map.122), calls=%async_computation.1 | async-start | bytes 262144 | tf_op jit(solution)/shard_map/all_to_all | solution.py:30
  37.9 0.7 fusion.8
  38.5 0.8 constant_dynamic-slice_fusion.4
  39.3 0.7 fusion.11.action_ref
  40.0 1.2 %copy-done.1 = bf16[1,64,8192]{2,1,0:T(8,128)(2,1)S(1)} copy-done((bf16[1,64,8192]{2,1,0:T(8,128)(2,1)S(1)}, bf16[1,64,8192]{2,1,0:T(8,128)(2,1)}, u32[]{:S(2)}) %copy-start.1) | copy-done | bytes 1048600
  41.4 8.7 %all-to-all-done.1.got_ref = bf16[64,8,128]{2,1,0:T(8,128)(2,1)S(1)} async-done(((bf16[64,8,128]{2,1,0:T(8,128)(2,1)}), bf16[64,8,128]{2,1,0:T(8,128)(2,1)S(1)}, u32[]{:S(2)}, u32[]{:S(2)}) %all-to-all-start.1) | async-done | bytes 131104 | tf_op jit(solution)/shard_map/all_to_all | solution.py:30
  50.1 1.0 shard_map.123
  51.6 14.9 %all_to_all.25.got_ref = bf16[64,4,128]{2,1,0:T(4,128)(2,1)S(1)} all-to-all(bf16[64,4,128]{2,1,0:T(4,128)(2,1)S(1)} %fusion.1), channel_id=1, replica_groups=mesh['role'=2,'grp'=2,'tp_0'=4,'tp_1'=8,'tp_2'=2] {'grp','tp_0','tp_1'}, dimensions={0} | all-to-all | bytes 131072 | tf_op jit(solution)/shard_map/all_to_all | solution.py:30
  66.5 0.7 shard_map.125
  67.2 4.6 %all-to-all-start.3 = ((bf16[64,4,128]{2,1,0:T(4,128)(2,1)}), bf16[64,4,128]{2,1,0:T(4,128)(2,1)S(1)}, u32[]{:S(2)}, u32[]{:S(2)}) async-start(bf16[64,4,128]{2,1,0:T(4,128)(2,1)} %shard_map.125), calls=%async_computation.3 | async-start | bytes 131072 | tf_op jit(solution)/shard_map/all_to_all | solution.py:30
  71.8 11.0 %all-to-all-done.3 = bf16[64,4,128]{2,1,0:T(4,128)(2,1)S(1)} async-done(((bf16[64,4,128]{2,1,0:T(4,128)(2,1)}), bf16[64,4,128]{2,1,0:T(4,128)(2,1)S(1)}, u32[]{:S(2)}, u32[]{:S(2)}) %all-to-all-start.3) | async-done | bytes 65568 | tf_op jit(solution)/shard_map/all_to_all | solution.py:30
  82.8 3.6 %collective-permute-start.6 = (bf16[64,4,128]{2,1,0:T(4,128)(2,1)S(1)}, bf16[64,4,128]{2,1,0:T(4,128)(2,1)S(1)}, u32[]{:S(2)}, u32[]{:S(2)}) collective-permute-start(bf16[64,4,128]{2,1,0:T(4,128)(2,1)S(1)} %all-to-all-done.3), channel_id=1, source_target_pairs={{0,1},{1,0},{2,3},{3,2},{4,5},{5,4},{6,7},{7,6},{8,9},{9,8},{10,11... | collective-permute-start | bytes 196616 | tf_op jit(solution)/shard_map/ppermute | solution.py:26
  86.8 3.3 %copy-done = bf16[8192,501]{0,1:T(8,128)(2,1)S(1)} copy-done((bf16[8192,501]{0,1:T(8,128)(2,1)S(1)}, bf16[8192,501]{0,1:T(8,128)(2,1)}, u32[]{:S(2)}) %copy-start) | copy-done | bytes 8208408
  90.5 2.4 %shard_map.127.near_ref = f32[8,128]{1,0:T(8,128)S(1)} custom-call(bf16[64,8,128]{2,1,0:T(8,128)(2,1)S(1)} %fusion.4.u_ref, bf16[501,8192]{1,0:T(8,128)(2,1)S(1)} %bitcast.25, s32[1,8]{1,0:T(1,128)S(1)} %fusion.11.action_ref, bf16[8,128]{1,0:T(8,128)(2,1)S(1)} %shard_map.126.touched_ref), custom_call_target="tpu_custom_call" | custom-call | flops 65667072 | bytes 4104192 | tf_op jit(solution)/shard_map/pallas_call | solution.py:49
  93.2 1.1 %collective-permute-done.7.far_ref = f32[8,128]{1,0:T(8,128)S(1)} collective-permute-done((f32[8,128]{1,0:T(8,128)S(1)}, f32[8,128]{1,0:T(8,128)S(1)}, u32[]{:S(2)}, u32[]{:S(2)}) %collective-permute-start.7) | collective-permute-done | bytes 4128 | tf_op jit(solution)/shard_map/ppermute | solution.py:26
  94.3 0.7 shard_map.128
  95.1 6.1 %all-to-all-start.4 = ((f32[128,1,128]{2,1,0:T(1,128)}), f32[128,1,128]{2,1,0:T(1,128)S(1)}, u32[]{:S(2)}, u32[]{:S(2)}) async-start(f32[128,1,128]{2,1,0:T(1,128)} %shard_map.128), calls=%async_computation.4 | async-start | bytes 131072 | tf_op jit(solution)/shard_map/all_to_all | solution.py:30
  101.3 0.9 collective-permute-start.8
  102.2 1.8 %collective-permute-done.8.normed_ref = bf16[8,64]{1,0:T(8,128)(2,1)S(1)} collective-permute-done((bf16[8,64]{1,0:T(8,128)(2,1)S(1)}, bf16[8,64]{1,0:T(8,128)(2,1)S(1)}, u32[]{:S(2)}, u32[]{:S(2)}) %collective-permute-start.8) | collective-permute-done | bytes 1056 | tf_op jit(solution)/shard_map/ppermute | solution.py:303
  104.0 7.8 %all-to-all-done.4.heard_ref = f32[128,1,128]{2,1,0:T(1,128)S(1)} async-done(((f32[128,1,128]{2,1,0:T(1,128)}), f32[128,1,128]{2,1,0:T(1,128)S(1)}, u32[]{:S(2)}, u32[]{:S(2)}) %all-to-all-start.4) | async-done | bytes 65568 | tf_op jit(solution)/shard_map/all_to_all | solution.py:30
  111.8 0.7 shard_map.129
  (41 shorter events, 3.2 us)
Async XLA Ops:
  0.6 5.1 %collective-permute-start = (bf16[2,8,64]{2,1,0:T(8,128)(2,1)}, bf16[2,8,64]{2,1,0:T(8,128)(2,1)S(1)}, u32[]{:S(2)}, u32[]{:S(2)}) collective-permute-start(bf16[2,8,64]{2,1,0:T(8,128)(2,1)} %param.11), channel_id=1, source_target_pairs={{0,1},{1,0},{2,3},{3,2},{4,5},{5,4},{6,7},{7,6},{8,9},{9,8},{10,11... | collective-permute-start | bytes 6152 | tf_op jit(solution)/shard_map/ppermute | solution.py:26
  4.0 15.1 %collective-permute-start.1 = (f32[1,64]{1,0:T(1,128)}, f32[1,64]{1,0:T(1,128)S(1)}, u32[]{:S(2)}, u32[]{:S(2)}) collective-permute-start(f32[1,64]{1,0:T(1,128)} %param.18), channel_id=1, source_target_pairs={{0,1},{1,0},{2,3},{3,2},{4,5},{5,4},{6,7},{7,6},{8,9},{9,8},{10,11... | collective-permute-start | bytes 776 | tf_op jit(solution)/shard_map/ppermute | solution.py:26
  6.4 23.6 %all-to-all-start = ((bf16[64,4,128]{2,1,0:T(4,128)(2,1)}), bf16[64,4,128]{2,1,0:T(4,128)(2,1)S(1)}, u32[]{:S(2)}, u32[]{:S(2)}) async-start(bf16[64,4,128]{2,1,0:T(4,128)(2,1)} %broadcast_in_dim.5), calls=%async_computation | async-start | bytes 131072 | tf_op jit(solution)/shard_map/all_to_all | solution.py:30
  19.0 11.0 %collective-permute-start.2 = (bf16[8,32,1024]{2,1,0:T(8,128)(2,1)}, bf16[8,32,1024]{2,1,0:T(8,128)(2,1)S(1)}, u32[]{:S(2)}, u32[]{:S(2)}) collective-permute-start(bf16[8,32,1024]{2,1,0:T(8,128)(2,1)} %param.14), channel_id=1, source_target_pairs={{0,1},{1,0},{2,3},{3,2},{4,5},{5,4},{6,7},{7,6},{8,9},{9,8},{10,11... | collective-permute-start | bytes 1572872 | tf_op jit(solution)/shard_map/ppermute | solution.py:26
  19.8 10.2 %collective-permute-start.3 = (bf16[8,32,1024]{2,1,0:T(8,128)(2,1)}, bf16[8,32,1024]{2,1,0:T(8,128)(2,1)S(1)}, u32[]{:S(2)}, u32[]{:S(2)}) collective-permute-start(bf16[8,32,1024]{2,1,0:T(8,128)(2,1)} %param.15), channel_id=1, source_target_pairs={{0,1},{1,0},{2,3},{3,2},{4,5},{5,4},{6,7},{7,6},{8,9},{9,8},{10,11... | collective-permute-start | bytes 1572872 | tf_op jit(solution)/shard_map/ppermute | solution.py:26
  31.2 19.8 %collective-permute-start.4 = (bf16[64,8192]{1,0:T(8,128)(2,1)}, bf16[64,8192]{1,0:T(8,128)(2,1)S(1)}, u32[]{:S(2)}, u32[]{:S(2)}) collective-permute-start(bf16[64,8192]{1,0:T(8,128)(2,1)} %bitcast.26), channel_id=1, source_target_pairs={{0,1},{1,0},{2,3},{3,2},{4,5},{5,4},{6,7},{7,6},{8,9},{9,8},{10,11... | collective-permute-start | bytes 3145736 | tf_op jit(solution)/shard_map/ppermute | solution.py:26
  33.1 17.0 %all-to-all-start.1 = ((bf16[64,8,128]{2,1,0:T(8,128)(2,1)}), bf16[64,8,128]{2,1,0:T(8,128)(2,1)S(1)}, u32[]{:S(2)}, u32[]{:S(2)}) async-start(bf16[64,8,128]{2,1,0:T(8,128)(2,1)} %shard_map.122), calls=%async_computation.1 | async-start | bytes 262144 | tf_op jit(solution)/shard_map/all_to_all | solution.py:30
  37.8 3.6 %collective-permute-start.5 = (bf16[2,8,64]{2,1,0:T(8,128)(2,1)}, bf16[2,8,64]{2,1,0:T(8,128)(2,1)S(1)}, u32[]{:S(2)}, u32[]{:S(2)}) collective-permute-start(bf16[2,8,64]{2,1,0:T(8,128)(2,1)} %param.20), channel_id=1, source_target_pairs={{0,1},{1,0},{2,3},{3,2},{4,5},{5,4},{6,7},{7,6},{8,9},{9,8},{10,11... | collective-permute-start | bytes 6152 | tf_op jit(solution)/shard_map/ppermute | solution.py:26
  40.0 1.2 %copy-start.1 = (bf16[1,64,8192]{2,1,0:T(8,128)(2,1)S(1)}, bf16[1,64,8192]{2,1,0:T(8,128)(2,1)}, u32[]{:S(2)}) copy-start(bf16[1,64,8192]{2,1,0:T(8,128)(2,1)} %param.17) | copy-start | bytes 3145732
  67.2 15.6 %all-to-all-start.3 = ((bf16[64,4,128]{2,1,0:T(4,128)(2,1)}), bf16[64,4,128]{2,1,0:T(4,128)(2,1)S(1)}, u32[]{:S(2)}, u32[]{:S(2)}) async-start(bf16[64,4,128]{2,1,0:T(4,128)(2,1)} %shard_map.125), calls=%async_computation.3 | async-start | bytes 131072 | tf_op jit(solution)/shard_map/all_to_all | solution.py:30
  82.8 7.3 %collective-permute-start.6 = (bf16[64,4,128]{2,1,0:T(4,128)(2,1)S(1)}, bf16[64,4,128]{2,1,0:T(4,128)(2,1)S(1)}, u32[]{:S(2)}, u32[]{:S(2)}) collective-permute-start(bf16[64,4,128]{2,1,0:T(4,128)(2,1)S(1)} %all-to-all-done.3), channel_id=1, source_target_pairs={{0,1},{1,0},{2,3},{3,2},{4,5},{5,4},{6,7},{7,6},{8,9},{9,8},{10,11... | collective-permute-start | bytes 196616 | tf_op jit(solution)/shard_map/ppermute | solution.py:26
  86.8 3.3 %copy-start = (bf16[8192,501]{0,1:T(8,128)(2,1)S(1)}, bf16[8192,501]{0,1:T(8,128)(2,1)}, u32[]{:S(2)}) copy-start(bf16[8192,501]{0,1:T(8,128)(2,1)} %param.19) | copy-start | bytes 24625156
  92.9 1.4 %collective-permute-start.7 = (f32[8,128]{1,0:T(8,128)S(1)}, f32[8,128]{1,0:T(8,128)S(1)}, u32[]{:S(2)}, u32[]{:S(2)}) collective-permute-start(f32[8,128]{1,0:T(8,128)S(1)} %shard_map.127.near_ref), channel_id=1, source_target_pairs={{0,1},{1,0},{2,3},{3,2},{4,5},{5,4},{6,7},{7,6},{8,9},{9,8},{10,11... | collective-permute-start | bytes 12296 | tf_op jit(solution)/shard_map/ppermute | solution.py:26
  95.1 16.7 %all-to-all-start.4 = ((f32[128,1,128]{2,1,0:T(1,128)}), f32[128,1,128]{2,1,0:T(1,128)S(1)}, u32[]{:S(2)}, u32[]{:S(2)}) async-start(f32[128,1,128]{2,1,0:T(1,128)} %shard_map.128), calls=%async_computation.4 | async-start | bytes 131072 | tf_op jit(solution)/shard_map/all_to_all | solution.py:30
  101.3 2.8 %collective-permute-start.8 = (bf16[8,64]{1,0:T(8,128)(2,1)S(1)}, bf16[8,64]{1,0:T(8,128)(2,1)S(1)}, u32[]{:S(2)}, u32[]{:S(2)}) collective-permute-start(bf16[8,64]{1,0:T(8,128)(2,1)S(1)} %slice_select_fusion), channel_id=1, source_target_pairs={{0,128},{128,0},{1,129},{129,1},{2,130},{130,2},{3,131},{131,3},{4... | collective-permute-start | bytes 3080 | tf_op jit(solution)/shard_map/ppermute | solution.py:303

commit v8 on v7

--- a/solution.py
+++ b/solution.py
@@ -45,11 +45,12 @@
 SMEM = pl.BlockSpec(memory_space=pltpu.SMEM)
 
 
-def call(kernel, shapes, specs, limit, cost, *operands):
+def call(kernel, shapes, specs, limit, cost, *operands, scratch=()):
     return pl.pallas_call(
         kernel,
         out_shape=shapes,
         in_specs=specs,
+        scratch_shapes=scratch,
         out_specs=jax.tree.map(lambda _: VMEM, shapes),
         compiler_params=pltpu.CompilerParams(vmem_limit_bytes=limit * 2**20),
         cost_estimate=pl.CostEstimate(
@@ -120,7 +121,7 @@
         out_ref[2 * t + 1] = odd[t]
 
 
-def merge_kernel(at_ref, got_ref, q_ref, fk_ref, fv_ref, near_ref, far_ref):
+def merge_kernel(step_ref, core_ref, got_ref, q_ref, fk_ref, fv_ref, near_ref, far_ref):
     x = got_ref[...].astype(F32)
     stats = pltpu.roll(x, HALF, 1)
     tops = stats[:, :, 0:1]
@@ -129,7 +130,7 @@
     scale = 1.0 / math.sqrt(HEAD_SIZE)
     s0 = jnp.sum(fk_ref[0] * q, 1, keepdims=True) * scale
     s1 = jnp.sum(fk_ref[1] * q, 1, keepdims=True) * scale
-    second = at_ref[0] >= 1
+    second = step_ref[0] >= 1
     s1 = jnp.where(second, s1, LOW)
     peak = jnp.maximum(jnp.max(tops, 0), jnp.maximum(s0, s1))
     factor = jnp.exp(tops - peak[None])
@@ -140,7 +141,7 @@
     row = lax.broadcasted_iota(jnp.int32, (8, 128), 0)
     attended = jnp.where(row < HALF, above / below, 0.0)
     turned = pltpu.roll(attended, 64, 1)
-    first = at_ref[1] == 0
+    first = core_ref[0] == 0
     near_ref[...] = jnp.where(first, attended, turned)[:HALF, :64].astype(BF)
     far_ref[...] = jnp.where(first, turned, attended)[:HALF, :64].astype(BF)
 
@@ -150,7 +151,20 @@
     out_ref[...] = jnp.broadcast_to(state.astype(BF)[None], out_ref.shape)
 
 
-def head_kernel(u_ref, head_ref, action_ref, touched_ref, out_ref):
+def head_kernel(
+    core_ref, chip_ref, near_ref, far_ref, got_ref, head_ref, action_ref, touched_ref, out_ref, own_ref, u_ref
+):
+    near, far = near_ref[...].astype(F32), far_ref[...].astype(F32)
+    first = core_ref[0] == 0
+    whole = jnp.concatenate([jnp.where(first, near, far), jnp.where(first, far, near)], 1)
+    square = jnp.sum(jnp.sum(whole * whole, 0), 1, keepdims=True)
+    inverse = lax.rsqrt(square / D + 1e-05)
+    gain = got_ref[...].astype(F32)
+    gain = gain + pltpu.roll(gain, 6, 1)
+    left = lax.broadcasted_iota(jnp.int32, (CHIPS, 1, HEAD_SIZE), 2) < 64
+    gain = jnp.where(left, pltpu.roll(gain[:, 4:5], 64, 2), gain[:, 5:6])
+    u_ref[...] = (whole * inverse[None] * gain).astype(BF)
+    own_ref[...] = u_ref[chip_ref[0]]
     u = jnp.concatenate([u_ref[i] for i in range(CHIPS)], 1)
     logits = lax.dot_general(head_ref[...], u, NT, preferred_element_type=F32)
     ids = lax.broadcasted_iota(jnp.int32, logits.shape, 0)
@@ -217,8 +231,8 @@
     )
     q = exchange(sent, CHIP).reshape(CHIPS * HALF, HEAD_SIZE)
 
-    keys, values, gain, gain_far, _ = lax.optimization_barrier(
-        (stored_key_cache, stored_value_cache, gain_sides, swap(gain_sides), sent)
+    keys, values, lengths, gain, gain_far, _ = lax.optimization_barrier(
+        (stored_key_cache, stored_value_cache, lengths, gain_sides, swap(gain_sides), sent)
     )
     keys_far, values_far = swap(keys), swap(values)
     keys, values = rows_of(keys, row0), rows_of(values, row0)
@@ -264,10 +278,11 @@
     near, far = call(
         merge_kernel,
         (part, part),
-        [SMEM] + [VMEM] * 4,
+        [SMEM] * 2 + [VMEM] * 4,
         16,
         CHIPS * 8 * HEAD_SIZE * 8,
-        jnp.stack([step, core]),
+        step[None],
+        core[None],
         got,
         q_chip,
         fresh(new_keys),
@@ -290,29 +305,26 @@
         r_chip,
     )
     mine = exchange(sent, CHIP)
-    head_t, got, _ = lax.optimization_barrier((head.T, got, mine))
+    head_t, _ = lax.optimization_barrier((head.T, mine))
     touched = call(touch_kernel, jax.ShapeDtypeStruct((8, 128), BF), [VMEM], 24, 1 << 24, head_t)
-    gains = got[:, HALF:, 64:].astype(F32).reshape(CHIPS, 2, HEAD_SIZE).sum(1)
-    whole = by_core(core, mine, swap(mine), 1).astype(F32)
-    square = jnp.sum(jnp.sum(whole * whole, 0), -1, keepdims=True)
-    inverse = lax.rsqrt(square / D + 1e-05)
-    normed = (whole * inverse[None] * gains[:, None, :]).astype(BF)
-    own = lax.dynamic_index_in_dim(normed, chip, 0, keepdims=False)
-    own = jnp.where(core == 0, own[:, :64], own[:, 64:])
-    to_side = [(0, 1), (1, 0)]
-    peer_normed = lax.ppermute(own, "role", to_side)
-    width = head.shape[1]
-    local = call(
+    local, own = call(
         head_kernel,
-        jax.ShapeDtypeStruct((8, 128), F32),
-        [VMEM] * 4,
+        (jax.ShapeDtypeStruct((8, 128), F32), jax.ShapeDtypeStruct((8, HEAD_SIZE), BF)),
+        [SMEM] * 2 + [VMEM] * 6,
         24,
-        2 * 8 * D * width,
-        normed,
+        2 * 8 * D * head.shape[1],
+        core[None],
+        chip[None],
+        mine,
+        swap(mine),
+        got,
         head_t,
         action,
         touched,
-    )
+        scratch=[pltpu.VMEM((CHIPS, 8, HEAD_SIZE), BF)],
+    )
+    own = jnp.where(core == 0, own[:, :64], own[:, 64:])
+    peer_normed = lax.ppermute(own, "role", [(0, 1), (1, 0)])
     packed = call(
         pack_kernel,
         jax.ShapeDtypeStruct((2 * CHIPS, 1, HEAD_SIZE), F32),

time: 113 us -> 113 us (level)
  blocking collectives: 14.9 us -> 30.4 us
  waiting for transfers between devices: 37.8 us -> 25.3 us
  starting transfers between devices: 38.9 us -> 34.2 us
  local copies, waits for them, and re-layouts: 10.3 us -> 13.5 us
    all_to_all x1 -> x2, blocking collectives: 14.9 us -> 30.4 us  [exchange(): return lax.all_to_all(x, axes, split_axis=0, concat_axis=0, tiled=True)]
    all_to_all x4 -> x3, waiting for transfers between devices: 34.8 us -> 22.1 us  [exchange(): return lax.all_to_all(x, axes, split_axis=0, concat_axis=0, tiled=True)]
    all_to_all x4 -> x3, starting transfers between devices: 27.9 us -> 23.3 us  [exchange(): return lax.all_to_all(x, axes, split_axis=0, concat_axis=0, tiled=True)]
    unnamed x4 -> x6, local copies, waits for them, and re-layouts: 4.56 us -> 7.91 us
  transfers between devices with their start and end apart: 13 -> 12, of which waited for: 6 -> 6; matrix products, arithmetic and copies ran while one was open for 7% -> 7% of each run, Pallas kernels for 1% -> 0%
where the time goes in v8:
time: 113 us; the launch traced here: 112 us
  starting transfers between devices  34.2 us (30%)
  blocking collectives  30.4 us (27%)
  waiting for transfers between devices  25.3 us (22%)
  local copies, waits for them, and re-layouts  13.5 us (12%)
  Pallas kernels  5.91 us (5%)
  other arithmetic  1.92 us (2%)
    all_to_all x2, blocking collectives, exchange(): return lax.all_to_all(x, axes, split_axis=0, concat_axis=0, tiled=True)  30.4 us
    all_to_all x3, starting transfers between devices, exchange(): return lax.all_to_all(x, axes, split_axis=0, concat_axis=0, tiled=True)  23.3 us
    all_to_all x3, waiting for transfers between devices, exchange(): return lax.all_to_all(x, axes, split_axis=0, concat_axis=0, tiled=True)  22.1 us
    ppermute x8, starting transfers between devices, swap(): return lax.ppermute(x, CORE, [(0, 1), (1, 0)])  9.97 us
    unnamed x6, local copies, waits for them, and re-layouts  7.91 us
    pallas_call x8, Pallas kernels, call(): pl.pallas_call(kernel, out_shape=shapes, in_specs=specs, scratch_shapes=s...  5.91 us
    dynamic_slice x5, local copies, waits for them, and re-layouts, rows_of(): return lax.dynamic_slice_in_dim(x, start, HALF, axis)  3.37 us
  transfers between devices with their start and end apart: 12, of which 6 were waited for; matrix products, arithmetic and copies ran while one was open for 7% of the time, Pallas kernels for 0%

profile of v8, /device:TPU:1, one launch (start us, length us, event | category | flops | bytes accessed | tf_op | source)
XLA Modules:
  0.0 112.5 jit_solution(15491511858761480619)
XLA Ops:
  0.6 3.3 %collective-permute-start = (bf16[2,8,64]{2,1,0:T(8,128)(2,1)}, bf16[2,8,64]{2,1,0:T(8,128)(2,1)S(1)}, u32[]{:S(2)}, u32[]{:S(2)}) collective-permute-start(bf16[2,8,64]{2,1,0:T(8,128)(2,1)} %param.11), channel_id=1, source_target_pairs={{0,1},{1,0},{2,3},{3,2},{4,5},{5,4},{6,7},{7,6},{8,9},{9,8},{10,11... | collective-permute-start | bytes 6152 | tf_op jit(solution)/shard_map/ppermute | solution.py:26
  4.1 0.7 fusion.2
  5.1 0.6 broadcast_in_dim.27
  5.7 12.5 %all-to-all-start = ((bf16[64,4,128]{2,1,0:T(4,128)(2,1)}), bf16[64,4,128]{2,1,0:T(4,128)(2,1)S(1)}, u32[]{:S(2)}, u32[]{:S(2)}) async-start(bf16[64,4,128]{2,1,0:T(4,128)(2,1)} %broadcast_in_dim.27), calls=%async_computation | async-start | bytes 131072 | tf_op jit(solution)/shard_map/all_to_all | solution.py:30
  18.3 1.0 constant_dynamic-slice_fusion.6.k_ref
  19.3 0.7 collective-permute-start.2
  20.1 0.7 dynamic_slice.44
  20.8 0.7 fusion.8
  21.8 1.0 constant_dynamic-slice_fusion.5.v_ref
  22.8 6.6 %all-to-all-done = bf16[64,4,128]{2,1,0:T(4,128)(2,1)S(1)} async-done(((bf16[64,4,128]{2,1,0:T(4,128)(2,1)}), bf16[64,4,128]{2,1,0:T(4,128)(2,1)S(1)}, u32[]{:S(2)}, u32[]{:S(2)}) %all-to-all-start) | async-done | bytes 65568 | tf_op jit(solution)/shard_map/all_to_all | solution.py:30
  29.4 1.2 %shard_map.122 = bf16[64,8,128]{2,1,0:T(8,128)(2,1)} custom-call(s32[1]{0:T(128)} %bitcast.1.core_ref, bf16[256,128]{1,0:T(8,128)(2,1)S(1)} %bitcast.27, bf16[4,32,1024]{2,1,0:T(8,128)(2,1)S(1)} %constant_dynamic-slice_fusion.6.k_ref, bf16[4,32,1024]{2,1,0:T(8,128)(2,1)S(1)} %constant_dynamic-slice_fusion.5.v_ref, ...), custom_call_target="tpu_custom_call" | custom-call | flops 33554432 | bytes 2097152 | tf_op jit(solution)/shard_map/pallas_call | solution.py:49
  30.6 1.7 %collective-permute-start.4 = (bf16[64,8192]{1,0:T(8,128)(2,1)}, bf16[64,8192]{1,0:T(8,128)(2,1)S(1)}, u32[]{:S(2)}, u32[]{:S(2)}) collective-permute-start(bf16[64,8192]{1,0:T(8,128)(2,1)} %bitcast.25), channel_id=1, source_target_pairs={{0,1},{1,0},{2,3},{3,2},{4,5},{5,4},{6,7},{7,6},{8,9},{9,8},{10,11... | collective-permute-start | bytes 3145736 | tf_op jit(solution)/shard_map/ppermute | solution.py:26
  32.3 4.7 %all-to-all-start.1 = ((bf16[64,8,128]{2,1,0:T(8,128)(2,1)}), bf16[64,8,128]{2,1,0:T(8,128)(2,1)S(1)}, u32[]{:S(2)}, u32[]{:S(2)}) async-start(bf16[64,8,128]{2,1,0:T(8,128)(2,1)} %shard_map.122), calls=%async_computation.1 | async-start | bytes 262144 | tf_op jit(solution)/shard_map/all_to_all | solution.py:30
  37.0 0.4 collective-permute-start.5
  37.4 0.7 fusion.4
  38.1 0.8 constant_dynamic-slice_fusion.3
  38.9 0.7 fusion.7.action_ref
  39.6 1.2 %copy-done.2 = bf16[1,64,8192]{2,1,0:T(8,128)(2,1)S(1)} copy-done((bf16[1,64,8192]{2,1,0:T(8,128)(2,1)S(1)}, bf16[1,64,8192]{2,1,0:T(8,128)(2,1)}, u32[]{:S(2)}) %copy-start.2) | copy-done | bytes 1048600
  41.0 7.7 %all-to-all-done.1.got_ref = bf16[64,8,128]{2,1,0:T(8,128)(2,1)S(1)} async-done(((bf16[64,8,128]{2,1,0:T(8,128)(2,1)}), bf16[64,8,128]{2,1,0:T(8,128)(2,1)S(1)}, u32[]{:S(2)}, u32[]{:S(2)}) %all-to-all-start.1) | async-done | bytes 131104 | tf_op jit(solution)/shard_map/all_to_all | solution.py:30
  49.6 15.6 %all_to_all.25.got_ref = bf16[64,4,128]{2,1,0:T(4,128)(2,1)S(1)} all-to-all(bf16[64,4,128]{2,1,0:T(4,128)(2,1)S(1)} %fusion.1), channel_id=1, replica_groups=mesh['role'=2,'grp'=2,'tp_0'=4,'tp_1'=8,'tp_2'=2] {'grp','tp_0','tp_1'}, dimensions={0} | all-to-all | bytes 131072 | tf_op jit(solution)/shard_map/all_to_all | solution.py:30
  65.3 14.8 %all_to_all.26.near_ref = bf16[64,4,128]{2,1,0:T(4,128)(2,1)S(1)} all-to-all(bf16[64,4,128]{2,1,0:T(4,128)(2,1)S(1)} %shard_map.125), channel_id=1, replica_groups=mesh['role'=2,'grp'=2,'tp_0'=4,'tp_1'=8,'tp_2'=2] {'grp','tp_0','tp_1'}, dimensions={0} | all-to-all | bytes 131072 | tf_op jit(solution)/shard_map/all_to_all | solution.py:30
  80.2 3.5 %collective-permute-start.6 = (bf16[64,4,128]{2,1,0:T(4,128)(2,1)S(1)}, bf16[64,4,128]{2,1,0:T(4,128)(2,1)S(1)}, u32[]{:S(2)}, u32[]{:S(2)}) collective-permute-start(bf16[64,4,128]{2,1,0:T(4,128)(2,1)S(1)} %all_to_all.26.near_ref), channel_id=1, source_target_pairs={{0,1},{1,0},{2,3},{3,2},{4,5},{5,4},{6,7},{7,6},{8,9},{9,8},{10,11... | collective-permute-start | bytes 196616 | tf_op jit(solution)/shard_map/ppermute | solution.py:26
  83.7 3.3 %copy-done = bf16[8192,501]{0,1:T(8,128)(2,1)S(1)} copy-done((bf16[8192,501]{0,1:T(8,128)(2,1)S(1)}, bf16[8192,501]{0,1:T(8,128)(2,1)}, u32[]{:S(2)}) %copy-start) | copy-done | bytes 8208408
  87.0 3.3 %copy-done.1 = bf16[8192,501]{0,1:T(8,128)(2,1)S(1)} copy-done((bf16[8192,501]{0,1:T(8,128)(2,1)S(1)}, bf16[8192,501]{0,1:T(8,128)(2,1)}, u32[]{:S(2)}) %copy-start.1) | copy-done | bytes 8208408
  90.4 2.7 %shard_map.127 = (f32[8,128]{1,0:T(8,128)S(1)}, bf16[8,128]{1,0:T(8,128)(2,1)S(1)}) custom-call(s32[1]{0:T(128)} %bitcast.1.core_ref, s32[1]{0:T(128)} %bitcast.2.chip_ref, bf16[64,4,128]{2,1,0:T(4,128)(2,1)S(1)} %all_to_all.26.near_ref, bf16[64,4,128]{2,1,0:T(4,128)(2,1)S(1)} %collective-permute-done.6.far_ref, ...), custom_call_target="tpu_custom_call" | custom-call | flops 65667072 | bytes 4104192 | tf_op jit(solution)/shard_map/pallas_call | solution.py:49
  93.1 1.2 %collective-permute-done.7.far_ref = f32[8,128]{1,0:T(8,128)S(1)} collective-permute-done((f32[8,128]{1,0:T(8,128)S(1)}, f32[8,128]{1,0:T(8,128)S(1)}, u32[]{:S(2)}, u32[]{:S(2)}) %collective-permute-start.7) | collective-permute-done | bytes 4128 | tf_op jit(solution)/shard_map/ppermute | solution.py:26
  94.3 0.7 shard_map.128
  95.0 6.1 %all-to-all-start.4 = ((f32[128,1,128]{2,1,0:T(1,128)}), f32[128,1,128]{2,1,0:T(1,128)S(1)}, u32[]{:S(2)}, u32[]{:S(2)}) async-start(f32[128,1,128]{2,1,0:T(1,128)} %shard_map.128), calls=%async_computation.4 | async-start | bytes 131072 | tf_op jit(solution)/shard_map/all_to_all | solution.py:30
  101.2 0.9 collective-permute-start.8
  102.1 1.8 %collective-permute-done.8.normed_ref = bf16[8,64]{1,0:T(8,128)(2,1)S(1)} collective-permute-done((bf16[8,64]{1,0:T(8,128)(2,1)S(1)}, bf16[8,64]{1,0:T(8,128)(2,1)S(1)}, u32[]{:S(2)}, u32[]{:S(2)}) %collective-permute-start.8) | collective-permute-done | bytes 1056 | tf_op jit(solution)/shard_map/ppermute | solution.py:327
  104.0 7.8 %all-to-all-done.4.heard_ref = f32[128,1,128]{2,1,0:T(1,128)S(1)} async-done(((f32[128,1,128]{2,1,0:T(1,128)}), f32[128,1,128]{2,1,0:T(1,128)S(1)}, u32[]{:S(2)}, u32[]{:S(2)}) %all-to-all-start.4) | async-done | bytes 65568 | tf_op jit(solution)/shard_map/all_to_all | solution.py:30
  111.7 0.7 shard_map.129
  (34 shorter events, 2.2 us)
Async XLA Ops:
  0.6 4.4 %collective-permute-start = (bf16[2,8,64]{2,1,0:T(8,128)(2,1)}, bf16[2,8,64]{2,1,0:T(8,128)(2,1)S(1)}, u32[]{:S(2)}, u32[]{:S(2)}) collective-permute-start(bf16[2,8,64]{2,1,0:T(8,128)(2,1)} %param.11), channel_id=1, source_target_pairs={{0,1},{1,0},{2,3},{3,2},{4,5},{5,4},{6,7},{7,6},{8,9},{9,8},{10,11... | collective-permute-start | bytes 6152 | tf_op jit(solution)/shard_map/ppermute | solution.py:26
  4.0 14.3 %collective-permute-start.1 = (f32[1,64]{1,0:T(1,128)}, f32[1,64]{1,0:T(1,128)S(1)}, u32[]{:S(2)}, u32[]{:S(2)}) collective-permute-start(f32[1,64]{1,0:T(1,128)} %param.18), channel_id=1, source_target_pairs={{0,1},{1,0},{2,3},{3,2},{4,5},{5,4},{6,7},{7,6},{8,9},{9,8},{10,11... | collective-permute-start | bytes 776 | tf_op jit(solution)/shard_map/ppermute | solution.py:26
  5.7 23.7 %all-to-all-start = ((bf16[64,4,128]{2,1,0:T(4,128)(2,1)}), bf16[64,4,128]{2,1,0:T(4,128)(2,1)S(1)}, u32[]{:S(2)}, u32[]{:S(2)}) async-start(bf16[64,4,128]{2,1,0:T(4,128)(2,1)} %broadcast_in_dim.27), calls=%async_computation | async-start | bytes 131072 | tf_op jit(solution)/shard_map/all_to_all | solution.py:30
  19.3 10.1 %collective-permute-start.2 = (bf16[8,32,1024]{2,1,0:T(8,128)(2,1)}, bf16[8,32,1024]{2,1,0:T(8,128)(2,1)S(1)}, u32[]{:S(2)}, u32[]{:S(2)}) collective-permute-start(bf16[8,32,1024]{2,1,0:T(8,128)(2,1)} %param.14), channel_id=1, source_target_pairs={{0,1},{1,0},{2,3},{3,2},{4,5},{5,4},{6,7},{7,6},{8,9},{9,8},{10,11... | collective-permute-start | bytes 1572872 | tf_op jit(solution)/shard_map/ppermute | solution.py:26
  20.0 9.4 %collective-permute-start.3 = (bf16[8,32,1024]{2,1,0:T(8,128)(2,1)}, bf16[8,32,1024]{2,1,0:T(8,128)(2,1)S(1)}, u32[]{:S(2)}, u32[]{:S(2)}) collective-permute-start(bf16[8,32,1024]{2,1,0:T(8,128)(2,1)} %param.15), channel_id=1, source_target_pairs={{0,1},{1,0},{2,3},{3,2},{4,5},{5,4},{6,7},{7,6},{8,9},{9,8},{10,11... | collective-permute-start | bytes 1572872 | tf_op jit(solution)/shard_map/ppermute | solution.py:26
  30.6 18.5 %collective-permute-start.4 = (bf16[64,8192]{1,0:T(8,128)(2,1)}, bf16[64,8192]{1,0:T(8,128)(2,1)S(1)}, u32[]{:S(2)}, u32[]{:S(2)}) collective-permute-start(bf16[64,8192]{1,0:T(8,128)(2,1)} %bitcast.25), channel_id=1, source_target_pairs={{0,1},{1,0},{2,3},{3,2},{4,5},{5,4},{6,7},{7,6},{8,9},{9,8},{10,11... | collective-permute-start | bytes 3145736 | tf_op jit(solution)/shard_map/ppermute | solution.py:26
  32.3 16.4 %all-to-all-start.1 = ((bf16[64,8,128]{2,1,0:T(8,128)(2,1)}), bf16[64,8,128]{2,1,0:T(8,128)(2,1)S(1)}, u32[]{:S(2)}, u32[]{:S(2)}) async-start(bf16[64,8,128]{2,1,0:T(8,128)(2,1)} %shard_map.122), calls=%async_computation.1 | async-start | bytes 262144 | tf_op jit(solution)/shard_map/all_to_all | solution.py:30
  37.0 3.9 %collective-permute-start.5 = (bf16[2,8,64]{2,1,0:T(8,128)(2,1)}, bf16[2,8,64]{2,1,0:T(8,128)(2,1)S(1)}, u32[]{:S(2)}, u32[]{:S(2)}) collective-permute-start(bf16[2,8,64]{2,1,0:T(8,128)(2,1)} %param.20), channel_id=1, source_target_pairs={{0,1},{1,0},{2,3},{3,2},{4,5},{5,4},{6,7},{7,6},{8,9},{9,8},{10,11... | collective-permute-start | bytes 6152 | tf_op jit(solution)/shard_map/ppermute | solution.py:26
  39.6 1.2 %copy-start.2 = (bf16[1,64,8192]{2,1,0:T(8,128)(2,1)S(1)}, bf16[1,64,8192]{2,1,0:T(8,128)(2,1)}, u32[]{:S(2)}) copy-start(bf16[1,64,8192]{2,1,0:T(8,128)(2,1)} %param.17) | copy-start | bytes 3145732
  80.2 6.9 %collective-permute-start.6 = (bf16[64,4,128]{2,1,0:T(4,128)(2,1)S(1)}, bf16[64,4,128]{2,1,0:T(4,128)(2,1)S(1)}, u32[]{:S(2)}, u32[]{:S(2)}) collective-permute-start(bf16[64,4,128]{2,1,0:T(4,128)(2,1)S(1)} %all_to_all.26.near_ref), channel_id=1, source_target_pairs={{0,1},{1,0},{2,3},{3,2},{4,5},{5,4},{6,7},{7,6},{8,9},{9,8},{10,11... | collective-permute-start | bytes 196616 | tf_op jit(solution)/shard_map/ppermute | solution.py:26
  83.7 3.3 %copy-start = (bf16[8192,501]{0,1:T(8,128)(2,1)S(1)}, bf16[8192,501]{0,1:T(8,128)(2,1)}, u32[]{:S(2)}) copy-start(bf16[8192,501]{0,1:T(8,128)(2,1)} %param.19) | copy-start | bytes 24625156
  87.0 3.3 %copy-start.1 = (bf16[8192,501]{0,1:T(8,128)(2,1)S(1)}, bf16[8192,501]{0,1:T(8,128)(2,1)}, u32[]{:S(2)}) copy-start(bf16[8192,501]{0,1:T(8,128)(2,1)} %param.19) | copy-start | bytes 24625156
  93.0 1.3 %collective-permute-start.7 = (f32[8,128]{1,0:T(8,128)S(1)}, f32[8,128]{1,0:T(8,128)S(1)}, u32[]{:S(2)}, u32[]{:S(2)}) collective-permute-start(f32[8,128]{1,0:T(8,128)S(1)} %get-tuple-element.36.near_ref), channel_id=1, source_target_pairs={{0,1},{1,0},{2,3},{3,2},{4,5},{5,4},{6,7},{7,6},{8,9},{9,8},{10,11... | collective-permute-start | bytes 12296 | tf_op jit(solution)/shard_map/ppermute | solution.py:26
  95.0 16.7 %all-to-all-start.4 = ((f32[128,1,128]{2,1,0:T(1,128)}), f32[128,1,128]{2,1,0:T(1,128)S(1)}, u32[]{:S(2)}, u32[]{:S(2)}) async-start(f32[128,1,128]{2,1,0:T(1,128)} %shard_map.128), calls=%async_computation.4 | async-start | bytes 131072 | tf_op jit(solution)/shard_map/all_to_all | solution.py:30
  101.2 2.8 %collective-permute-start.8 = (bf16[8,64]{1,0:T(8,128)(2,1)S(1)}, bf16[8,64]{1,0:T(8,128)(2,1)S(1)}, u32[]{:S(2)}, u32[]{:S(2)}) collective-permute-start(bf16[8,64]{1,0:T(8,128)(2,1)S(1)} %slice_select_fusion), channel_id=1, source_target_pairs={{0,128},{128,0},{1,129},{129,1},{2,130},{130,2},{3,131},{131,3},{4... | collective-permute-start | bytes 3080 | tf_op jit(solution)/shard_map/ppermute | solution.py:327

commit v9 on v8

--- a/solution.py
+++ b/solution.py
@@ -61,10 +61,6 @@
 
 def load_kernel(x_ref, out_ref):
     out_ref[...] = x_ref[...]
-
-
-def touch_kernel(x_ref, out_ref):
-    out_ref[...] = x_ref[0:16, 0:128][0:8]
 
 
 def attend_kernel(core_ref, q_ref, k_ref, v_ref, kf_ref, vf_ref, ok_ref, pack_ref, out_ref):
@@ -152,7 +148,7 @@
 
 
 def head_kernel(
-    core_ref, chip_ref, near_ref, far_ref, got_ref, head_ref, action_ref, touched_ref, out_ref, own_ref, u_ref
+    core_ref, chip_ref, near_ref, far_ref, got_ref, head_ref, action_ref, out_ref, own_ref, u_ref
 ):
     near, far = near_ref[...].astype(F32), far_ref[...].astype(F32)
     first = core_ref[0] == 0
@@ -306,11 +302,11 @@
     )
     mine = exchange(sent, CHIP)
     head_t, _ = lax.optimization_barrier((head.T, mine))
-    touched = call(touch_kernel, jax.ShapeDtypeStruct((8, 128), BF), [VMEM], 24, 1 << 24, head_t)
+    head_t = call(load_kernel, jax.ShapeDtypeStruct(head_t.shape, BF), [VMEM], 24, 1 << 24, head_t)
     local, own = call(
         head_kernel,
         (jax.ShapeDtypeStruct((8, 128), F32), jax.ShapeDtypeStruct((8, HEAD_SIZE), BF)),
-        [SMEM] * 2 + [VMEM] * 6,
+        [SMEM] * 2 + [VMEM] * 5,
         24,
         2 * 8 * D * head.shape[1],
         core[None],
@@ -320,7 +316,6 @@
         got,
         head_t,
         action,
-        touched,
         scratch=[pltpu.VMEM((CHIPS, 8, HEAD_SIZE), BF)],
     )
     own = jnp.where(core == 0, own[:, :64], own[:, 64:])

time: 113 us -> 111 us (0.982)
  local copies, waits for them, and re-layouts: 13.5 us -> 10.1 us
    unnamed x6 -> x4, local copies, waits for them, and re-layouts: 7.91 us -> 4.57 us
  transfers between devices with their start and end apart: 12 -> 12, of which waited for: 6 -> 6; matrix products, arithmetic and copies ran while one was open for 7% -> 7% of each run, Pallas kernels for 0% -> 1%
where the time goes in v9:
time: 111 us; the launch traced here: 110 us
  starting transfers between devices  33.8 us (30%)
  blocking collectives  30.6 us (28%)
  waiting for transfers between devices  25.9 us (23%)
  local copies, waits for them, and re-layouts  10.1 us (9%)
  Pallas kernels  6.45 us (6%)
  other arithmetic  1.92 us (2%)
    all_to_all x2, blocking collectives, exchange(): return lax.all_to_all(x, axes, split_axis=0, concat_axis=0, tiled=True)  30.6 us
    all_to_all x3, starting transfers between devices, exchange(): return lax.all_to_all(x, axes, split_axis=0, concat_axis=0, tiled=True)  23.3 us
    all_to_all x3, waiting for transfers between devices, exchange(): return lax.all_to_all(x, axes, split_axis=0, concat_axis=0, tiled=True)  22.4 us
    ppermute x8, starting transfers between devices, swap(): return lax.ppermute(x, CORE, [(0, 1), (1, 0)])  9.55 us
    pallas_call x8, Pallas kernels, call(): pl.pallas_call(kernel, out_shape=shapes, in_specs=specs, scratch_shapes=s...  6.45 us
    unnamed x4, local copies, waits for them, and re-layouts  4.57 us
    dynamic_slice x5, local copies, waits for them, and re-layouts, rows_of(): return lax.dynamic_slice_in_dim(x, start, HALF, axis)  3.37 us
  transfers between devices with their start and end apart: 12, of which 6 were waited for; matrix products, arithmetic and copies ran while one was open for 7% of the time, Pallas kernels for 1%

profile of v9, /device:TPU:1, one launch (start us, length us, event | category | flops | bytes accessed | tf_op | source)
XLA Modules:
  0.0 110.0 jit_solution(15254967893560901963)
XLA Ops:
  0.6 3.3 %collective-permute-start.1 = (f32[1,64]{1,0:T(1,128)}, f32[1,64]{1,0:T(1,128)S(1)}, u32[]{:S(2)}, u32[]{:S(2)}) collective-permute-start(f32[1,64]{1,0:T(1,128)} %param.18), channel_id=1, source_target_pairs={{0,1},{1,0},{2,3},{3,2},{4,5},{5,4},{6,7},{7,6},{8,9},{9,8},{10,11... | collective-permute-start | bytes 776 | tf_op jit(solution)/shard_map/ppermute | solution.py:26
  4.1 0.7 fusion.2
  5.4 0.6 broadcast_in_dim.27
  6.1 12.6 %all-to-all-start = ((bf16[64,4,128]{2,1,0:T(4,128)(2,1)}), bf16[64,4,128]{2,1,0:T(4,128)(2,1)S(1)}, u32[]{:S(2)}, u32[]{:S(2)}) async-start(bf16[64,4,128]{2,1,0:T(4,128)(2,1)} %broadcast_in_dim.27), calls=%async_computation | async-start | bytes 131072 | tf_op jit(solution)/shard_map/all_to_all | solution.py:30
  18.6 1.0 constant_dynamic-slice_fusion.6.k_ref
  19.6 0.5 collective-permute-start.2
  20.1 0.7 dynamic_slice.44
  20.9 0.7 fusion.8
  21.9 1.0 constant_dynamic-slice_fusion.5.v_ref
  22.9 7.0 %all-to-all-done = bf16[64,4,128]{2,1,0:T(4,128)(2,1)S(1)} async-done(((bf16[64,4,128]{2,1,0:T(4,128)(2,1)}), bf16[64,4,128]{2,1,0:T(4,128)(2,1)S(1)}, u32[]{:S(2)}, u32[]{:S(2)}) %all-to-all-start) | async-done | bytes 65568 | tf_op jit(solution)/shard_map/all_to_all | solution.py:30
  29.9 1.2 %shard_map.122 = bf16[64,8,128]{2,1,0:T(8,128)(2,1)} custom-call(s32[1]{0:T(128)} %bitcast.1.core_ref, bf16[256,128]{1,0:T(8,128)(2,1)S(1)} %bitcast.26, bf16[4,32,1024]{2,1,0:T(8,128)(2,1)S(1)} %constant_dynamic-slice_fusion.6.k_ref, bf16[4,32,1024]{2,1,0:T(8,128)(2,1)S(1)} %constant_dynamic-slice_fusion.5.v_ref, ...), custom_call_target="tpu_custom_call" | custom-call | flops 33554432 | bytes 2097152 | tf_op jit(solution)/shard_map/pallas_call | solution.py:49
  31.1 1.3 %collective-permute-start.4 = (bf16[64,8192]{1,0:T(8,128)(2,1)}, bf16[64,8192]{1,0:T(8,128)(2,1)S(1)}, u32[]{:S(2)}, u32[]{:S(2)}) collective-permute-start(bf16[64,8192]{1,0:T(8,128)(2,1)} %bitcast.24), channel_id=1, source_target_pairs={{0,1},{1,0},{2,3},{3,2},{4,5},{5,4},{6,7},{7,6},{8,9},{9,8},{10,11... | collective-permute-start | bytes 3145736 | tf_op jit(solution)/shard_map/ppermute | solution.py:26
  32.4 4.7 %all-to-all-start.1 = ((bf16[64,8,128]{2,1,0:T(8,128)(2,1)}), bf16[64,8,128]{2,1,0:T(8,128)(2,1)S(1)}, u32[]{:S(2)}, u32[]{:S(2)}) async-start(bf16[64,8,128]{2,1,0:T(8,128)(2,1)} %shard_map.122), calls=%async_computation.1 | async-start | bytes 262144 | tf_op jit(solution)/shard_map/all_to_all | solution.py:30
  37.1 0.5 collective-permute-start.5
  37.6 0.7 fusion.4
  38.3 0.8 constant_dynamic-slice_fusion.3
  39.1 0.7 fusion.7.action_ref
  39.8 1.2 %copy-done.1 = bf16[1,64,8192]{2,1,0:T(8,128)(2,1)S(1)} copy-done((bf16[1,64,8192]{2,1,0:T(8,128)(2,1)S(1)}, bf16[1,64,8192]{2,1,0:T(8,128)(2,1)}, u32[]{:S(2)}) %copy-start.1) | copy-done | bytes 1048600
  41.2 7.6 %all-to-all-done.1.got_ref = bf16[64,8,128]{2,1,0:T(8,128)(2,1)S(1)} async-done(((bf16[64,8,128]{2,1,0:T(8,128)(2,1)}), bf16[64,8,128]{2,1,0:T(8,128)(2,1)S(1)}, u32[]{:S(2)}, u32[]{:S(2)}) %all-to-all-start.1) | async-done | bytes 131104 | tf_op jit(solution)/shard_map/all_to_all | solution.py:30
  49.7 15.8 %all_to_all.25.got_ref = bf16[64,4,128]{2,1,0:T(4,128)(2,1)S(1)} all-to-all(bf16[64,4,128]{2,1,0:T(4,128)(2,1)S(1)} %fusion.1), channel_id=1, replica_groups=mesh['role'=2,'grp'=2,'tp_0'=4,'tp_1'=8,'tp_2'=2] {'grp','tp_0','tp_1'}, dimensions={0} | all-to-all | bytes 131072 | tf_op jit(solution)/shard_map/all_to_all | solution.py:30
  65.6 14.8 %all_to_all.26.near_ref = bf16[64,4,128]{2,1,0:T(4,128)(2,1)S(1)} all-to-all(bf16[64,4,128]{2,1,0:T(4,128)(2,1)S(1)} %shard_map.125), channel_id=1, replica_groups=mesh['role'=2,'grp'=2,'tp_0'=4,'tp_1'=8,'tp_2'=2] {'grp','tp_0','tp_1'}, dimensions={0} | all-to-all | bytes 131072 | tf_op jit(solution)/shard_map/all_to_all | solution.py:30
  80.4 3.4 %collective-permute-start.6 = (bf16[64,4,128]{2,1,0:T(4,128)(2,1)S(1)}, bf16[64,4,128]{2,1,0:T(4,128)(2,1)S(1)}, u32[]{:S(2)}, u32[]{:S(2)}) collective-permute-start(bf16[64,4,128]{2,1,0:T(4,128)(2,1)S(1)} %all_to_all.26.near_ref), channel_id=1, source_target_pairs={{0,1},{1,0},{2,3},{3,2},{4,5},{5,4},{6,7},{7,6},{8,9},{9,8},{10,11... | collective-permute-start | bytes 196616 | tf_op jit(solution)/shard_map/ppermute | solution.py:26
  83.8 3.3 %copy-done = bf16[8192,501]{0,1:T(8,128)(2,1)S(1)} copy-done((bf16[8192,501]{0,1:T(8,128)(2,1)S(1)}, bf16[8192,501]{0,1:T(8,128)(2,1)}, u32[]{:S(2)}) %copy-start) | copy-done | bytes 8208408
  87.1 0.5 shard_map.126.head_ref
  87.7 2.7 %shard_map.127 = (f32[8,128]{1,0:T(8,128)S(1)}, bf16[8,128]{1,0:T(8,128)(2,1)S(1)}) custom-call(s32[1]{0:T(128)} %bitcast.1.core_ref, s32[1]{0:T(128)} %bitcast.2.chip_ref, bf16[64,4,128]{2,1,0:T(4,128)(2,1)S(1)} %all_to_all.26.near_ref, bf16[64,4,128]{2,1,0:T(4,128)(2,1)S(1)} %collective-permute-done.6.far_ref, ...), custom_call_target="tpu_custom_call" | custom-call | flops 65667072 | bytes 4104192 | tf_op jit(solution)/shard_map/pallas_call | solution.py:49
  90.7 1.2 %collective-permute-done.7.far_ref = f32[8,128]{1,0:T(8,128)S(1)} collective-permute-done((f32[8,128]{1,0:T(8,128)S(1)}, f32[8,128]{1,0:T(8,128)S(1)}, u32[]{:S(2)}, u32[]{:S(2)}) %collective-permute-start.7) | collective-permute-done | bytes 4128 | tf_op jit(solution)/shard_map/ppermute | solution.py:26
  91.8 0.7 shard_map.128
  92.5 6.1 %all-to-all-start.4 = ((f32[128,1,128]{2,1,0:T(1,128)}), f32[128,1,128]{2,1,0:T(1,128)S(1)}, u32[]{:S(2)}, u32[]{:S(2)}) async-start(f32[128,1,128]{2,1,0:T(1,128)} %shard_map.128), calls=%async_computation.4 | async-start | bytes 131072 | tf_op jit(solution)/shard_map/all_to_all | solution.py:30
  98.7 0.9 collective-permute-start.8
  99.6 1.8 %collective-permute-done.8.normed_ref = bf16[8,64]{1,0:T(8,128)(2,1)S(1)} collective-permute-done((bf16[8,64]{1,0:T(8,128)(2,1)S(1)}, bf16[8,64]{1,0:T(8,128)(2,1)S(1)}, u32[]{:S(2)}, u32[]{:S(2)}) %collective-permute-start.8) | collective-permute-done | bytes 1056 | tf_op jit(solution)/shard_map/ppermute | solution.py:322
  101.5 7.8 %all-to-all-done.4.heard_ref = f32[128,1,128]{2,1,0:T(1,128)S(1)} async-done(((f32[128,1,128]{2,1,0:T(1,128)}), f32[128,1,128]{2,1,0:T(1,128)S(1)}, u32[]{:S(2)}, u32[]{:S(2)}) %all-to-all-start.4) | async-done | bytes 65568 | tf_op jit(solution)/shard_map/all_to_all | solution.py:30
  109.3 0.7 shard_map.129
  (32 shorter events, 2.6 us)
Async XLA Ops:
  0.6 18.0 %collective-permute-start.1 = (f32[1,64]{1,0:T(1,128)}, f32[1,64]{1,0:T(1,128)S(1)}, u32[]{:S(2)}, u32[]{:S(2)}) collective-permute-start(f32[1,64]{1,0:T(1,128)} %param.18), channel_id=1, source_target_pairs={{0,1},{1,0},{2,3},{3,2},{4,5},{5,4},{6,7},{7,6},{8,9},{9,8},{10,11... | collective-permute-start | bytes 776 | tf_op jit(solution)/shard_map/ppermute | solution.py:26
  4.0 1.4 %collective-permute-start = (bf16[2,8,64]{2,1,0:T(8,128)(2,1)}, bf16[2,8,64]{2,1,0:T(8,128)(2,1)S(1)}, u32[]{:S(2)}, u32[]{:S(2)}) collective-permute-start(bf16[2,8,64]{2,1,0:T(8,128)(2,1)} %param.11), channel_id=1, source_target_pairs={{0,1},{1,0},{2,3},{3,2},{4,5},{5,4},{6,7},{7,6},{8,9},{9,8},{10,11... | collective-permute-start | bytes 6152 | tf_op jit(solution)/shard_map/ppermute | solution.py:26
  6.1 23.8 %all-to-all-start = ((bf16[64,4,128]{2,1,0:T(4,128)(2,1)}), bf16[64,4,128]{2,1,0:T(4,128)(2,1)S(1)}, u32[]{:S(2)}, u32[]{:S(2)}) async-start(bf16[64,4,128]{2,1,0:T(4,128)(2,1)} %broadcast_in_dim.27), calls=%async_computation | async-start | bytes 131072 | tf_op jit(solution)/shard_map/all_to_all | solution.py:30
  19.6 10.3 %collective-permute-start.2 = (bf16[8,32,1024]{2,1,0:T(8,128)(2,1)}, bf16[8,32,1024]{2,1,0:T(8,128)(2,1)S(1)}, u32[]{:S(2)}, u32[]{:S(2)}) collective-permute-start(bf16[8,32,1024]{2,1,0:T(8,128)(2,1)} %param.14), channel_id=1, source_target_pairs={{0,1},{1,0},{2,3},{3,2},{4,5},{5,4},{6,7},{7,6},{8,9},{9,8},{10,11... | collective-permute-start | bytes 1572872 | tf_op jit(solution)/shard_map/ppermute | solution.py:26
  20.9 9.0 %collective-permute-start.3 = (bf16[8,32,1024]{2,1,0:T(8,128)(2,1)}, bf16[8,32,1024]{2,1,0:T(8,128)(2,1)S(1)}, u32[]{:S(2)}, u32[]{:S(2)}) collective-permute-start(bf16[8,32,1024]{2,1,0:T(8,128)(2,1)} %param.15), channel_id=1, source_target_pairs={{0,1},{1,0},{2,3},{3,2},{4,5},{5,4},{6,7},{7,6},{8,9},{9,8},{10,11... | collective-permute-start | bytes 1572872 | tf_op jit(solution)/shard_map/ppermute | solution.py:26
  31.1 18.1 %collective-permute-start.4 = (bf16[64,8192]{1,0:T(8,128)(2,1)}, bf16[64,8192]{1,0:T(8,128)(2,1)S(1)}, u32[]{:S(2)}, u32[]{:S(2)}) collective-permute-start(bf16[64,8192]{1,0:T(8,128)(2,1)} %bitcast.24), channel_id=1, source_target_pairs={{0,1},{1,0},{2,3},{3,2},{4,5},{5,4},{6,7},{7,6},{8,9},{9,8},{10,11... | collective-permute-start | bytes 3145736 | tf_op jit(solution)/shard_map/ppermute | solution.py:26
  32.4 16.3 %all-to-all-start.1 = ((bf16[64,8,128]{2,1,0:T(8,128)(2,1)}), bf16[64,8,128]{2,1,0:T(8,128)(2,1)S(1)}, u32[]{:S(2)}, u32[]{:S(2)}) async-start(bf16[64,8,128]{2,1,0:T(8,128)(2,1)} %shard_map.122), calls=%async_computation.1 | async-start | bytes 262144 | tf_op jit(solution)/shard_map/all_to_all | solution.py:30
  37.1 4.0 %collective-permute-start.5 = (bf16[2,8,64]{2,1,0:T(8,128)(2,1)}, bf16[2,8,64]{2,1,0:T(8,128)(2,1)S(1)}, u32[]{:S(2)}, u32[]{:S(2)}) collective-permute-start(bf16[2,8,64]{2,1,0:T(8,128)(2,1)} %param.20), channel_id=1, source_target_pairs={{0,1},{1,0},{2,3},{3,2},{4,5},{5,4},{6,7},{7,6},{8,9},{9,8},{10,11... | collective-permute-start | bytes 6152 | tf_op jit(solution)/shard_map/ppermute | solution.py:26
  39.8 1.2 %copy-start.1 = (bf16[1,64,8192]{2,1,0:T(8,128)(2,1)S(1)}, bf16[1,64,8192]{2,1,0:T(8,128)(2,1)}, u32[]{:S(2)}) copy-start(bf16[1,64,8192]{2,1,0:T(8,128)(2,1)} %param.17) | copy-start | bytes 3145732
  80.4 7.3 %collective-permute-start.6 = (bf16[64,4,128]{2,1,0:T(4,128)(2,1)S(1)}, bf16[64,4,128]{2,1,0:T(4,128)(2,1)S(1)}, u32[]{:S(2)}, u32[]{:S(2)}) collective-permute-start(bf16[64,4,128]{2,1,0:T(4,128)(2,1)S(1)} %all_to_all.26.near_ref), channel_id=1, source_target_pairs={{0,1},{1,0},{2,3},{3,2},{4,5},{5,4},{6,7},{7,6},{8,9},{9,8},{10,11... | collective-permute-start | bytes 196616 | tf_op jit(solution)/shard_map/ppermute | solution.py:26
  83.8 3.3 %copy-start = (bf16[8192,501]{0,1:T(8,128)(2,1)S(1)}, bf16[8192,501]{0,1:T(8,128)(2,1)}, u32[]{:S(2)}) copy-start(bf16[8192,501]{0,1:T(8,128)(2,1)} %param.19) | copy-start | bytes 24625156
  90.4 1.4 %collective-permute-start.7 = (f32[8,128]{1,0:T(8,128)S(1)}, f32[8,128]{1,0:T(8,128)S(1)}, u32[]{:S(2)}, u32[]{:S(2)}) collective-permute-start(f32[8,128]{1,0:T(8,128)S(1)} %get-tuple-element.36.near_ref), channel_id=1, source_target_pairs={{0,1},{1,0},{2,3},{3,2},{4,5},{5,4},{6,7},{7,6},{8,9},{9,8},{10,11... | collective-permute-start | bytes 12296 | tf_op jit(solution)/shard_map/ppermute | solution.py:26
  92.5 16.7 %all-to-all-start.4 = ((f32[128,1,128]{2,1,0:T(1,128)}), f32[128,1,128]{2,1,0:T(1,128)S(1)}, u32[]{:S(2)}, u32[]{:S(2)}) async-start(f32[128,1,128]{2,1,0:T(1,128)} %shard_map.128), calls=%async_computation.4 | async-start | bytes 131072 | tf_op jit(solution)/shard_map/all_to_all | solution.py:30
  98.7 2.8 %collective-permute-start.8 = (bf16[8,64]{1,0:T(8,128)(2,1)S(1)}, bf16[8,64]{1,0:T(8,128)(2,1)S(1)}, u32[]{:S(2)}, u32[]{:S(2)}) collective-permute-start(bf16[8,64]{1,0:T(8,128)(2,1)S(1)} %slice_select_fusion), channel_id=1, source_target_pairs={{0,128},{128,0},{1,129},{129,1},{2,130},{130,2},{3,131},{131,3},{4... | collective-permute-start | bytes 3080 | tf_op jit(solution)/shard_map/ppermute | solution.py:322

commit v10 on v9

--- a/solution.py
+++ b/solution.py
@@ -73,7 +73,7 @@
         cols = slice(kv * HEAD_SIZE, (kv + 1) * HEAD_SIZE)
         parts = []
         for r in range(HALF):
-            parts += [near[r, :, cols], far[base + r, :, cols]]
+            parts += [near[base + r, :, cols], far[base + r, :, cols]]
         return jnp.concatenate(parts, 0)
 
     s = jnp.concatenate(
@@ -231,7 +231,8 @@
         (stored_key_cache, stored_value_cache, lengths, gain_sides, swap(gain_sides), sent)
     )
     keys_far, values_far = swap(keys), swap(values)
-    keys, values = rows_of(keys, row0), rows_of(values, row0)
+    to_self = [(0, 0), (1, 1)]
+    keys, values = lax.ppermute(keys, CORE, to_self), lax.ppermute(values, CORE, to_self)
     gain_chip = by_core(core, gain, gain_far, 0)
 
     lens = rows_of(lengths, row0)
@@ -262,7 +263,7 @@
         (wo_sides[0], resid, actions, step_token_keys, step_token_values, sent)
     )
     w_far = swap(w_side)
-    w_mine = call(load_kernel, jax.ShapeDtypeStruct(w_side.shape, BF), [VMEM], 8, 1 << 20, w_side)
+    w_mine = lax.ppermute(w_side, CORE, to_self)
     r_chip = chip_rows(resid, swap(resid)).astype(F32)
     kv = chip // GROUP
 

time: 111 us -> 112 us (level)
  starting transfers between devices: 33.8 us -> 37.4 us
  local copies, waits for them, and re-layouts: 10.1 us -> 6.97 us
  waiting for transfers between devices: 25.9 us -> 27.3 us
    ppermute x0 -> x3, starting transfers between devices: none -> 3.31 us  [the longest x1 1.23 us: on_device(): w_mine = lax.ppermute(w_side, CORE, to_self)]
    dynamic_slice x5 -> x3, local copies, waits for them, and re-layouts: 3.37 us -> 1.42 us  [rows_of(): return lax.dynamic_slice_in_dim(x, start, HALF, axis)]
    all_to_all x3, waiting for transfers between devices: 22.4 us -> 23.8 us  [exchange(): return lax.all_to_all(x, axes, split_axis=0, concat_axis=0, tiled=True)]
    unnamed x4 -> x2, local copies, waits for them, and re-layouts: 4.57 us -> 3.34 us
    pallas_call x8 -> x7, Pallas kernels: 6.45 us -> 6.4 us  [call(): pl.pallas_call(kernel, out_shape=shapes, in_specs=specs, scratch_shapes=s...]
  transfers between devices with their start and end apart: 12 -> 15, of which waited for: 6 -> 6; matrix products, arithmetic and copies ran while one was open for 7% -> 5% of each run, Pallas kernels for 1% -> 1%
where the time goes in v10:
time: 112 us; the launch traced here: 111 us
  starting transfers between devices  37.4 us (33%)
  blocking collectives  30.2 us (27%)
  waiting for transfers between devices  27.3 us (24%)
  local copies, waits for them, and re-layouts  6.97 us (6%)
  Pallas kernels  6.4 us (6%)
  other arithmetic  1.92 us (2%)
    all_to_all x2, blocking collectives, exchange(): return lax.all_to_all(x, axes, split_axis=0, concat_axis=0, tiled=True)  30.2 us
    all_to_all x3, waiting for transfers between devices, exchange(): return lax.all_to_all(x, axes, split_axis=0, concat_axis=0, tiled=True)  23.8 us
    all_to_all x3, starting transfers between devices, exchange(): return lax.all_to_all(x, axes, split_axis=0, concat_axis=0, tiled=True)  23.5 us
    ppermute x8, starting transfers between devices, swap(): return lax.ppermute(x, CORE, [(0, 1), (1, 0)])  9.71 us
    pallas_call x7, Pallas kernels, call(): pl.pallas_call(kernel, out_shape=shapes, in_specs=specs, scratch_shapes=s...  6.4 us
    unnamed x2, local copies, waits for them, and re-layouts  3.34 us
  transfers between devices with their start and end apart: 15, of which 6 were waited for; matrix products, arithmetic and copies ran while one was open for 5% of the time, Pallas kernels for 1%

profile of v10, /device:TPU:1, one launch (start us, length us, event | category | flops | bytes accessed | tf_op | source)
XLA Modules:
  0.0 111.5 jit_solution(2161295919618485474)
XLA Ops:
  0.6 3.3 %collective-permute-start.1 = (f32[1,64]{1,0:T(1,128)}, f32[1,64]{1,0:T(1,128)S(1)}, u32[]{:S(2)}, u32[]{:S(2)}) collective-permute-start(f32[1,64]{1,0:T(1,128)} %param.18), channel_id=1, source_target_pairs={{0,1},{1,0},{2,3},{3,2},{4,5},{5,4},{6,7},{7,6},{8,9},{9,8},{10,11... | collective-permute-start | bytes 776 | tf_op jit(solution)/shard_map/ppermute | solution.py:26
  4.1 0.7 fusion.2
  4.8 0.5 collective-permute-done
  5.4 0.6 broadcast_in_dim.27
  6.1 12.6 %all-to-all-start = ((bf16[64,4,128]{2,1,0:T(4,128)(2,1)}), bf16[64,4,128]{2,1,0:T(4,128)(2,1)S(1)}, u32[]{:S(2)}, u32[]{:S(2)}) async-start(bf16[64,4,128]{2,1,0:T(4,128)(2,1)} %broadcast_in_dim.27), calls=%async_computation | async-start | bytes 131072 | tf_op jit(solution)/shard_map/all_to_all | solution.py:30
  18.6 0.5 collective-permute-start.4
  19.2 1.0 collective-permute-start.2
  20.3 1.0 collective-permute-start.3
  21.3 0.7 dynamic_slice.36
  22.0 0.7 fusion.8
  23.0 6.9 %all-to-all-done = bf16[64,4,128]{2,1,0:T(4,128)(2,1)S(1)} async-done(((bf16[64,4,128]{2,1,0:T(4,128)(2,1)}), bf16[64,4,128]{2,1,0:T(4,128)(2,1)S(1)}, u32[]{:S(2)}, u32[]{:S(2)}) %all-to-all-start) | async-done | bytes 65568 | tf_op jit(solution)/shard_map/all_to_all | solution.py:30
  29.9 1.2 %shard_map.122 = bf16[64,8,128]{2,1,0:T(8,128)(2,1)} custom-call(s32[1]{0:T(128)} %bitcast.1.core_ref, bf16[256,128]{1,0:T(8,128)(2,1)S(1)} %bitcast.24, bf16[8,32,1024]{2,1,0:T(8,128)(2,1)S(1)} %collective-permute-done.2.k_ref, bf16[8,32,1024]{2,1,0:T(8,128)(2,1)S(1)} %collective-permute-done.3.v_ref, ...), custom_call_target="tpu_custom_call" | custom-call | flops 33554432 | bytes 2097152 | tf_op jit(solution)/shard_map/pallas_call | solution.py:49
  31.1 1.3 %collective-permute-start.7 = (bf16[64,8192]{1,0:T(8,128)(2,1)}, bf16[64,8192]{1,0:T(8,128)(2,1)S(1)}, u32[]{:S(2)}, u32[]{:S(2)}) collective-permute-start(bf16[64,8192]{1,0:T(8,128)(2,1)} %bitcast.25), channel_id=1, source_target_pairs={{0,1},{1,0},{2,3},{3,2},{4,5},{5,4},{6,7},{7,6},{8,9},{9,8},{10,11... | collective-permute-start | bytes 3145736 | tf_op jit(solution)/shard_map/ppermute | solution.py:26
  32.4 1.2 %collective-permute-start.6 = (bf16[64,8192]{1,0:T(8,128)(2,1)}, bf16[64,8192]{1,0:T(8,128)(2,1)S(1)}, u32[]{:S(2)}, u32[]{:S(2)}) collective-permute-start(bf16[64,8192]{1,0:T(8,128)(2,1)} %bitcast.26), channel_id=1, source_target_pairs={{0,0},{1,1},{2,2},{3,3},{4,4},{5,5},{6,6},{7,7},{8,8},{9,9},{10,10... | collective-permute-start | bytes 3145736 | tf_op jit(solution)/shard_map/ppermute | solution.py:266
  33.7 4.8 %all-to-all-start.1 = ((bf16[64,8,128]{2,1,0:T(8,128)(2,1)}), bf16[64,8,128]{2,1,0:T(8,128)(2,1)S(1)}, u32[]{:S(2)}, u32[]{:S(2)}) async-start(bf16[64,8,128]{2,1,0:T(8,128)(2,1)} %shard_map.122), calls=%async_computation.1 | async-start | bytes 262144 | tf_op jit(solution)/shard_map/all_to_all | solution.py:30
  38.9 0.7 fusion.4
  39.6 0.8 constant_dynamic-slice_fusion.3
  40.3 0.7 fusion.7.action_ref
  41.1 9.1 %all-to-all-done.1.got_ref = bf16[64,8,128]{2,1,0:T(8,128)(2,1)S(1)} async-done(((bf16[64,8,128]{2,1,0:T(8,128)(2,1)}), bf16[64,8,128]{2,1,0:T(8,128)(2,1)S(1)}, u32[]{:S(2)}, u32[]{:S(2)}) %all-to-all-start.1) | async-done | bytes 131104 | tf_op jit(solution)/shard_map/all_to_all | solution.py:30
  51.2 15.4 %all_to_all.25.got_ref = bf16[64,4,128]{2,1,0:T(4,128)(2,1)S(1)} all-to-all(bf16[64,4,128]{2,1,0:T(4,128)(2,1)S(1)} %fusion.1), channel_id=1, replica_groups=mesh['role'=2,'grp'=2,'tp_0'=4,'tp_1'=8,'tp_2'=2] {'grp','tp_0','tp_1'}, dimensions={0} | all-to-all | bytes 131072 | tf_op jit(solution)/shard_map/all_to_all | solution.py:30
  66.7 14.8 %all_to_all.26.near_ref = bf16[64,4,128]{2,1,0:T(4,128)(2,1)S(1)} all-to-all(bf16[64,4,128]{2,1,0:T(4,128)(2,1)S(1)} %shard_map.124), channel_id=1, replica_groups=mesh['role'=2,'grp'=2,'tp_0'=4,'tp_1'=8,'tp_2'=2] {'grp','tp_0','tp_1'}, dimensions={0} | all-to-all | bytes 131072 | tf_op jit(solution)/shard_map/all_to_all | solution.py:30
  81.5 3.7 %collective-permute-start.9 = (bf16[64,4,128]{2,1,0:T(4,128)(2,1)S(1)}, bf16[64,4,128]{2,1,0:T(4,128)(2,1)S(1)}, u32[]{:S(2)}, u32[]{:S(2)}) collective-permute-start(bf16[64,4,128]{2,1,0:T(4,128)(2,1)S(1)} %all_to_all.26.near_ref), channel_id=1, source_target_pairs={{0,1},{1,0},{2,3},{3,2},{4,5},{5,4},{6,7},{7,6},{8,9},{9,8},{10,11... | collective-permute-start | bytes 196616 | tf_op jit(solution)/shard_map/ppermute | solution.py:26
  85.2 3.3 %copy-done = bf16[8192,501]{0,1:T(8,128)(2,1)S(1)} copy-done((bf16[8192,501]{0,1:T(8,128)(2,1)S(1)}, bf16[8192,501]{0,1:T(8,128)(2,1)}, u32[]{:S(2)}) %copy-start) | copy-done | bytes 8208408
  88.6 0.5 shard_map.125.head_ref
  89.1 2.7 %shard_map.126 = (f32[8,128]{1,0:T(8,128)S(1)}, bf16[8,128]{1,0:T(8,128)(2,1)S(1)}) custom-call(s32[1]{0:T(128)} %bitcast.1.core_ref, s32[1]{0:T(128)} %bitcast.2.chip_ref, bf16[64,4,128]{2,1,0:T(4,128)(2,1)S(1)} %all_to_all.26.near_ref, bf16[64,4,128]{2,1,0:T(4,128)(2,1)S(1)} %collective-permute-done.9.far_ref, ...), custom_call_target="tpu_custom_call" | custom-call | flops 65667072 | bytes 4104192 | tf_op jit(solution)/shard_map/pallas_call | solution.py:49
  92.1 1.2 %collective-permute-done.10.far_ref = f32[8,128]{1,0:T(8,128)S(1)} collective-permute-done((f32[8,128]{1,0:T(8,128)S(1)}, f32[8,128]{1,0:T(8,128)S(1)}, u32[]{:S(2)}, u32[]{:S(2)}) %collective-permute-start.10) | collective-permute-done | bytes 4128 | tf_op jit(solution)/shard_map/ppermute | solution.py:26
  93.2 0.7 shard_map.127
  94.0 6.1 %all-to-all-start.4 = ((f32[128,1,128]{2,1,0:T(1,128)}), f32[128,1,128]{2,1,0:T(1,128)S(1)}, u32[]{:S(2)}, u32[]{:S(2)}) async-start(f32[128,1,128]{2,1,0:T(1,128)} %shard_map.127), calls=%async_computation.4 | async-start | bytes 131072 | tf_op jit(solution)/shard_map/all_to_all | solution.py:30
  100.2 0.9 collective-permute-start.11
  101.1 1.8 %collective-permute-done.11.normed_ref = bf16[8,64]{1,0:T(8,128)(2,1)S(1)} collective-permute-done((bf16[8,64]{1,0:T(8,128)(2,1)S(1)}, bf16[8,64]{1,0:T(8,128)(2,1)S(1)}, u32[]{:S(2)}, u32[]{:S(2)}) %collective-permute-start.11) | collective-permute-done | bytes 1056 | tf_op jit(solution)/shard_map/ppermute | solution.py:323
  102.9 7.8 %all-to-all-done.4.heard_ref = f32[128,1,128]{2,1,0:T(1,128)S(1)} async-done(((f32[128,1,128]{2,1,0:T(1,128)}), f32[128,1,128]{2,1,0:T(1,128)S(1)}, u32[]{:S(2)}, u32[]{:S(2)}) %all-to-all-start.4) | async-done | bytes 65568 | tf_op jit(solution)/shard_map/all_to_all | solution.py:30
  110.7 0.7 shard_map.128
  (33 shorter events, 2.4 us)
Async XLA Ops:
  0.6 18.0 %collective-permute-start.1 = (f32[1,64]{1,0:T(1,128)}, f32[1,64]{1,0:T(1,128)S(1)}, u32[]{:S(2)}, u32[]{:S(2)}) collective-permute-start(f32[1,64]{1,0:T(1,128)} %param.18), channel_id=1, source_target_pairs={{0,1},{1,0},{2,3},{3,2},{4,5},{5,4},{6,7},{7,6},{8,9},{9,8},{10,11... | collective-permute-start | bytes 776 | tf_op jit(solution)/shard_map/ppermute | solution.py:26
  4.0 1.4 %collective-permute-start = (bf16[2,8,64]{2,1,0:T(8,128)(2,1)}, bf16[2,8,64]{2,1,0:T(8,128)(2,1)S(1)}, u32[]{:S(2)}, u32[]{:S(2)}) collective-permute-start(bf16[2,8,64]{2,1,0:T(8,128)(2,1)} %param.11), channel_id=1, source_target_pairs={{0,1},{1,0},{2,3},{3,2},{4,5},{5,4},{6,7},{7,6},{8,9},{9,8},{10,11... | collective-permute-start | bytes 6152 | tf_op jit(solution)/shard_map/ppermute | solution.py:26
  6.1 23.8 %all-to-all-start = ((bf16[64,4,128]{2,1,0:T(4,128)(2,1)}), bf16[64,4,128]{2,1,0:T(4,128)(2,1)S(1)}, u32[]{:S(2)}, u32[]{:S(2)}) async-start(bf16[64,4,128]{2,1,0:T(4,128)(2,1)} %broadcast_in_dim.27), calls=%async_computation | async-start | bytes 131072 | tf_op jit(solution)/shard_map/all_to_all | solution.py:30
  18.6 11.3 %collective-permute-start.4 = (bf16[8,32,1024]{2,1,0:T(8,128)(2,1)}, bf16[8,32,1024]{2,1,0:T(8,128)(2,1)S(1)}, u32[]{:S(2)}, u32[]{:S(2)}) collective-permute-start(bf16[8,32,1024]{2,1,0:T(8,128)(2,1)} %param.14), channel_id=1, source_target_pairs={{0,1},{1,0},{2,3},{3,2},{4,5},{5,4},{6,7},{7,6},{8,9},{9,8},{10,11... | collective-permute-start | bytes 1572872 | tf_op jit(solution)/shard_map/ppermute | solution.py:26
  19.2 10.7 %collective-permute-start.2 = (bf16[8,32,1024]{2,1,0:T(8,128)(2,1)}, bf16[8,32,1024]{2,1,0:T(8,128)(2,1)S(1)}, u32[]{:S(2)}, u32[]{:S(2)}) collective-permute-start(bf16[8,32,1024]{2,1,0:T(8,128)(2,1)} %param.14), channel_id=1, source_target_pairs={{0,0},{1,1},{2,2},{3,3},{4,4},{5,5},{6,6},{7,7},{8,8},{9,9},{10,10... | collective-permute-start | bytes 1572872 | tf_op jit(solution)/shard_map/ppermute | solution.py:235
  20.2 9.7 %collective-permute-start.5 = (bf16[8,32,1024]{2,1,0:T(8,128)(2,1)}, bf16[8,32,1024]{2,1,0:T(8,128)(2,1)S(1)}, u32[]{:S(2)}, u32[]{:S(2)}) collective-permute-start(bf16[8,32,1024]{2,1,0:T(8,128)(2,1)} %param.15), channel_id=1, source_target_pairs={{0,1},{1,0},{2,3},{3,2},{4,5},{5,4},{6,7},{7,6},{8,9},{9,8},{10,11... | collective-permute-start | bytes 1572872 | tf_op jit(solution)/shard_map/ppermute | solution.py:26
  20.3 9.6 %collective-permute-start.3 = (bf16[8,32,1024]{2,1,0:T(8,128)(2,1)}, bf16[8,32,1024]{2,1,0:T(8,128)(2,1)S(1)}, u32[]{:S(2)}, u32[]{:S(2)}) collective-permute-start(bf16[8,32,1024]{2,1,0:T(8,128)(2,1)} %param.15), channel_id=1, source_target_pairs={{0,0},{1,1},{2,2},{3,3},{4,4},{5,5},{6,6},{7,7},{8,8},{9,9},{10,10... | collective-permute-start | bytes 1572872 | tf_op jit(solution)/shard_map/ppermute | solution.py:235
  31.1 19.6 %collective-permute-start.7 = (bf16[64,8192]{1,0:T(8,128)(2,1)}, bf16[64,8192]{1,0:T(8,128)(2,1)S(1)}, u32[]{:S(2)}, u32[]{:S(2)}) collective-permute-start(bf16[64,8192]{1,0:T(8,128)(2,1)} %bitcast.25), channel_id=1, source_target_pairs={{0,1},{1,0},{2,3},{3,2},{4,5},{5,4},{6,7},{7,6},{8,9},{9,8},{10,11... | collective-permute-start | bytes 3145736 | tf_op jit(solution)/shard_map/ppermute | solution.py:26
  32.4 18.5 %collective-permute-start.6 = (bf16[64,8192]{1,0:T(8,128)(2,1)}, bf16[64,8192]{1,0:T(8,128)(2,1)S(1)}, u32[]{:S(2)}, u32[]{:S(2)}) collective-permute-start(bf16[64,8192]{1,0:T(8,128)(2,1)} %bitcast.26), channel_id=1, source_target_pairs={{0,0},{1,1},{2,2},{3,3},{4,4},{5,5},{6,6},{7,7},{8,8},{9,9},{10,10... | collective-permute-start | bytes 3145736 | tf_op jit(solution)/shard_map/ppermute | solution.py:266
  33.7 16.6 %all-to-all-start.1 = ((bf16[64,8,128]{2,1,0:T(8,128)(2,1)}), bf16[64,8,128]{2,1,0:T(8,128)(2,1)S(1)}, u32[]{:S(2)}, u32[]{:S(2)}) async-start(bf16[64,8,128]{2,1,0:T(8,128)(2,1)} %shard_map.122), calls=%async_computation.1 | async-start | bytes 262144 | tf_op jit(solution)/shard_map/all_to_all | solution.py:30
  38.5 2.6 %collective-permute-start.8 = (bf16[2,8,64]{2,1,0:T(8,128)(2,1)}, bf16[2,8,64]{2,1,0:T(8,128)(2,1)S(1)}, u32[]{:S(2)}, u32[]{:S(2)}) collective-permute-start(bf16[2,8,64]{2,1,0:T(8,128)(2,1)} %param.20), channel_id=1, source_target_pairs={{0,1},{1,0},{2,3},{3,2},{4,5},{5,4},{6,7},{7,6},{8,9},{9,8},{10,11... | collective-permute-start | bytes 6152 | tf_op jit(solution)/shard_map/ppermute | solution.py:26
  81.5 7.6 %collective-permute-start.9 = (bf16[64,4,128]{2,1,0:T(4,128)(2,1)S(1)}, bf16[64,4,128]{2,1,0:T(4,128)(2,1)S(1)}, u32[]{:S(2)}, u32[]{:S(2)}) collective-permute-start(bf16[64,4,128]{2,1,0:T(4,128)(2,1)S(1)} %all_to_all.26.near_ref), channel_id=1, source_target_pairs={{0,1},{1,0},{2,3},{3,2},{4,5},{5,4},{6,7},{7,6},{8,9},{9,8},{10,11... | collective-permute-start | bytes 196616 | tf_op jit(solution)/shard_map/ppermute | solution.py:26
  85.2 3.3 %copy-start = (bf16[8192,501]{0,1:T(8,128)(2,1)S(1)}, bf16[8192,501]{0,1:T(8,128)(2,1)}, u32[]{:S(2)}) copy-start(bf16[8192,501]{0,1:T(8,128)(2,1)} %param.19) | copy-start | bytes 24625156
  91.8 1.4 %collective-permute-start.10 = (f32[8,128]{1,0:T(8,128)S(1)}, f32[8,128]{1,0:T(8,128)S(1)}, u32[]{:S(2)}, u32[]{:S(2)}) collective-permute-start(f32[8,128]{1,0:T(8,128)S(1)} %get-tuple-element.36.near_ref), channel_id=1, source_target_pairs={{0,1},{1,0},{2,3},{3,2},{4,5},{5,4},{6,7},{7,6},{8,9},{9,8},{10,11... | collective-permute-start | bytes 12296 | tf_op jit(solution)/shard_map/ppermute | solution.py:26
  94.0 16.8 %all-to-all-start.4 = ((f32[128,1,128]{2,1,0:T(1,128)}), f32[128,1,128]{2,1,0:T(1,128)S(1)}, u32[]{:S(2)}, u32[]{:S(2)}) async-start(f32[128,1,128]{2,1,0:T(1,128)} %shard_map.127), calls=%async_computation.4 | async-start | bytes 131072 | tf_op jit(solution)/shard_map/all_to_all | solution.py:30
  100.2 2.8 %collective-permute-start.11 = (bf16[8,64]{1,0:T(8,128)(2,1)S(1)}, bf16[8,64]{1,0:T(8,128)(2,1)S(1)}, u32[]{:S(2)}, u32[]{:S(2)}) collective-permute-start(bf16[8,64]{1,0:T(8,128)(2,1)S(1)} %slice_select_fusion), channel_id=1, source_target_pairs={{0,128},{128,0},{1,129},{129,1},{2,130},{130,2},{3,131},{131,3},{4... | collective-permute-start | bytes 3080 | tf_op jit(solution)/shard_map/ppermute | solution.py:323

commit v11 on v9

--- a/solution.py
+++ b/solution.py
@@ -148,7 +148,7 @@
 
 
 def head_kernel(
-    core_ref, chip_ref, near_ref, far_ref, got_ref, head_ref, action_ref, out_ref, own_ref, u_ref
+    core_ref, chip_ref, step_ref, base_ref, near_ref, far_ref, got_ref, head_ref, action_ref, out_ref, own_ref, u_ref
 ):
     near, far = near_ref[...].astype(F32), far_ref[...].astype(F32)
     first = core_ref[0] == 0
@@ -164,12 +164,13 @@
     u = jnp.concatenate([u_ref[i] for i in range(CHIPS)], 1)
     logits = lax.dot_general(head_ref[...], u, NT, preferred_element_type=F32)
     ids = lax.broadcasted_iota(jnp.int32, logits.shape, 0)
+    action = jnp.where(step_ref[0] == 0, action_ref[0:1, :], action_ref[1:2, :])
     high = jnp.max(logits, 0, keepdims=True)
     out_ref[...] = jnp.zeros_like(out_ref)
     out_ref[0:1, 0:8] = high
     out_ref[1:2, 0:8] = jnp.sum(jnp.exp(logits - high), 0, keepdims=True)
     out_ref[2:3, 0:8] = jnp.sum(
-        jnp.where(ids == action_ref[...], logits, 0.0), 0, keepdims=True
+        jnp.where(ids + base_ref[0] == action, logits, 0.0), 0, keepdims=True
     )
 
 
@@ -287,9 +288,7 @@
     share = jnp.dot(near, w_mine, preferred_element_type=F32)
     share = share + jnp.dot(far, w_far, preferred_element_type=F32)
     share = share.astype(BF).reshape(HALF, CHIPS, HEAD_SIZE).transpose(1, 0, 2)
-    action = lax.dynamic_index_in_dim(actions, step, 0, keepdims=True)
-    action = action - place * head.shape[1]
-    share, r_chip, action = lax.optimization_barrier((share, r_chip, action))
+    share, r_chip = lax.optimization_barrier((share, r_chip))
     shares = exchange(share, CHIP)
     sent = call(
         state_kernel,
@@ -306,16 +305,18 @@
     local, own = call(
         head_kernel,
         (jax.ShapeDtypeStruct((8, 128), F32), jax.ShapeDtypeStruct((8, HEAD_SIZE), BF)),
-        [SMEM] * 2 + [VMEM] * 5,
+        [SMEM] * 4 + [VMEM] * 5,
         24,
         2 * 8 * D * head.shape[1],
         core[None],
         chip[None],
+        step[None],
+        (place * head.shape[1])[None],
         mine,
         swap(mine),
         got,
         head_t,
-        action,
+        actions,
         scratch=[pltpu.VMEM((CHIPS, 8, HEAD_SIZE), BF)],
     )
     own = jnp.where(core == 0, own[:, :64], own[:, 64:])

time: 111 us -> 111 us (level)
    unnamed x4 -> x6, local copies, waits for them, and re-layouts: 4.57 us -> 4.69 us
  transfers between devices with their start and end apart: 12 -> 12, of which waited for: 6 -> 6; matrix products, arithmetic and copies ran while one was open for 7% -> 6% of each run, Pallas kernels for 1% -> 1%
where the time goes in v11:
time: 111 us; the launch traced here: 110 us
  starting transfers between devices  34.1 us (31%)
  blocking collectives  30.3 us (27%)
  waiting for transfers between devices  26.6 us (24%)
  local copies, waits for them, and re-layouts  10.3 us (9%)
  Pallas kernels  6.42 us (6%)
  other arithmetic  1.23 us (1%)
    all_to_all x2, blocking collectives, exchange(): return lax.all_to_all(x, axes, split_axis=0, concat_axis=0, tiled=True)  30.3 us
    all_to_all x3, starting transfers between devices, exchange(): return lax.all_to_all(x, axes, split_axis=0, concat_axis=0, tiled=True)  23.3 us
    all_to_all x3, waiting for transfers between devices, exchange(): return lax.all_to_all(x, axes, split_axis=0, concat_axis=0, tiled=True)  23.1 us
    ppermute x8, starting transfers between devices, swap(): return lax.ppermute(x, CORE, [(0, 1), (1, 0)])  9.82 us
    pallas_call x8, Pallas kernels, call(): pl.pallas_call(kernel, out_shape=shapes, in_specs=specs, scratch_shapes=s...  6.42 us
    unnamed x6, local copies, waits for them, and re-layouts  4.69 us
    dynamic_slice x5, local copies, waits for them, and re-layouts, rows_of(): return lax.dynamic_slice_in_dim(x, start, HALF, axis)  3.38 us
  transfers between devices with their start and end apart: 12, of which 6 were waited for; matrix products, arithmetic and copies ran while one was open for 6% of the time, Pallas kernels for 1%

profile of v11, /device:TPU:1, one launch (start us, length us, event | category | flops | bytes accessed | tf_op | source)
XLA Modules:
  0.0 110.1 jit_solution(7648620389011379950)
XLA Ops:
  0.6 3.3 %collective-permute-start.1 = (f32[1,64]{1,0:T(1,128)}, f32[1,64]{1,0:T(1,128)S(1)}, u32[]{:S(2)}, u32[]{:S(2)}) collective-permute-start(f32[1,64]{1,0:T(1,128)} %param.18), channel_id=1, source_target_pairs={{0,1},{1,0},{2,3},{3,2},{4,5},{5,4},{6,7},{7,6},{8,9},{9,8},{10,11... | collective-permute-start | bytes 776 | tf_op jit(solution)/shard_map/ppermute | solution.py:26
  4.1 0.7 fusion.2
  4.8 0.5 collective-permute-done
  5.4 0.6 broadcast_in_dim.32
  6.1 12.5 %all-to-all-start = ((bf16[64,4,128]{2,1,0:T(4,128)(2,1)}), bf16[64,4,128]{2,1,0:T(4,128)(2,1)S(1)}, u32[]{:S(2)}, u32[]{:S(2)}) async-start(bf16[64,4,128]{2,1,0:T(4,128)(2,1)} %broadcast_in_dim.32), calls=%async_computation | async-start | bytes 131072 | tf_op jit(solution)/shard_map/all_to_all | solution.py:30
  18.6 1.0 constant_dynamic-slice_fusion.5.k_ref
  19.6 0.5 collective-permute-start.2
  20.1 0.7 dynamic_slice.40
  20.9 0.7 fusion.7
  21.9 1.0 constant_dynamic-slice_fusion.4.v_ref
  22.9 7.0 %all-to-all-done = bf16[64,4,128]{2,1,0:T(4,128)(2,1)S(1)} async-done(((bf16[64,4,128]{2,1,0:T(4,128)(2,1)}), bf16[64,4,128]{2,1,0:T(4,128)(2,1)S(1)}, u32[]{:S(2)}, u32[]{:S(2)}) %all-to-all-start) | async-done | bytes 65568 | tf_op jit(solution)/shard_map/all_to_all | solution.py:30
  29.9 1.2 %shard_map.122 = bf16[64,8,128]{2,1,0:T(8,128)(2,1)} custom-call(s32[1]{0:T(128)} %bitcast.1.core_ref, bf16[256,128]{1,0:T(8,128)(2,1)S(1)} %bitcast.27, bf16[4,32,1024]{2,1,0:T(8,128)(2,1)S(1)} %constant_dynamic-slice_fusion.5.k_ref, bf16[4,32,1024]{2,1,0:T(8,128)(2,1)S(1)} %constant_dynamic-slice_fusion.4.v_ref, ...), custom_call_target="tpu_custom_call" | custom-call | flops 33554432 | bytes 2097152 | tf_op jit(solution)/shard_map/pallas_call | solution.py:49
  31.1 1.3 %collective-permute-start.4 = (bf16[64,8192]{1,0:T(8,128)(2,1)}, bf16[64,8192]{1,0:T(8,128)(2,1)S(1)}, u32[]{:S(2)}, u32[]{:S(2)}) collective-permute-start(bf16[64,8192]{1,0:T(8,128)(2,1)} %bitcast.25), channel_id=1, source_target_pairs={{0,1},{1,0},{2,3},{3,2},{4,5},{5,4},{6,7},{7,6},{8,9},{9,8},{10,11... | collective-permute-start | bytes 3145736 | tf_op jit(solution)/shard_map/ppermute | solution.py:26
  32.4 4.7 %all-to-all-start.1 = ((bf16[64,8,128]{2,1,0:T(8,128)(2,1)}), bf16[64,8,128]{2,1,0:T(8,128)(2,1)S(1)}, u32[]{:S(2)}, u32[]{:S(2)}) async-start(bf16[64,8,128]{2,1,0:T(8,128)(2,1)} %shard_map.122), calls=%async_computation.1 | async-start | bytes 262144 | tf_op jit(solution)/shard_map/all_to_all | solution.py:30
  37.1 0.5 collective-permute-start.5
  37.6 0.8 constant_dynamic-slice_fusion.2
  38.4 0.7 fusion.4
  39.1 1.2 %copy-done.1 = bf16[1,64,8192]{2,1,0:T(8,128)(2,1)S(1)} copy-done((bf16[1,64,8192]{2,1,0:T(8,128)(2,1)S(1)}, bf16[1,64,8192]{2,1,0:T(8,128)(2,1)}, u32[]{:S(2)}) %copy-start.1) | copy-done | bytes 1048600
  40.5 8.3 %all-to-all-done.1.got_ref = bf16[64,8,128]{2,1,0:T(8,128)(2,1)S(1)} async-done(((bf16[64,8,128]{2,1,0:T(8,128)(2,1)}), bf16[64,8,128]{2,1,0:T(8,128)(2,1)S(1)}, u32[]{:S(2)}, u32[]{:S(2)}) %all-to-all-start.1) | async-done | bytes 131104 | tf_op jit(solution)/shard_map/all_to_all | solution.py:30
  49.7 15.5 %all_to_all.25.got_ref = bf16[64,4,128]{2,1,0:T(4,128)(2,1)S(1)} all-to-all(bf16[64,4,128]{2,1,0:T(4,128)(2,1)S(1)} %fusion.1), channel_id=1, replica_groups=mesh['role'=2,'grp'=2,'tp_0'=4,'tp_1'=8,'tp_2'=2] {'grp','tp_0','tp_1'}, dimensions={0} | all-to-all | bytes 131072 | tf_op jit(solution)/shard_map/all_to_all | solution.py:30
  65.3 14.8 %all_to_all.26.near_ref = bf16[64,4,128]{2,1,0:T(4,128)(2,1)S(1)} all-to-all(bf16[64,4,128]{2,1,0:T(4,128)(2,1)S(1)} %shard_map.125), channel_id=1, replica_groups=mesh['role'=2,'grp'=2,'tp_0'=4,'tp_1'=8,'tp_2'=2] {'grp','tp_0','tp_1'}, dimensions={0} | all-to-all | bytes 131072 | tf_op jit(solution)/shard_map/all_to_all | solution.py:30
  80.1 3.7 %collective-permute-start.6 = (bf16[64,4,128]{2,1,0:T(4,128)(2,1)S(1)}, bf16[64,4,128]{2,1,0:T(4,128)(2,1)S(1)}, u32[]{:S(2)}, u32[]{:S(2)}) collective-permute-start(bf16[64,4,128]{2,1,0:T(4,128)(2,1)S(1)} %all_to_all.26.near_ref), channel_id=1, source_target_pairs={{0,1},{1,0},{2,3},{3,2},{4,5},{5,4},{6,7},{7,6},{8,9},{9,8},{10,11... | collective-permute-start | bytes 196616 | tf_op jit(solution)/shard_map/ppermute | solution.py:26
  83.8 3.3 %copy-done = bf16[8192,501]{0,1:T(8,128)(2,1)S(1)} copy-done((bf16[8192,501]{0,1:T(8,128)(2,1)S(1)}, bf16[8192,501]{0,1:T(8,128)(2,1)}, u32[]{:S(2)}) %copy-start) | copy-done | bytes 8208408
  87.2 0.5 shard_map.126.head_ref
  87.8 2.6 %shard_map.127 = (f32[8,128]{1,0:T(8,128)S(1)}, bf16[8,128]{1,0:T(8,128)(2,1)S(1)}) custom-call(s32[1]{0:T(128)} %bitcast.1.core_ref, s32[1]{0:T(128)} %bitcast.2.chip_ref, s32[1]{0:T(128)} %bitcast.3.step_ref, s32[1]{0:T(128)} %bitcast.4.base_ref, bf16[64,4,128]{2,1,0:T(4,128)(2,1)S(1)} %all_to_all.26.near_ref, ...), custom_call_target="tpu_custom_call" | custom-call | flops 65667072 | bytes 4104192 | tf_op jit(solution)/shard_map/pallas_call | solution.py:49
  90.8 1.2 %collective-permute-done.7.far_ref = f32[8,128]{1,0:T(8,128)S(1)} collective-permute-done((f32[8,128]{1,0:T(8,128)S(1)}, f32[8,128]{1,0:T(8,128)S(1)}, u32[]{:S(2)}, u32[]{:S(2)}) %collective-permute-start.7) | collective-permute-done | bytes 4128 | tf_op jit(solution)/shard_map/ppermute | solution.py:26
  91.9 0.7 shard_map.128
  92.7 6.1 %all-to-all-start.4 = ((f32[128,1,128]{2,1,0:T(1,128)}), f32[128,1,128]{2,1,0:T(1,128)S(1)}, u32[]{:S(2)}, u32[]{:S(2)}) async-start(f32[128,1,128]{2,1,0:T(1,128)} %shard_map.128), calls=%async_computation.4 | async-start | bytes 131072 | tf_op jit(solution)/shard_map/all_to_all | solution.py:30
  98.9 0.9 collective-permute-start.8
  99.8 1.8 %collective-permute-done.8.normed_ref = bf16[8,64]{1,0:T(8,128)(2,1)S(1)} collective-permute-done((bf16[8,64]{1,0:T(8,128)(2,1)S(1)}, bf16[8,64]{1,0:T(8,128)(2,1)S(1)}, u32[]{:S(2)}, u32[]{:S(2)}) %collective-permute-start.8) | collective-permute-done | bytes 1056 | tf_op jit(solution)/shard_map/ppermute | solution.py:323
  101.6 7.8 %all-to-all-done.4.heard_ref = f32[128,1,128]{2,1,0:T(1,128)S(1)} async-done(((f32[128,1,128]{2,1,0:T(1,128)}), f32[128,1,128]{2,1,0:T(1,128)S(1)}, u32[]{:S(2)}, u32[]{:S(2)}) %all-to-all-start.4) | async-done | bytes 65568 | tf_op jit(solution)/shard_map/all_to_all | solution.py:30
  109.4 0.7 shard_map.129
  (33 shorter events, 2.3 us)
Async XLA Ops:
  0.6 18.0 %collective-permute-start.1 = (f32[1,64]{1,0:T(1,128)}, f32[1,64]{1,0:T(1,128)S(1)}, u32[]{:S(2)}, u32[]{:S(2)}) collective-permute-start(f32[1,64]{1,0:T(1,128)} %param.18), channel_id=1, source_target_pairs={{0,1},{1,0},{2,3},{3,2},{4,5},{5,4},{6,7},{7,6},{8,9},{9,8},{10,11... | collective-permute-start | bytes 776 | tf_op jit(solution)/shard_map/ppermute | solution.py:26
  4.0 1.4 %collective-permute-start = (bf16[2,8,64]{2,1,0:T(8,128)(2,1)}, bf16[2,8,64]{2,1,0:T(8,128)(2,1)S(1)}, u32[]{:S(2)}, u32[]{:S(2)}) collective-permute-start(bf16[2,8,64]{2,1,0:T(8,128)(2,1)} %param.11), channel_id=1, source_target_pairs={{0,1},{1,0},{2,3},{3,2},{4,5},{5,4},{6,7},{7,6},{8,9},{9,8},{10,11... | collective-permute-start | bytes 6152 | tf_op jit(solution)/shard_map/ppermute | solution.py:26
  6.1 23.8 %all-to-all-start = ((bf16[64,4,128]{2,1,0:T(4,128)(2,1)}), bf16[64,4,128]{2,1,0:T(4,128)(2,1)S(1)}, u32[]{:S(2)}, u32[]{:S(2)}) async-start(bf16[64,4,128]{2,1,0:T(4,128)(2,1)} %broadcast_in_dim.32), calls=%async_computation | async-start | bytes 131072 | tf_op jit(solution)/shard_map/all_to_all | solution.py:30
  19.6 10.3 %collective-permute-start.2 = (bf16[8,32,1024]{2,1,0:T(8,128)(2,1)}, bf16[8,32,1024]{2,1,0:T(8,128)(2,1)S(1)}, u32[]{:S(2)}, u32[]{:S(2)}) collective-permute-start(bf16[8,32,1024]{2,1,0:T(8,128)(2,1)} %param.14), channel_id=1, source_target_pairs={{0,1},{1,0},{2,3},{3,2},{4,5},{5,4},{6,7},{7,6},{8,9},{9,8},{10,11... | collective-permute-start | bytes 1572872 | tf_op jit(solution)/shard_map/ppermute | solution.py:26
  20.9 9.0 %collective-permute-start.3 = (bf16[8,32,1024]{2,1,0:T(8,128)(2,1)}, bf16[8,32,1024]{2,1,0:T(8,128)(2,1)S(1)}, u32[]{:S(2)}, u32[]{:S(2)}) collective-permute-start(bf16[8,32,1024]{2,1,0:T(8,128)(2,1)} %param.15), channel_id=1, source_target_pairs={{0,1},{1,0},{2,3},{3,2},{4,5},{5,4},{6,7},{7,6},{8,9},{9,8},{10,11... | collective-permute-start | bytes 1572872 | tf_op jit(solution)/shard_map/ppermute | solution.py:26
  31.1 18.1 %collective-permute-start.4 = (bf16[64,8192]{1,0:T(8,128)(2,1)}, bf16[64,8192]{1,0:T(8,128)(2,1)S(1)}, u32[]{:S(2)}, u32[]{:S(2)}) collective-permute-start(bf16[64,8192]{1,0:T(8,128)(2,1)} %bitcast.25), channel_id=1, source_target_pairs={{0,1},{1,0},{2,3},{3,2},{4,5},{5,4},{6,7},{7,6},{8,9},{9,8},{10,11... | collective-permute-start | bytes 3145736 | tf_op jit(solution)/shard_map/ppermute | solution.py:26
  32.4 16.3 %all-to-all-start.1 = ((bf16[64,8,128]{2,1,0:T(8,128)(2,1)}), bf16[64,8,128]{2,1,0:T(8,128)(2,1)S(1)}, u32[]{:S(2)}, u32[]{:S(2)}) async-start(bf16[64,8,128]{2,1,0:T(8,128)(2,1)} %shard_map.122), calls=%async_computation.1 | async-start | bytes 262144 | tf_op jit(solution)/shard_map/all_to_all | solution.py:30
  37.1 3.3 %collective-permute-start.5 = (bf16[2,8,64]{2,1,0:T(8,128)(2,1)}, bf16[2,8,64]{2,1,0:T(8,128)(2,1)S(1)}, u32[]{:S(2)}, u32[]{:S(2)}) collective-permute-start(bf16[2,8,64]{2,1,0:T(8,128)(2,1)} %param.20), channel_id=1, source_target_pairs={{0,1},{1,0},{2,3},{3,2},{4,5},{5,4},{6,7},{7,6},{8,9},{9,8},{10,11... | collective-permute-start | bytes 6152 | tf_op jit(solution)/shard_map/ppermute | solution.py:26
  39.1 1.2 %copy-start.1 = (bf16[1,64,8192]{2,1,0:T(8,128)(2,1)S(1)}, bf16[1,64,8192]{2,1,0:T(8,128)(2,1)}, u32[]{:S(2)}) copy-start(bf16[1,64,8192]{2,1,0:T(8,128)(2,1)} %param.17) | copy-start | bytes 3145732
  80.1 7.6 %collective-permute-start.6 = (bf16[64,4,128]{2,1,0:T(4,128)(2,1)S(1)}, bf16[64,4,128]{2,1,0:T(4,128)(2,1)S(1)}, u32[]{:S(2)}, u32[]{:S(2)}) collective-permute-start(bf16[64,4,128]{2,1,0:T(4,128)(2,1)S(1)} %all_to_all.26.near_ref), channel_id=1, source_target_pairs={{0,1},{1,0},{2,3},{3,2},{4,5},{5,4},{6,7},{7,6},{8,9},{9,8},{10,11... | collective-permute-start | bytes 196616 | tf_op jit(solution)/shard_map/ppermute | solution.py:26
  83.8 3.3 %copy-start = (bf16[8192,501]{0,1:T(8,128)(2,1)S(1)}, bf16[8192,501]{0,1:T(8,128)(2,1)}, u32[]{:S(2)}) copy-start(bf16[8192,501]{0,1:T(8,128)(2,1)} %param.19) | copy-start | bytes 24625156
  87.2 0.7 copy-start.2
  90.5 1.4 %collective-permute-start.7 = (f32[8,128]{1,0:T(8,128)S(1)}, f32[8,128]{1,0:T(8,128)S(1)}, u32[]{:S(2)}, u32[]{:S(2)}) collective-permute-start(f32[8,128]{1,0:T(8,128)S(1)} %get-tuple-element.34.near_ref), channel_id=1, source_target_pairs={{0,1},{1,0},{2,3},{3,2},{4,5},{5,4},{6,7},{7,6},{8,9},{9,8},{10,11... | collective-permute-start | bytes 12296 | tf_op jit(solution)/shard_map/ppermute | solution.py:26
  92.7 16.7 %all-to-all-start.4 = ((f32[128,1,128]{2,1,0:T(1,128)}), f32[128,1,128]{2,1,0:T(1,128)S(1)}, u32[]{:S(2)}, u32[]{:S(2)}) async-start(f32[128,1,128]{2,1,0:T(1,128)} %shard_map.128), calls=%async_computation.4 | async-start | bytes 131072 | tf_op jit(solution)/shard_map/all_to_all | solution.py:30
  98.9 2.8 %collective-permute-start.8 = (bf16[8,64]{1,0:T(8,128)(2,1)S(1)}, bf16[8,64]{1,0:T(8,128)(2,1)S(1)}, u32[]{:S(2)}, u32[]{:S(2)}) collective-permute-start(bf16[8,64]{1,0:T(8,128)(2,1)S(1)} %slice_select_fusion), channel_id=1, source_target_pairs={{0,128},{128,0},{1,129},{129,1},{2,130},{130,2},{3,131},{131,3},{4... | collective-permute-start | bytes 3080 | tf_op jit(solution)/shard_map/ppermute | solution.py:323

commit v12 on v9

--- a/solution.py
+++ b/solution.py
@@ -234,7 +234,7 @@
     keys, values = rows_of(keys, row0), rows_of(values, row0)
     gain_chip = by_core(core, gain, gain_far, 0)
 
-    lens = rows_of(lengths, row0)
+    lens = jnp.where(core == 0, lengths[:HALF], lengths[HALF:])
     at = jnp.arange(slots, dtype=jnp.int32)
     position = jnp.concatenate([place * slots + at, (place + 1 - 2 * core) * slots + at])
     valid = (position[None, :] < lens[:, None]).astype(F32).reshape(1, 4 * 2 * slots)

time: 111 us -> 111 us (level)
    dynamic_slice x5 -> x4, local copies, waits for them, and re-layouts: 3.37 us -> 2.64 us  [rows_of(): return lax.dynamic_slice_in_dim(x, start, HALF, axis)]
where the time goes in v12:
time: 111 us; the launch traced here: 110 us
  starting transfers between devices  33.9 us (31%)
  blocking collectives  30.6 us (28%)
  waiting for transfers between devices  25.8 us (23%)
  local copies, waits for them, and re-layouts  9.4 us (8%)
  Pallas kernels  6.45 us (6%)
  other arithmetic  2.72 us (2%)
    all_to_all x2, blocking collectives, exchange(): return lax.all_to_all(x, axes, split_axis=0, concat_axis=0, tiled=True)  30.6 us
    all_to_all x3, starting transfers between devices, exchange(): return lax.all_to_all(x, axes, split_axis=0, concat_axis=0, tiled=True)  23.4 us
    all_to_all x3, waiting for transfers between devices, exchange(): return lax.all_to_all(x, axes, split_axis=0, concat_axis=0, tiled=True)  22.3 us
    ppermute x8, starting transfers between devices, swap(): return lax.ppermute(x, CORE, [(0, 1), (1, 0)])  9.55 us
    pallas_call x8, Pallas kernels, call(): pl.pallas_call(kernel, out_shape=shapes, in_specs=specs, scratch_shapes=s...  6.45 us
    unnamed x4, local copies, waits for them, and re-layouts  4.57 us
    dynamic_slice x4, local copies, waits for them, and re-layouts, rows_of(): return lax.dynamic_slice_in_dim(x, start, HALF, axis)  2.64 us
  transfers between devices with their start and end apart: 12, of which 6 were waited for; matrix products, arithmetic and copies ran while one was open for 7% of the time, Pallas kernels for 1%

profile of v12, /device:TPU:1, one launch (start us, length us, event | category | flops | bytes accessed | tf_op | source)
XLA Modules:
  0.0 110.1 jit_solution(7006538694048565543)
XLA Ops:
  0.6 3.3 %collective-permute-start.1 = (f32[1,64]{1,0:T(1,128)}, f32[1,64]{1,0:T(1,128)S(1)}, u32[]{:S(2)}, u32[]{:S(2)}) collective-permute-start(f32[1,64]{1,0:T(1,128)} %param.18), channel_id=1, source_target_pairs={{0,1},{1,0},{2,3},{3,2},{4,5},{5,4},{6,7},{7,6},{8,9},{9,8},{10,11... | collective-permute-start | bytes 776 | tf_op jit(solution)/shard_map/ppermute | solution.py:26
  4.1 0.7 fusion.2
  5.4 0.6 broadcast_in_dim.27
  6.1 12.6 %all-to-all-start = ((bf16[64,4,128]{2,1,0:T(4,128)(2,1)}), bf16[64,4,128]{2,1,0:T(4,128)(2,1)S(1)}, u32[]{:S(2)}, u32[]{:S(2)}) async-start(bf16[64,4,128]{2,1,0:T(4,128)(2,1)} %broadcast_in_dim.27), calls=%async_computation | async-start | bytes 131072 | tf_op jit(solution)/shard_map/all_to_all | solution.py:30
  18.6 1.0 constant_dynamic-slice_fusion.6.k_ref
  19.6 0.5 collective-permute-start.2
  20.1 0.8 broadcast_select_fusion
  21.0 0.7 fusion.8
  22.0 1.0 constant_dynamic-slice_fusion.5.v_ref
  23.0 6.9 %all-to-all-done = bf16[64,4,128]{2,1,0:T(4,128)(2,1)S(1)} async-done(((bf16[64,4,128]{2,1,0:T(4,128)(2,1)}), bf16[64,4,128]{2,1,0:T(4,128)(2,1)S(1)}, u32[]{:S(2)}, u32[]{:S(2)}) %all-to-all-start) | async-done | bytes 65568 | tf_op jit(solution)/shard_map/all_to_all | solution.py:30
  29.9 1.2 %shard_map.122 = bf16[64,8,128]{2,1,0:T(8,128)(2,1)} custom-call(s32[1]{0:T(128)} %bitcast.1.core_ref, bf16[256,128]{1,0:T(8,128)(2,1)S(1)} %bitcast.26, bf16[4,32,1024]{2,1,0:T(8,128)(2,1)S(1)} %constant_dynamic-slice_fusion.6.k_ref, bf16[4,32,1024]{2,1,0:T(8,128)(2,1)S(1)} %constant_dynamic-slice_fusion.5.v_ref, ...), custom_call_target="tpu_custom_call" | custom-call | flops 33554432 | bytes 2097152 | tf_op jit(solution)/shard_map/pallas_call | solution.py:49
  31.1 1.3 %collective-permute-start.4 = (bf16[64,8192]{1,0:T(8,128)(2,1)}, bf16[64,8192]{1,0:T(8,128)(2,1)S(1)}, u32[]{:S(2)}, u32[]{:S(2)}) collective-permute-start(bf16[64,8192]{1,0:T(8,128)(2,1)} %bitcast.24), channel_id=1, source_target_pairs={{0,1},{1,0},{2,3},{3,2},{4,5},{5,4},{6,7},{7,6},{8,9},{9,8},{10,11... | collective-permute-start | bytes 3145736 | tf_op jit(solution)/shard_map/ppermute | solution.py:26
  32.4 4.7 %all-to-all-start.1 = ((bf16[64,8,128]{2,1,0:T(8,128)(2,1)}), bf16[64,8,128]{2,1,0:T(8,128)(2,1)S(1)}, u32[]{:S(2)}, u32[]{:S(2)}) async-start(bf16[64,8,128]{2,1,0:T(8,128)(2,1)} %shard_map.122), calls=%async_computation.1 | async-start | bytes 262144 | tf_op jit(solution)/shard_map/all_to_all | solution.py:30
  37.2 0.5 collective-permute-start.5
  37.7 0.7 fusion.4
  38.4 0.8 constant_dynamic-slice_fusion.3
  39.2 0.7 fusion.7.action_ref
  39.9 1.2 %copy-done.1 = bf16[1,64,8192]{2,1,0:T(8,128)(2,1)S(1)} copy-done((bf16[1,64,8192]{2,1,0:T(8,128)(2,1)S(1)}, bf16[1,64,8192]{2,1,0:T(8,128)(2,1)}, u32[]{:S(2)}) %copy-start.1) | copy-done | bytes 1048600
  41.3 7.6 %all-to-all-done.1.got_ref = bf16[64,8,128]{2,1,0:T(8,128)(2,1)S(1)} async-done(((bf16[64,8,128]{2,1,0:T(8,128)(2,1)}), bf16[64,8,128]{2,1,0:T(8,128)(2,1)S(1)}, u32[]{:S(2)}, u32[]{:S(2)}) %all-to-all-start.1) | async-done | bytes 131104 | tf_op jit(solution)/shard_map/all_to_all | solution.py:30
  49.8 15.8 %all_to_all.25.got_ref = bf16[64,4,128]{2,1,0:T(4,128)(2,1)S(1)} all-to-all(bf16[64,4,128]{2,1,0:T(4,128)(2,1)S(1)} %fusion.1), channel_id=1, replica_groups=mesh['role'=2,'grp'=2,'tp_0'=4,'tp_1'=8,'tp_2'=2] {'grp','tp_0','tp_1'}, dimensions={0} | all-to-all | bytes 131072 | tf_op jit(solution)/shard_map/all_to_all | solution.py:30
  65.6 14.8 %all_to_all.26.near_ref = bf16[64,4,128]{2,1,0:T(4,128)(2,1)S(1)} all-to-all(bf16[64,4,128]{2,1,0:T(4,128)(2,1)S(1)} %shard_map.125), channel_id=1, replica_groups=mesh['role'=2,'grp'=2,'tp_0'=4,'tp_1'=8,'tp_2'=2] {'grp','tp_0','tp_1'}, dimensions={0} | all-to-all | bytes 131072 | tf_op jit(solution)/shard_map/all_to_all | solution.py:30
  80.4 3.4 %collective-permute-start.6 = (bf16[64,4,128]{2,1,0:T(4,128)(2,1)S(1)}, bf16[64,4,128]{2,1,0:T(4,128)(2,1)S(1)}, u32[]{:S(2)}, u32[]{:S(2)}) collective-permute-start(bf16[64,4,128]{2,1,0:T(4,128)(2,1)S(1)} %all_to_all.26.near_ref), channel_id=1, source_target_pairs={{0,1},{1,0},{2,3},{3,2},{4,5},{5,4},{6,7},{7,6},{8,9},{9,8},{10,11... | collective-permute-start | bytes 196616 | tf_op jit(solution)/shard_map/ppermute | solution.py:26
  83.9 3.3 %copy-done = bf16[8192,501]{0,1:T(8,128)(2,1)S(1)} copy-done((bf16[8192,501]{0,1:T(8,128)(2,1)S(1)}, bf16[8192,501]{0,1:T(8,128)(2,1)}, u32[]{:S(2)}) %copy-start) | copy-done | bytes 8208408
  87.2 0.5 shard_map.126.head_ref
  87.8 2.7 %shard_map.127 = (f32[8,128]{1,0:T(8,128)S(1)}, bf16[8,128]{1,0:T(8,128)(2,1)S(1)}) custom-call(s32[1]{0:T(128)} %bitcast.1.core_ref, s32[1]{0:T(128)} %bitcast.2.chip_ref, bf16[64,4,128]{2,1,0:T(4,128)(2,1)S(1)} %all_to_all.26.near_ref, bf16[64,4,128]{2,1,0:T(4,128)(2,1)S(1)} %collective-permute-done.6.far_ref, ...), custom_call_target="tpu_custom_call" | custom-call | flops 65667072 | bytes 4104192 | tf_op jit(solution)/shard_map/pallas_call | solution.py:49
  90.7 1.2 %collective-permute-done.7.far_ref = f32[8,128]{1,0:T(8,128)S(1)} collective-permute-done((f32[8,128]{1,0:T(8,128)S(1)}, f32[8,128]{1,0:T(8,128)S(1)}, u32[]{:S(2)}, u32[]{:S(2)}) %collective-permute-start.7) | collective-permute-done | bytes 4128 | tf_op jit(solution)/shard_map/ppermute | solution.py:26
  91.9 0.7 shard_map.128
  92.6 6.1 %all-to-all-start.4 = ((f32[128,1,128]{2,1,0:T(1,128)}), f32[128,1,128]{2,1,0:T(1,128)S(1)}, u32[]{:S(2)}, u32[]{:S(2)}) async-start(f32[128,1,128]{2,1,0:T(1,128)} %shard_map.128), calls=%async_computation.4 | async-start | bytes 131072 | tf_op jit(solution)/shard_map/all_to_all | solution.py:30
  98.8 0.9 collective-permute-start.8
  99.7 1.8 %collective-permute-done.8.normed_ref = bf16[8,64]{1,0:T(8,128)(2,1)S(1)} collective-permute-done((bf16[8,64]{1,0:T(8,128)(2,1)S(1)}, bf16[8,64]{1,0:T(8,128)(2,1)S(1)}, u32[]{:S(2)}, u32[]{:S(2)}) %collective-permute-start.8) | collective-permute-done | bytes 1056 | tf_op jit(solution)/shard_map/ppermute | solution.py:322
  101.5 7.8 %all-to-all-done.4.heard_ref = f32[128,1,128]{2,1,0:T(1,128)S(1)} async-done(((f32[128,1,128]{2,1,0:T(1,128)}), f32[128,1,128]{2,1,0:T(1,128)S(1)}, u32[]{:S(2)}, u32[]{:S(2)}) %all-to-all-start.4) | async-done | bytes 65568 | tf_op jit(solution)/shard_map/all_to_all | solution.py:30
  109.3 0.7 shard_map.129
  (32 shorter events, 2.6 us)
Async XLA Ops:
  0.6 18.0 %collective-permute-start.1 = (f32[1,64]{1,0:T(1,128)}, f32[1,64]{1,0:T(1,128)S(1)}, u32[]{:S(2)}, u32[]{:S(2)}) collective-permute-start(f32[1,64]{1,0:T(1,128)} %param.18), channel_id=1, source_target_pairs={{0,1},{1,0},{2,3},{3,2},{4,5},{5,4},{6,7},{7,6},{8,9},{9,8},{10,11... | collective-permute-start | bytes 776 | tf_op jit(solution)/shard_map/ppermute | solution.py:26
  4.0 1.4 %collective-permute-start = (bf16[2,8,64]{2,1,0:T(8,128)(2,1)}, bf16[2,8,64]{2,1,0:T(8,128)(2,1)S(1)}, u32[]{:S(2)}, u32[]{:S(2)}) collective-permute-start(bf16[2,8,64]{2,1,0:T(8,128)(2,1)} %param.11), channel_id=1, source_target_pairs={{0,1},{1,0},{2,3},{3,2},{4,5},{5,4},{6,7},{7,6},{8,9},{9,8},{10,11... | collective-permute-start | bytes 6152 | tf_op jit(solution)/shard_map/ppermute | solution.py:26
  6.1 23.8 %all-to-all-start = ((bf16[64,4,128]{2,1,0:T(4,128)(2,1)}), bf16[64,4,128]{2,1,0:T(4,128)(2,1)S(1)}, u32[]{:S(2)}, u32[]{:S(2)}) async-start(bf16[64,4,128]{2,1,0:T(4,128)(2,1)} %broadcast_in_dim.27), calls=%async_computation | async-start | bytes 131072 | tf_op jit(solution)/shard_map/all_to_all | solution.py:30
  19.6 10.3 %collective-permute-start.2 = (bf16[8,32,1024]{2,1,0:T(8,128)(2,1)}, bf16[8,32,1024]{2,1,0:T(8,128)(2,1)S(1)}, u32[]{:S(2)}, u32[]{:S(2)}) collective-permute-start(bf16[8,32,1024]{2,1,0:T(8,128)(2,1)} %param.14), channel_id=1, source_target_pairs={{0,1},{1,0},{2,3},{3,2},{4,5},{5,4},{6,7},{7,6},{8,9},{9,8},{10,11... | collective-permute-start | bytes 1572872 | tf_op jit(solution)/shard_map/ppermute | solution.py:26
  20.9 9.0 %collective-permute-start.3 = (bf16[8,32,1024]{2,1,0:T(8,128)(2,1)}, bf16[8,32,1024]{2,1,0:T(8,128)(2,1)S(1)}, u32[]{:S(2)}, u32[]{:S(2)}) collective-permute-start(bf16[8,32,1024]{2,1,0:T(8,128)(2,1)} %param.15), channel_id=1, source_target_pairs={{0,1},{1,0},{2,3},{3,2},{4,5},{5,4},{6,7},{7,6},{8,9},{9,8},{10,11... | collective-permute-start | bytes 1572872 | tf_op jit(solution)/shard_map/ppermute | solution.py:26
  31.1 18.2 %collective-permute-start.4 = (bf16[64,8192]{1,0:T(8,128)(2,1)}, bf16[64,8192]{1,0:T(8,128)(2,1)S(1)}, u32[]{:S(2)}, u32[]{:S(2)}) collective-permute-start(bf16[64,8192]{1,0:T(8,128)(2,1)} %bitcast.24), channel_id=1, source_target_pairs={{0,1},{1,0},{2,3},{3,2},{4,5},{5,4},{6,7},{7,6},{8,9},{9,8},{10,11... | collective-permute-start | bytes 3145736 | tf_op jit(solution)/shard_map/ppermute | solution.py:26
  32.4 16.4 %all-to-all-start.1 = ((bf16[64,8,128]{2,1,0:T(8,128)(2,1)}), bf16[64,8,128]{2,1,0:T(8,128)(2,1)S(1)}, u32[]{:S(2)}, u32[]{:S(2)}) async-start(bf16[64,8,128]{2,1,0:T(8,128)(2,1)} %shard_map.122), calls=%async_computation.1 | async-start | bytes 262144 | tf_op jit(solution)/shard_map/all_to_all | solution.py:30
  37.2 4.0 %collective-permute-start.5 = (bf16[2,8,64]{2,1,0:T(8,128)(2,1)}, bf16[2,8,64]{2,1,0:T(8,128)(2,1)S(1)}, u32[]{:S(2)}, u32[]{:S(2)}) collective-permute-start(bf16[2,8,64]{2,1,0:T(8,128)(2,1)} %param.20), channel_id=1, source_target_pairs={{0,1},{1,0},{2,3},{3,2},{4,5},{5,4},{6,7},{7,6},{8,9},{9,8},{10,11... | collective-permute-start | bytes 6152 | tf_op jit(solution)/shard_map/ppermute | solution.py:26
  39.9 1.2 %copy-start.1 = (bf16[1,64,8192]{2,1,0:T(8,128)(2,1)S(1)}, bf16[1,64,8192]{2,1,0:T(8,128)(2,1)}, u32[]{:S(2)}) copy-start(bf16[1,64,8192]{2,1,0:T(8,128)(2,1)} %param.17) | copy-start | bytes 3145732
  80.4 7.3 %collective-permute-start.6 = (bf16[64,4,128]{2,1,0:T(4,128)(2,1)S(1)}, bf16[64,4,128]{2,1,0:T(4,128)(2,1)S(1)}, u32[]{:S(2)}, u32[]{:S(2)}) collective-permute-start(bf16[64,4,128]{2,1,0:T(4,128)(2,1)S(1)} %all_to_all.26.near_ref), channel_id=1, source_target_pairs={{0,1},{1,0},{2,3},{3,2},{4,5},{5,4},{6,7},{7,6},{8,9},{9,8},{10,11... | collective-permute-start | bytes 196616 | tf_op jit(solution)/shard_map/ppermute | solution.py:26
  83.9 3.3 %copy-start = (bf16[8192,501]{0,1:T(8,128)(2,1)S(1)}, bf16[8192,501]{0,1:T(8,128)(2,1)}, u32[]{:S(2)}) copy-start(bf16[8192,501]{0,1:T(8,128)(2,1)} %param.19) | copy-start | bytes 24625156
  90.4 1.4 %collective-permute-start.7 = (f32[8,128]{1,0:T(8,128)S(1)}, f32[8,128]{1,0:T(8,128)S(1)}, u32[]{:S(2)}, u32[]{:S(2)}) collective-permute-start(f32[8,128]{1,0:T(8,128)S(1)} %get-tuple-element.36.near_ref), channel_id=1, source_target_pairs={{0,1},{1,0},{2,3},{3,2},{4,5},{5,4},{6,7},{7,6},{8,9},{9,8},{10,11... | collective-permute-start | bytes 12296 | tf_op jit(solution)/shard_map/ppermute | solution.py:26
  92.6 16.7 %all-to-all-start.4 = ((f32[128,1,128]{2,1,0:T(1,128)}), f32[128,1,128]{2,1,0:T(1,128)S(1)}, u32[]{:S(2)}, u32[]{:S(2)}) async-start(f32[128,1,128]{2,1,0:T(1,128)} %shard_map.128), calls=%async_computation.4 | async-start | bytes 131072 | tf_op jit(solution)/shard_map/all_to_all | solution.py:30
  98.8 2.8 %collective-permute-start.8 = (bf16[8,64]{1,0:T(8,128)(2,1)S(1)}, bf16[8,64]{1,0:T(8,128)(2,1)S(1)}, u32[]{:S(2)}, u32[]{:S(2)}) collective-permute-start(bf16[8,64]{1,0:T(8,128)(2,1)S(1)} %slice_select_fusion), channel_id=1, source_target_pairs={{0,128},{128,0},{1,129},{129,1},{2,130},{130,2},{3,131},{131,3},{4... | collective-permute-start | bytes 3080 | tf_op jit(solution)/shard_map/ppermute | solution.py:322
